TPU v7x, 32 devices: a whole 2x2x4 slice. The times are simulated.
32 devices in a mesh: seq: 8 (over z, y), head: 4 (over x, core).
Axes of the slice: x: 2, y: 2, z: 4, core: 2. Of those that a mesh axis runs over, the one named last changes fastest.
Arguments:
- tokens: bfloat16 [2048, 3072], P('seq'), may hold values from -18 to 18
- w_qkv: bfloat16 [3, 3072, 2048], P(None, 'seq', 'head'), may hold values from -0.109375 to 0.109375
- gains: float32 [2, 2048], P(None, 'head'), may hold values from 0.5 to 1.5
- cotangent: bfloat16 [2048, 2048], P('seq', 'head'), may hold values from -6 to 6
- token_clip: int32 [2048], replicated, may hold values from 0 to 2, as said below
- key_live: int32 [2048], replicated, may hold values 0 or 1
- damp_mask: int32 [3072, 2048], P('seq', 'head'), may hold values 0 or 1
Outputs:
- fisher_ratio: float32 [3, 3072, 2048], P(None, 'seq', 'head')
- dampened: bfloat16 [3, 3072, 2048], P(None, 'seq', 'head')
Inputs may be any that keep to these rules, and one draw needn't show every extreme that they name: token_clip never decreases along the tokens (each clip is one contiguous run of tokens); every clip has at least one token and the longest has exactly 1536.
All inputs are finite; a program needn't handle non-finite values. No bound on the sum of `damp_mask` on one device may be relied on, other than what follows from the above.
Results may differ from a plain program's by a relative error of at most 0.03.
Values may be sent and summed in bfloat16 or wider, within the bound.
No kernel may reach another device: no remote copies, remote signals or barrier semaphores. Data moves between devices by JAX's collectives and lax.ppermute only.
A program may use at most 192 MiB of HBM per device.

v0:
```python
import math

import jax
import jax.numpy as jnp
from jax import lax
from jax.sharding import PartitionSpec as P

D = 3072
HD = 128
HEADS = 16
CLIPS = 3


def normed(values, gain_row, head_count):
    shaped = values.reshape(values.shape[0], head_count, HD)
    inverse = lax.rsqrt(jnp.mean(shaped * shaped, -1, keepdims=True) + 1e-06)
    return (shaped * inverse * gain_row.reshape(head_count, HD), inverse, shaped)


def unnorm(upstream, shaped, inverse, gain_row, head_count):
    gain_grid = gain_row.reshape(head_count, HD)
    cubed = inverse * inverse * inverse
    return inverse * gain_grid * upstream - shaped * cubed * jnp.mean(
        shaped * gain_grid * upstream, -1, keepdims=True
    )


def by_clip(grad_rows, clip_ids):
    return jnp.concatenate(
        [
            grad_rows * (clip_ids == clip_no).astype(jnp.bfloat16)[..., None]
            for clip_no in range(CLIPS)
        ],
        -1,
    )


def on_device(tokens, w_qkv, gains, cotangent, token_clip, key_live, damp_mask):
    tok_rows = tokens.shape[0]
    width_dev = w_qkv.shape[2]
    rows_dev = w_qkv.shape[1]
    head_count = width_dev // HD
    all_tokens = token_clip.shape[0]
    seq_rank = lax.axis_index("seq")
    score_scale = 1.0 / math.sqrt(HD)
    columns = tokens
    projected = jnp.einsum(
        "tr,jrc->jtc",
        columns,
        lax.all_gather(w_qkv, "seq", axis=1, tiled=True),
        preferred_element_type=jnp.float32,
    )
    query_n, query_inv, query_raw = normed(projected[0], gains[0], head_count)
    key_n, key_inv, key_raw = normed(projected[1], gains[1], head_count)
    query_b = query_n.astype(jnp.bfloat16)
    local_kv = jnp.concatenate(
        [
            key_n.astype(jnp.bfloat16).reshape(tok_rows, width_dev),
            projected[2].astype(jnp.bfloat16),
        ],
        1,
    )
    all_kv = lax.all_gather(local_kv, "seq", axis=0, tiled=True)
    keys_all = all_kv[:, :width_dev].reshape(all_tokens, head_count, HD)
    values_all = all_kv[:, width_dev:].reshape(all_tokens, head_count, HD)
    first_row = seq_rank * tok_rows
    clip_here = lax.dynamic_slice_in_dim(token_clip, first_row, tok_rows)
    positions = first_row + jnp.arange(tok_rows, dtype=jnp.int32)
    key_positions = jnp.arange(all_tokens, dtype=jnp.int32)
    allowed = (clip_here[:, None] == token_clip[None, :]) & (
        (key_live[None, :] == 1) | (positions[:, None] == key_positions[None, :])
    )
    scores = (
        jnp.einsum("thd,khd->htk", query_b, keys_all, preferred_element_type=jnp.float32)
        * score_scale
    )
    scores = jnp.where(allowed[None], scores, -1e30)
    peak = jnp.max(scores, -1, keepdims=True)
    expd = jnp.exp(scores - peak)
    probs = expd / jnp.sum(expd, -1, keepdims=True)
    grad_out = cotangent.reshape(tok_rows, head_count, HD)
    grad_p = jnp.einsum("thd,khd->htk", grad_out, values_all, preferred_element_type=jnp.float32)
    row_dot = jnp.sum(probs * grad_p, -1, keepdims=True)
    ds_half = (probs * (grad_p - row_dot)).astype(jnp.bfloat16)
    probs_half = probs.astype(jnp.bfloat16)
    grad_qn = (
        jnp.einsum("htk,khd->thd", ds_half, keys_all, preferred_element_type=jnp.float32)
        * score_scale
    )
    key_part = (
        jnp.einsum("htk,thd->khd", ds_half, query_b, preferred_element_type=jnp.float32)
        * score_scale
    )
    value_part = jnp.einsum(
        "htk,thd->khd", probs_half, grad_out, preferred_element_type=jnp.float32
    )
    key_terms = jnp.concatenate(
        [key_part.reshape(all_tokens, width_dev), value_part.reshape(all_tokens, width_dev)], 1
    )
    summed = lax.psum_scatter(
        key_terms.astype(jnp.bfloat16), "seq", scatter_dimension=0, tiled=True
    ).astype(jnp.float32)
    grad_q = unnorm(grad_qn, query_raw, query_inv, gains[0], head_count)
    grad_k = unnorm(
        summed[:, :width_dev].reshape(tok_rows, head_count, HD),
        key_raw,
        key_inv,
        gains[1],
        head_count,
    )
    grad_proj = jnp.concatenate(
        [
            grad_q.reshape(tok_rows, width_dev),
            grad_k.reshape(tok_rows, width_dev),
            summed[:, width_dev:],
        ],
        1,
    ).astype(jnp.bfloat16)
    masked = by_clip(grad_proj, clip_here)
    columns = tokens
    per_clip = lax.psum_scatter(
        lax.dot_general(
            columns, masked, (((0,), (0,)), ((), ())), preferred_element_type=jnp.float32
        ).astype(jnp.bfloat16),
        "seq",
        scatter_dimension=0,
        tiled=True,
    ).astype(jnp.float32)
    fisher = jnp.sum(jnp.square(per_clip.reshape(rows_dev, CLIPS, 3, width_dev)), 1)
    fisher = jnp.transpose(fisher, (1, 0, 2))
    fisher_sum = lax.psum(jnp.sum(fisher), ("seq", "head"))
    fisher_mean = fisher_sum / (3 * D * HEADS * HD)
    fisher_ratio = fisher / (fisher_mean + 1e-06)
    dampened = (
        w_qkv.astype(jnp.float32) / (1.0 + damp_mask.astype(jnp.float32)[None] * fisher_ratio)
    ).astype(jnp.bfloat16)
    return (fisher_ratio, dampened)


def solution(mesh):
    return jax.shard_map(
        on_device,
        mesh=mesh,
        in_specs=(
            P("seq", None),
            P(None, "seq", "head"),
            P(None, "head"),
            P("seq", "head"),
            P(),
            P(),
            P("seq", "head"),
        ),
        out_specs=(P(None, "seq", "head"), P(None, "seq", "head")),
        check_vma=False,
    )
```

profile of v0, /device:TPU:0, one launch (start us, length us, event | category | flops | bytes accessed | tf_op | source)
XLA Modules:
  0.0 921.4 jit_solution(17862771791614844298)
XLA Ops:
  7.2 0.0 copy-start
  7.2 0.0 copy-start.11
  7.2 0.0 all-gather.3.cloned.1.call-start
  7.2 2.5 copy.16
  9.7 0.0 all-gather.3.cloned.1.call-update
  9.7 0.0 all-gather.5.cloned.1.call-start
  9.8 0.0 copy-done.11
  9.8 141.8 %all-gather.3.cloned.1.call-done = bf16[3,3072,512]{1,2,0:T(8,128)(2,1)} async-done(((bf16[3,384,512]{1,2,0:T(8,128)(2,1)}), bf16[3,3072,512]{1,2,0:T(8,128)(2,1)}) %all-gather.3.cloned.1.call-update) | async-done | bytes 9437200 | tf_op jit(solution)/shard_map/all_gather | solution.py:50
  151.6 0.0 copy-done
  151.6 5.2 fusion.23
  156.8 0.0 copy-start.5
  156.8 0.0 copy-start.8
  156.8 0.1 fusion.40
  156.9 0.0 copy-start.9
  156.9 0.0 copy-start.10
  157.0 0.1 multiply_reduce_fusion.2
  157.0 0.9 copy-done.5
  158.0 0.1 fusion.31
  158.1 0.8 pad_maximum_fusion.2
  158.9 0.0 all-gather.5.cloned.1.call-update
  159.0 0.0 reduce-scatter.5.cloned.1.call-start
  159.0 0.0 copy-done.8
  159.0 0.1 copy.33
  159.2 0.0 copy-done.9
  159.2 0.1 compare_convert_fusion.2
  159.3 0.0 copy-done.10
  159.3 0.9 fusion.20
  160.1 0.1 multiply_reduce_fusion.3
  160.2 72.1 %all-gather.5.cloned.1.call-done = bf16[2048,1024]{0,1:T(8,128)(2,1)} async-done(((bf16[256,1024]{0,1:T(8,128)(2,1)}), bf16[2048,1024]{0,1:T(8,128)(2,1)}) %all-gather.5.cloned.1.call-update) | async-done | bytes 4194320 | tf_op jit(solution)/shard_map/all_gather | solution.py:63
  232.3 4.9 fusion.39
  237.2 8.0 fusion.42
  245.1 4.4 fusion.11
  249.5 1.4 copy-done.4
  250.9 0.6 copy-done.6
  251.5 1.8 fusion.2
  253.3 1.4 fusion.4
  254.7 0.0 copy-start.2
  254.7 0.9 multiply_convert_fusion
  255.7 1.0 copy-done.2
  256.7 2.4 pad_maximum_fusion
  259.2 0.0 reduce-scatter.5.cloned.1.call-update
  259.2 0.2 reduce-scatter.7.cloned.1.call-start
  259.4 4.4 multiply_reduce_fusion.1
  263.8 0.1 subtract_convert_fusion
  264.0 82.1 %reduce-scatter.5.cloned.1.call-done = bf16[256,1024]{0,1:T(8,128)(2,1)} async-done(((bf16[2048,1024]{0,1:T(8,128)(2,1)}), bf16[256,1024]{0,1:T(8,128)(2,1)}) %reduce-scatter.5.cloned.1.call-update) | async-done | bytes 524304 | tf_op jit(solution)/shard_map/reduce_scatter | solution.py:100
  346.0 1.1 multiply_reduce_fusion
  347.2 1.3 fusion.34
  348.5 0.0 slice-done
  348.5 0.5 broadcast_multiply_fusion.2
  349.0 16.9 %fusion.1 = bf16[3072,4608]{0,1:T(8,128)(2,1)} fusion(bf16[256,3072]{1,0:T(8,128)(2,1)S(1)} %copy-done, bf16[256,1536]{0,1:T(8,128)(2,1)S(1)} %get-tuple-element.16, bf16[256,1536]{0,1:T(8,128)(2,1)S(1)} %get-tuple-element.15, bf16[256,1536]{0,1:T(8,128)(2,1)S(1)} %get-tuple-element.14), kind=kOutput, calls=%fused_computation.2 | convolution fusion | flops 7268990976 | bytes 32243712 | tf_op jit(solution)/shard_map/dot_general | solution.py:122
  365.9 33.6 %copy.31 = bf16[3072,4608]{1,0:T(8,128)(2,1)} copy(bf16[3072,4608]{0,1:T(8,128)(2,1)} %fusion.1) | data formatting | bytes 56623104
  399.5 0.0 reduce-scatter.7.cloned.1.call-update
  399.6 1.1 copy-done.7
  400.7 0.1 convert_element_type.59
  400.7 0.3 copy.24
  401.0 447.3 %reduce-scatter.7.cloned.1.call-done = bf16[384,4608]{1,0:T(8,128)(2,1)} async-done(((bf16[3072,4608]{1,0:T(8,128)(2,1)}), bf16[384,4608]{1,0:T(8,128)(2,1)}) %reduce-scatter.7.cloned.1.call-update) | async-done | bytes 3538960
  848.3 5.7 copy.32
  854.0 7.3 fusion.26
  861.3 39.5 %psum.7 = f32[]{:T(128)} all-reduce(f32[]{:T(128)} %get-tuple-element.10), channel_id=1, replica_groups=mesh['seq'=8,'head'=4] {'seq','head'}, use_global_device_ids=true, to_apply=%region_11.12 | all-reduce | flops 1 | bytes 8 | tf_op jit(solution)/shard_map/psum | solution.py:131
  900.8 5.1 reduce_sum.78
  906.7 0.0 copy-done.3
  906.7 3.6 divide_convert_fusion
  910.3 3.2 copy.25
  913.5 1.4 copy.26
  (16 shorter events, 0.1 us)
Async XLA Ops:
  7.2 144.4 %copy-start = (bf16[256,3072]{1,0:T(8,128)(2,1)S(1)}, bf16[256,3072]{1,0:T(8,128)(2,1)}, u32[]{:S(2)}) copy-start(bf16[256,3072]{1,0:T(8,128)(2,1)} %param.7) | copy-start | bytes 4718596
  7.2 2.6 copy-start.11
  7.2 144.4 %all-gather.3.cloned.1.call-start = ((), (), s32[]{:S(2)}) async-start(), calls=%async_computation.2 | async-start | bytes 10616832 | tf_op jit(solution)/shard_map/all_gather | solution.py:50
  9.7 222.6 %all-gather.5.cloned.1.call-start = ((), (), s32[]{:S(2)}) async-start(), calls=%async_computation.3 | async-start | bytes 4718592 | tf_op jit(solution)/shard_map/all_gather | solution.py:63
  156.8 1.1 copy-start.5
  156.8 2.2 copy-start.8
  156.9 2.3 copy-start.9
  156.9 2.3 copy-start.10
  159.0 187.1 %reduce-scatter.5.cloned.1.call-start = ((), (), s32[]{:S(2)}) async-start(), calls=%async_computation.4 | async-start | bytes 4718592 | tf_op jit(solution)/shard_map/reduce_scatter | solution.py:100
  245.1 5.8 copy-start.4
  245.1 6.4 copy-start.6
  254.7 2.0 copy-start.2
  259.2 589.1 %reduce-scatter.7.cloned.1.call-start = ((), (), s32[]{:S(2)}) async-start(), calls=%async_computation.5 | async-start | bytes 31850496
  346.0 2.5 slice-start
  399.5 1.1 copy-start.7
  900.8 5.9 copy-start.3
  910.3 4.6 copy-start.1
Sparse Core Ops, SparseCore 0:
  10.7 140.8 all-gather.2
  159.1 73.1 all-gather.4
  259.3 86.6 reduce-scatter.4
  399.7 448.5 reduce-scatter.6
where the time goes:
time: 923 us; the launch traced here: 921 us
  waiting for transfers between devices  743 us (80%)
  local copies, waits for them, and re-layouts  56.9 us (6%)
  matrix products  41.6 us (5%)
  blocking collectives  39.5 us (4%)
  other arithmetic  25.1 us (3%)
  between operations  14.8 us (2%)
    unnamed x5, waiting for transfers between devices  447 us
    all_gather x1, waiting for transfers between devices, on_device(): lax.all_gather(w_qkv, 'seq', axis=1, tiled=True)  142 us
    reduce_scatter x1, waiting for transfers between devices, on_device(): lax.psum_scatter(key_terms.astype(jnp.bfloat16), 'seq', scatter_dimension...  82.1 us
    all_gather x1, waiting for transfers between devices, on_device(): all_kv = lax.all_gather(local_kv, 'seq', axis=0, tiled=True)  72.1 us
    unnamed x29, local copies, waits for them, and re-layouts  51.5 us
    psum x1, blocking collectives, on_device(): fisher_sum = lax.psum(jnp.sum(fisher), ('seq', 'head'))  39.5 us
  transfers between devices with their start and end apart: 4, of which 4 were waited for; matrix products, arithmetic and copies ran while one was open for 1% of the time, Pallas kernels for 0%

commit v1 on v0

--- a/solution.py
+++ b/solution.py
@@ -1,19 +1,24 @@
+import functools
 import math
 
 import jax
 import jax.numpy as jnp
 from jax import lax
+from jax.experimental import pallas as pl
+from jax.experimental.pallas import tpu as pltpu
 from jax.sharding import PartitionSpec as P
 
 D = 3072
 HD = 128
 HEADS = 16
 CLIPS = 3
+EPS = 1e-6
+AXES = ("seq", "head")
 
 
 def normed(values, gain_row, head_count):
     shaped = values.reshape(values.shape[0], head_count, HD)
-    inverse = lax.rsqrt(jnp.mean(shaped * shaped, -1, keepdims=True) + 1e-06)
+    inverse = lax.rsqrt(jnp.mean(shaped * shaped, -1, keepdims=True) + EPS)
     return (shaped * inverse * gain_row.reshape(head_count, HD), inverse, shaped)
 
 
@@ -35,7 +40,7 @@
     )
 
 
-def on_device(tokens, w_qkv, gains, cotangent, token_clip, key_live, damp_mask):
+def row_sharded(tokens, w_qkv, gains, cotangent, token_clip, key_live, damp_mask):
     tok_rows = tokens.shape[0]
     width_dev = w_qkv.shape[2]
     rows_dev = w_qkv.shape[1]
@@ -43,10 +48,9 @@
     all_tokens = token_clip.shape[0]
     seq_rank = lax.axis_index("seq")
     score_scale = 1.0 / math.sqrt(HD)
-    columns = tokens
     projected = jnp.einsum(
         "tr,jrc->jtc",
-        columns,
+        tokens,
         lax.all_gather(w_qkv, "seq", axis=1, tiled=True),
         preferred_element_type=jnp.float32,
     )
@@ -117,10 +121,9 @@
         1,
     ).astype(jnp.bfloat16)
     masked = by_clip(grad_proj, clip_here)
-    columns = tokens
     per_clip = lax.psum_scatter(
         lax.dot_general(
-            columns, masked, (((0,), (0,)), ((), ())), preferred_element_type=jnp.float32
+            tokens, masked, (((0,), (0,)), ((), ())), preferred_element_type=jnp.float32
         ).astype(jnp.bfloat16),
         "seq",
         scatter_dimension=0,
@@ -128,16 +131,411 @@
     ).astype(jnp.float32)
     fisher = jnp.sum(jnp.square(per_clip.reshape(rows_dev, CLIPS, 3, width_dev)), 1)
     fisher = jnp.transpose(fisher, (1, 0, 2))
-    fisher_sum = lax.psum(jnp.sum(fisher), ("seq", "head"))
+    fisher_sum = lax.psum(jnp.sum(fisher), AXES)
     fisher_mean = fisher_sum / (3 * D * HEADS * HD)
-    fisher_ratio = fisher / (fisher_mean + 1e-06)
+    fisher_ratio = fisher / (fisher_mean + EPS)
     dampened = (
         w_qkv.astype(jnp.float32) / (1.0 + damp_mask.astype(jnp.float32)[None] * fisher_ratio)
     ).astype(jnp.bfloat16)
     return (fisher_ratio, dampened)
 
 
+def project_kernel(nb, tb, rows, quarter, place, *refs):
+    chunks = refs[:nb]
+    pieces = refs[nb : nb + quarter]
+    out32, out16 = refs[nb + quarter : nb + quarter + 2]
+    xs, ws, xsem, wsem = refs[nb + quarter + 2 :]
+    wcopies = []
+    for k in range(quarter):
+        start = pl.multiple_of(place[nb + k] * rows, rows)
+        for j in range(3):
+            wcopies.append(
+                pltpu.make_async_copy(
+                    pieces[k].at[pl.ds(j * rows, rows)],
+                    ws.at[pl.ds(start, rows), pl.ds(j * HD, HD)],
+                    wsem.at[k, j],
+                )
+            )
+    xcopies = [
+        pltpu.make_async_copy(chunks[b], xs.at[b], xsem.at[b]) for b in range(nb)
+    ]
+    for copy in wcopies:
+        copy.start()
+    for copy in xcopies:
+        copy.start()
+    for copy in wcopies:
+        copy.wait()
+    for b in range(nb):
+        xcopies[b].wait()
+        part = jnp.dot(xs[b], ws[...], preferred_element_type=jnp.float32)
+        here = pl.ds(pl.multiple_of(place[b] * tb, tb), tb)
+        out32[here, :] = part
+        out16[here, :] = part.astype(jnp.bfloat16)
+
+
+def head_kernel(nb, tb, rows, quarter, place, edges, *refs):
+    chunks = refs[:nb]
+    cots = refs[nb : nb + quarter]
+    cot_other, mine, other, gain, clip_row, key_code = refs[nb + quarter : nb + quarter + 6]
+    fisher_out, sum_out = refs[nb + quarter + 6 : nb + quarter + 8]
+    (xs, do, proj, qn, kn, vb, qn_t, kn_t, do_t, es, dps, dk, dv, dproj, grads, xsem, csem) = refs[
+        nb + quarter + 8 :
+    ]
+    scale = 1.0 / math.sqrt(HD)
+    cot_copies = []
+    for k in range(quarter):
+        for side in range(2):
+            src = (
+                cots[k].at[pl.ds(3 * rows, tb)]
+                if side == 0
+                else cot_other.at[pl.ds(k * tb, tb)]
+            )
+            block = place[nb + quarter * (1 + side) + k]
+            cot_copies.append(
+                pltpu.make_async_copy(
+                    src, do.at[pl.ds(pl.multiple_of(block * tb, tb), tb)], csem.at[side, k]
+                )
+            )
+    xcopies = [
+        pltpu.make_async_copy(
+            chunks[b], xs.at[pl.ds(pl.multiple_of(place[b] * tb, tb), tb)], xsem.at[b]
+        )
+        for b in range(nb)
+    ]
+    for copy in cot_copies + xcopies:
+        copy.start()
+
+    def normalise(b, carry):
+        here = pl.ds(pl.multiple_of(b * tb, tb), tb)
+        total = mine[here, :] + other[here, :].astype(jnp.float32)
+        proj[here, :] = total[:, : 2 * HD]
+        for j, (flat, turned) in enumerate(((qn, qn_t), (kn, kn_t))):
+            raw = total[:, j * HD : (j + 1) * HD]
+            inv = lax.rsqrt(jnp.mean(raw * raw, -1, keepdims=True) + EPS)
+            value = raw * inv * gain[j : j + 1, :]
+            flat[here, :] = value.astype(jnp.bfloat16)
+            turned[b] = value.T.astype(jnp.bfloat16)
+        vb[here, :] = total[:, 2 * HD :].astype(jnp.bfloat16)
+        return carry
+
+    lax.fori_loop(0, nb, normalise, 0)
+    for copy in cot_copies:
+        copy.wait()
+
+    def prepare(b, carry):
+        here = pl.ds(pl.multiple_of(b * tb, tb), tb)
+        do_t[b] = do[here, :].astype(jnp.float32).T.astype(jnp.bfloat16)
+        dk[here, :] = jnp.zeros((tb, HD), jnp.float32)
+        dv[here, :] = jnp.zeros((tb, HD), jnp.float32)
+        return carry
+
+    lax.fori_loop(0, nb, prepare, 0)
+
+    def backward_norm(upstream, here, j):
+        raw = proj[here, j * HD : (j + 1) * HD]
+        inv = lax.rsqrt(jnp.mean(raw * raw, -1, keepdims=True) + EPS)
+        weighted = gain[j : j + 1, :] * upstream
+        cubed = inv * inv * inv
+        return inv * weighted - raw * (cubed * jnp.mean(raw * weighted, -1, keepdims=True))
+
+    offset = lax.broadcasted_iota(jnp.int32, (tb, tb), 0) - lax.broadcasted_iota(
+        jnp.int32, (tb, tb), 1
+    )
+
+    def queries(i, carry):
+        rows_q = pl.ds(pl.multiple_of(i * tb, tb), tb)
+        q_t = qn_t[i]
+        d_t = do_t[i]
+        clip_q = clip_row[i]
+        first, last = edges[i], edges[nb + i]
+
+        def overlap(j):
+            return (edges[j] <= last) & (edges[nb + j] >= first)
+
+        def forward(j, sums):
+            def tile():
+                here = pl.ds(pl.multiple_of(j * tb, tb), tb)
+                s = jnp.dot(kn[here, :], q_t, preferred_element_type=jnp.float32)
+                allowed = (key_code[here, :] == clip_q) | (offset == (i - j) * tb)
+                e = jnp.where(allowed, jnp.exp2(s * (scale * math.log2(math.e))), 0.0)
+                dp = jnp.dot(vb[here, :], d_t, preferred_element_type=jnp.float32)
+                es[here, :] = e
+                dps[here, :] = dp
+                return (
+                    sums[0] + jnp.sum(e.reshape(tb // 8, 8, tb), 0),
+                    sums[1] + jnp.sum((e * dp).reshape(tb // 8, 8, tb), 0),
+                )
+
+            return lax.cond(overlap(j), tile, lambda: sums)
+
+        zero = jnp.zeros((8, tb), jnp.float32)
+        sum_e, sum_edp = lax.fori_loop(0, nb, forward, (zero, zero))
+        inv_l = 1.0 / jnp.sum(sum_e, 0, keepdims=True)
+        row_dot = jnp.sum(sum_edp, 0, keepdims=True) * inv_l
+        q_b = qn[rows_q, :]
+        d_b = do[rows_q, :]
+
+        def backward(j, dq_t):
+            def tile():
+                here = pl.ds(pl.multiple_of(j * tb, tb), tb)
+                p = es[here, :] * inv_l
+                ds = (p * (dps[here, :] - row_dot)).astype(jnp.bfloat16)
+                dv[here, :] += jnp.dot(
+                    p.astype(jnp.bfloat16), d_b, preferred_element_type=jnp.float32
+                )
+                dk[here, :] += jnp.dot(ds, q_b, preferred_element_type=jnp.float32)
+                return dq_t + jnp.dot(kn_t[j], ds, preferred_element_type=jnp.float32)
+
+            return lax.cond(overlap(j), tile, lambda: dq_t)
+
+        dq_t = lax.fori_loop(0, nb, backward, jnp.zeros((HD, tb), jnp.float32))
+        dproj[rows_q, :HD] = backward_norm(dq_t.T * scale, rows_q, 0).astype(jnp.bfloat16)
+        return carry
+
+    lax.fori_loop(0, nb, queries, 0)
+
+    def keys(b, carry):
+        here = pl.ds(pl.multiple_of(b * tb, tb), tb)
+        dproj[here, HD : 2 * HD] = backward_norm(dk[here, :] * scale, here, 1).astype(jnp.bfloat16)
+        dproj[here, 2 * HD :] = dv[here, :].astype(jnp.bfloat16)
+        return carry
+
+    lax.fori_loop(0, nb, keys, 0)
+    grads[...] = jnp.zeros_like(grads)
+    for copy in xcopies:
+        copy.wait()
+
+    def gradient(b, carry):
+        here = pl.ds(pl.multiple_of(b * tb, tb), tb)
+        turned = dproj[here, :].astype(jnp.float32).T
+
+        def one_clip(clip, carry):
+            part = jnp.where(clip_row[b] == clip, turned, 0.0).astype(jnp.bfloat16)
+            grads[clip] += jnp.dot(part, xs[here, :], preferred_element_type=jnp.float32)
+            return carry
+
+        lax.fori_loop(edges[b], edges[nb + b] + 1, one_clip, 0)
+        return carry
+
+    lax.fori_loop(0, nb, gradient, 0)
+    running = jnp.zeros((HD, rows), jnp.float32)
+    for block in range(quarter):
+        slot = place[nb + 3 * quarter + block]
+        for j in range(3):
+            span = (pl.ds(j * HD, HD), pl.ds(block * rows, rows))
+            squares = jnp.zeros((HD, rows), jnp.float32)
+            for clip in range(CLIPS):
+                g = grads[clip, span[0], span[1]]
+                squares += g * g
+            running += squares
+            fisher_out[slot, j * rows : (j + 1) * rows, :] = squares.T.astype(jnp.bfloat16)
+    sum_out[...] = jnp.full((8, HD), jnp.sum(running), jnp.float32)
+
+
+def finish_kernel(quarter, rows, shift, *refs):
+    pieces = refs[:quarter]
+    total, w, mask, ratio_out, damp_out = refs[quarter:]
+    lane = pl.program_id(0)
+    mean = total[0, 0] * (1.0 / (3 * D * HEADS * HD))
+    factor = 1.0 / jnp.full((1, HD), mean + EPS, jnp.float32)
+    damp = mask[...].astype(jnp.float32)
+    for k in range(quarter):
+
+        @pl.when(lax.rem(shift[0] + k, quarter) == lane)
+        def _():
+            for j in range(3):
+                ratio = pieces[k][j * rows : (j + 1) * rows, :].astype(jnp.float32) * factor
+                ratio_out[j] = ratio
+                damp_out[j] = (w[j].astype(jnp.float32) / (1.0 + damp * ratio)).astype(
+                    jnp.bfloat16
+                )
+
+
+def chip_per_head(tokens, w_qkv, gains, cotangent, token_clip, key_live, damp_mask, *, ns, nh):
+    tb, width = tokens.shape
+    rows, cols = w_qkv.shape[1:]
+    quarter = cols // HD
+    half = width // 2
+    all_tokens = token_clip.shape[0]
+    s = lax.axis_index("seq")
+    h = lax.axis_index("head")
+    core = h % 2
+    vmem = pl.BlockSpec(memory_space=pltpu.VMEM)
+    smem = pl.BlockSpec(memory_space=pltpu.SMEM)
+    hbm = pl.BlockSpec(memory_space=pl.ANY)
+
+    def index(si, hi):
+        return si * nh + hi
+
+    swap = [(index(a, b), index(a, b ^ 1)) for a in range(ns) for b in range(nh)]
+    out_perms = []
+    for k in range(quarter):
+        out_perms.append(
+            [
+                (index(a, b), index((b % 2) * quarter + (k + a) % quarter, b - b % 2 + a // quarter))
+                for a in range(ns)
+                for b in range(nh)
+            ]
+        )
+    back_perms = [[(b, a) for a, b in perm] for perm in out_perms]
+
+    gains_other = lax.ppermute(gains, AXES, swap)
+    pieces = []
+    for k in range(quarter):
+        col = ((k + s) % quarter) * HD
+        piece = jnp.concatenate(
+            [
+                lax.dynamic_slice_in_dim(w_qkv, col, HD, 2).reshape(3 * rows, HD),
+                lax.dynamic_slice_in_dim(cotangent, col, HD, 1),
+            ],
+            0,
+        )
+        pieces.append(lax.ppermute(piece, AXES, out_perms[k]))
+
+    ring = list(range(0, ns, 2)) + list(range(1, ns, 2))[::-1]
+    forth = [(ring[i], ring[(i + 1) % ns]) for i in range(ns)]
+    back = [(b, a) for a, b in forth]
+    position = [ring.index(i) for i in range(ns)]
+    mine = lax.dynamic_slice_in_dim(tokens, core * half, half, 1)
+    chunks, steps = [mine], [0]
+    ahead = behind = mine
+    for step in range(1, ns // 2):
+        ahead = lax.ppermute(ahead, "seq", forth)
+        behind = lax.ppermute(behind, "seq", back)
+        chunks += [ahead, behind]
+        steps += [-step, step]
+    chunks.append(
+        jnp.concatenate(
+            [
+                lax.ppermute(ahead[: tb // 2], "seq", forth),
+                lax.ppermute(behind[tb // 2 :], "seq", back),
+            ],
+            0,
+        )
+    )
+    steps.append(ns // 2)
+    order = jnp.array([[ring[(position[i] + d) % ns] for d in steps] for i in range(ns)], jnp.int32)
+    ks = jnp.arange(quarter, dtype=jnp.int32)
+    row_block = (s - ks) % quarter
+    place = jnp.concatenate(
+        [
+            lax.dynamic_index_in_dim(order, s, 0, False),
+            row_block,
+            row_block + core * quarter,
+            row_block + (1 - core) * quarter,
+            (s - ks) % quarter,
+        ]
+    ).astype(jnp.int32)
+
+    cot_mine = jnp.concatenate([p[3 * rows :] for p in pieces], 0)
+    cot_other = lax.ppermute(cot_mine, AXES, swap)
+
+    params = pltpu.CompilerParams(vmem_limit_bytes=56 * 1024 * 1024)
+    bf16, f32 = jnp.bfloat16, jnp.float32
+    part32, part16 = pl.pallas_call(
+        functools.partial(project_kernel, ns, tb, rows, quarter),
+        out_shape=(
+            jax.ShapeDtypeStruct((all_tokens, 3 * HD), f32),
+            jax.ShapeDtypeStruct((all_tokens, 3 * HD), bf16),
+        ),
+        in_specs=[smem] + [hbm] * (ns + quarter),
+        out_specs=(vmem, vmem),
+        scratch_shapes=[
+            pltpu.VMEM((ns, tb, half), bf16),
+            pltpu.VMEM((half, 3 * HD), bf16),
+            pltpu.SemaphoreType.DMA((ns,)),
+            pltpu.SemaphoreType.DMA((quarter, 3)),
+        ],
+        compiler_params=params,
+        name="project",
+    )(place, *chunks, *pieces)
+    other = lax.ppermute(part16, AXES, swap)
+
+    own_gain = (s // quarter) == core
+    gain = lax.dynamic_slice_in_dim(
+        jnp.where(own_gain, gains, gains_other), (s % quarter) * HD, HD, 1
+    )
+    clip_row = token_clip.reshape(ns, 1, tb)
+    key_code = jnp.where(key_live == 1, token_clip, -1)[:, None]
+    blocks = token_clip.reshape(ns, tb)
+    edges = jnp.concatenate([blocks[:, 0], blocks[:, -1]])
+    fisher, part_sum = pl.pallas_call(
+        functools.partial(head_kernel, ns, tb, rows, quarter),
+        out_shape=(
+            jax.ShapeDtypeStruct((quarter, 3 * rows, HD), bf16),
+            jax.ShapeDtypeStruct((8, HD), f32),
+        ),
+        in_specs=[smem, smem] + [hbm] * (ns + quarter + 1) + [vmem] * 5,
+        out_specs=(vmem, vmem),
+        scratch_shapes=[
+            pltpu.VMEM((all_tokens, half), bf16),
+            pltpu.VMEM((all_tokens, HD), bf16),
+            pltpu.VMEM((all_tokens, 2 * HD), f32),
+            pltpu.VMEM((all_tokens, HD), bf16),
+            pltpu.VMEM((all_tokens, HD), bf16),
+            pltpu.VMEM((all_tokens, HD), bf16),
+            pltpu.VMEM((ns, HD, tb), bf16),
+            pltpu.VMEM((ns, HD, tb), bf16),
+            pltpu.VMEM((ns, HD, tb), bf16),
+            pltpu.VMEM((all_tokens, tb), f32),
+            pltpu.VMEM((all_tokens, tb), f32),
+            pltpu.VMEM((all_tokens, HD), f32),
+            pltpu.VMEM((all_tokens, HD), f32),
+            pltpu.VMEM((all_tokens, 3 * HD), bf16),
+            pltpu.VMEM((CLIPS, 3 * HD, half), f32),
+            pltpu.SemaphoreType.DMA((ns,)),
+            pltpu.SemaphoreType.DMA((2, quarter)),
+        ],
+        compiler_params=params,
+        name="head",
+    )(place, edges, *chunks, *pieces, cot_other, part32, other, gain, clip_row, key_code)
+
+    returned = [lax.ppermute(fisher[k], AXES, back_perms[k]) for k in range(quarter)]
+    total = part_sum[:1]
+    bit = 1
+    while bit < nh:
+        total = total + lax.ppermute(total, "head", [(i, i ^ bit) for i in range(nh)])
+        bit *= 2
+    bit = 1
+    while bit < ns:
+        total = total + lax.ppermute(total, "seq", [(i, i ^ bit) for i in range(ns)])
+        bit *= 2
+    shift = (s % quarter).astype(jnp.int32).reshape(1)
+    full = lambda i, shift: (0, 0)
+    lanes = lambda i, shift: (0, 0, i)
+    return pl.pallas_call(
+        functools.partial(finish_kernel, quarter, rows),
+        out_shape=(
+            jax.ShapeDtypeStruct((3, rows, cols), f32),
+            jax.ShapeDtypeStruct((3, rows, cols), bf16),
+        ),
+        grid_spec=pltpu.PrefetchScalarGridSpec(
+            num_scalar_prefetch=1,
+            grid=(quarter,),
+            in_specs=[pl.BlockSpec((3 * rows, HD), full)] * quarter
+            + [
+                pl.BlockSpec((1, HD), full, memory_space=pltpu.SMEM),
+                pl.BlockSpec((3, rows, HD), lanes),
+                pl.BlockSpec((rows, HD), lambda i, shift: (0, i)),
+            ],
+            out_specs=(
+                pl.BlockSpec((3, rows, HD), lanes),
+                pl.BlockSpec((3, rows, HD), lanes),
+            ),
+        ),
+        compiler_params=params,
+        name="finish",
+    )(shift, *returned, total, w_qkv, damp_mask)
+
+
 def solution(mesh):
+    ns, nh = mesh.shape["seq"], mesh.shape["head"]
+
+    def on_device(*args):
+        if ns == 2 * (args[1].shape[2] // HD) and ns & (ns - 1) == 0 and nh % 2 == 0:
+            return chip_per_head(*args, ns=ns, nh=nh)
+        return row_sharded(*args)
+
     return jax.shard_map(
         on_device,
         mesh=mesh,

time: 923 us -> 201 us (0.22)
  waiting for transfers between devices: 743 us -> 84 us
  Pallas kernels: 0 us -> 53.5 us
  matrix products: 41.6 us -> 0 us
  local copies, waits for them, and re-layouts: 56.9 us -> 17 us
  blocking collectives: 39.5 us -> 0 us
  starting transfers between devices: 0.34 us -> 38.1 us
  other arithmetic: 25.1 us -> 6.74 us
  between operations: 14.8 us -> 0.94 us
    unnamed x5 -> x0, waiting for transfers between devices: 447 us -> none
    all_gather x2 -> x0, waiting for transfers between devices: 214 us -> none  [the longest x1 142 us: on_device(): lax.all_gather(w_qkv, 'seq', axis=1, tiled=True)]
    ppermute x0 -> x24, waiting for transfers between devices: none -> 84 us  [the longest x3 40.6 us: chip_per_head(): ahead = lax.ppermute(ahead, 'seq', forth)]
    reduce_scatter x1 -> x0, waiting for transfers between devices: 82.1 us -> none  [on_device(): lax.psum_scatter(key_terms.astype(jnp.bfloat16), 'seq', scatter_dimension...]
    pallas_call x0 -> x3, Pallas kernels: none -> 53.5 us  [the longest x1 38.1 us: chip_per_head(): pl.pallas_call(functools.partial(head_kernel, ns, tb, rows, quarter), out...]
    unnamed x29 -> x35, local copies, waits for them, and re-layouts: 51.5 us -> 5.39 us
    psum x1 -> x0, blocking collectives: 39.5 us -> none  [on_device(): fisher_sum = lax.psum(jnp.sum(fisher), ('seq', 'head'))]
    ppermute x0 -> x24, starting transfers between devices: none -> 38.1 us  [the longest x1 7.17 us: chip_per_head(): lax.ppermute(ahead[:tb // 2], 'seq', forth)]
  transfers between devices with their start and end apart: 4 -> 24, of which waited for: 4 -> 12; matrix products, arithmetic and copies ran while one was open for 1% -> 9% of each run, Pallas kernels for 0% -> 0%
where the time goes in v1:
time: 201 us; the launch traced here: 200 us
  waiting for transfers between devices  84 us (42%)
  Pallas kernels  53.5 us (27%)
  starting transfers between devices  38.1 us (19%)
  local copies, waits for them, and re-layouts  17 us (8%)
  other arithmetic  6.74 us (3%)
    ppermute x3, waiting for transfers between devices, chip_per_head(): ahead = lax.ppermute(ahead, 'seq', forth)  40.6 us
    pallas_call x1, Pallas kernels, chip_per_head(): pl.pallas_call(functools.partial(head_kernel, ns, tb, rows, quarter), out...  38.1 us
    ppermute x4, waiting for transfers between devices, chip_per_head(): pieces.append(lax.ppermute(piece, AXES, out_perms[k]))  14 us
    ppermute x1, waiting for transfers between devices, chip_per_head(): lax.ppermute(ahead[:tb // 2], 'seq', forth)  11.7 us
    ppermute x3, waiting for transfers between devices, chip_per_head(): lax.ppermute(total, 'seq', [(i, i ^ bit) for i in range(ns)])  10.9 us
    pallas_call x1, Pallas kernels, chip_per_head(): pl.pallas_call(functools.partial(project_kernel, ns, tb, rows, quarter),...  10.7 us
    ppermute x1, starting transfers between devices, chip_per_head(): lax.ppermute(ahead[:tb // 2], 'seq', forth)  7.17 us
    ppermute x4, starting transfers between devices, chip_per_head(): pieces.append(lax.ppermute(piece, AXES, out_perms[k]))  7.04 us
  transfers between devices with their start and end apart: 24, of which 12 were waited for; matrix products, arithmetic and copies ran while one was open for 9% of the time, Pallas kernels for 0%

profile of v1, /device:TPU:0, one launch (start us, length us, event | category | flops | bytes accessed | tf_op | source)
XLA Modules:
  0.0 200.3 jit_solution(9731678731283860116)
XLA Ops:
  0.7 1.4 copy-done
  2.1 3.1 %collective-permute-start = (bf16[256,1536]{1,0:T(8,128)(2,1)S(1)}, bf16[256,1536]{1,0:T(8,128)(2,1)}, u32[]{:S(2)}, u32[]{:S(2)}) collective-permute-start(bf16[256,1536]{1,0:T(8,128)(2,1)S(1)} %constant_dynamic-slice_fusion.10.refs_0_), channel_id=1, source_target_pairs={{0,8},{8,16},{16,24},{24,28},{28,20},{20,12},{12,4},{4,0},{1,9},{9... | collective-permute-start | bytes 2359304 | tf_op jit(solution)/shard_map/ppermute | solution.py:403
  5.2 17.6 %collective-permute-done.refs_1_ = bf16[256,1536]{1,0:T(8,128)(2,1)} collective-permute-done((bf16[256,1536]{1,0:T(8,128)(2,1)S(1)}, bf16[256,1536]{1,0:T(8,128)(2,1)}, u32[]{:S(2)}, u32[]{:S(2)}) %collective-permute-start) | collective-permute-done | bytes 786464 | tf_op jit(solution)/shard_map/ppermute | solution.py:403
  22.8 1.8 collective-permute-start.2
  24.6 0.2 collective-permute-start.3
  24.8 1.6 constant_dynamic-slice_fusion.2
  26.4 0.9 constant_dynamic-slice_fusion.3
  27.3 14.5 %collective-permute-done.2.refs_3_ = bf16[256,1536]{1,0:T(8,128)(2,1)} collective-permute-done((bf16[256,1536]{1,0:T(8,128)(2,1)}, bf16[256,1536]{1,0:T(8,128)(2,1)}, u32[]{:S(2)}, u32[]{:S(2)}) %collective-permute-start.2) | collective-permute-done | bytes 786464 | tf_op jit(solution)/shard_map/ppermute | solution.py:403
  41.8 1.5 collective-permute-start.4
  43.3 0.8 pad_maximum_fusion.2
  44.1 1.6 collective-permute-start.10
  45.7 0.4 collective-permute-start.5
  46.1 0.8 pad_maximum_fusion.3
  46.8 1.1 collective-permute-start.11
  47.9 0.8 pad_maximum_fusion
  48.6 4.4 %collective-permute-start.8 = (bf16[1408,128]{1,0:T(8,128)(2,1)}, bf16[1408,128]{1,0:T(8,128)(2,1)}, u32[]{:S(2)}, u32[]{:S(2)}) collective-permute-start(bf16[1408,128]{1,0:T(8,128)(2,1)} %pad_maximum_fusion), channel_id=1, source_target_pairs={{0,0},{1,16},{2,2},{3,18},{4,4},{5,20},{6,6},{7,22},{8,8},{9,24},{... | collective-permute-start | bytes 1081352 | tf_op jit(solution)/shard_map/ppermute | solution.py:393
  53.0 8.6 %collective-permute-done.4.refs_5_ = bf16[256,1536]{1,0:T(8,128)(2,1)S(1)} collective-permute-done((bf16[256,1536]{1,0:T(8,128)(2,1)}, bf16[256,1536]{1,0:T(8,128)(2,1)S(1)}, u32[]{:S(2)}, u32[]{:S(2)}) %collective-permute-start.4) | collective-permute-done | bytes 786464 | tf_op jit(solution)/shard_map/ppermute | solution.py:403
  61.6 0.8 slice.54
  62.4 7.2 %collective-permute-start.6 = (bf16[128,1536]{1,0:T(8,128)(2,1)}, bf16[128,1536]{1,0:T(8,128)(2,1)}, u32[]{:S(2)}, u32[]{:S(2)}) collective-permute-start(bf16[128,1536]{1,0:T(8,128)(2,1)} %slice.54), channel_id=1, source_target_pairs={{0,8},{8,16},{16,24},{24,28},{28,20},{20,12},{12,4},{4,0},{1,9},{9... | collective-permute-start | bytes 1179656 | tf_op jit(solution)/shard_map/ppermute | solution.py:410
  69.6 0.7 fusion.2
  70.3 0.6 concatenate.24.place
  70.9 1.5 collective-permute-done.5.refs_6_
  72.5 1.2 pad_maximum_fusion.1
  73.7 11.7 %collective-permute-done.6 = bf16[128,1536]{1,0:T(8,128)(2,1)} collective-permute-done((bf16[128,1536]{1,0:T(8,128)(2,1)}, bf16[128,1536]{1,0:T(8,128)(2,1)}, u32[]{:S(2)}, u32[]{:S(2)}) %collective-permute-start.6) | collective-permute-done | bytes 393248 | tf_op jit(solution)/shard_map/ppermute | solution.py:410
  85.5 1.0 constant_dynamic-update-slice_fusion.1
  86.5 2.3 %collective-permute-done.7 = bf16[128,1536]{1,0:T(8,128)(2,1)S(1)} collective-permute-done((bf16[128,1536]{1,0:T(8,128)(2,1)S(1)}, bf16[128,1536]{1,0:T(8,128)(2,1)S(1)}, u32[]{:S(2)}, u32[]{:S(2)}) %collective-permute-start.7) | collective-permute-done | bytes 393248 | tf_op jit(solution)/shard_map/ppermute | solution.py:411
  89.0 14.0 %collective-permute-done.9.refs_9_ = bf16[1408,128]{1,0:T(8,128)(2,1)S(1)} collective-permute-done((bf16[1408,128]{1,0:T(8,128)(2,1)S(1)}, bf16[1408,128]{1,0:T(8,128)(2,1)S(1)}, u32[]{:S(2)}, u32[]{:S(2)}) %collective-permute-start.9) | collective-permute-done | bytes 360480 | tf_op jit(solution)/shard_map/ppermute | solution.py:393
  102.9 0.7 copy-done.7
  103.7 10.7 %project.1 = (f32[2048,384]{1,0:T(8,128)}, bf16[2048,384]{1,0:T(8,128)(2,1)}) custom-call(s32[24]{0:T(128)} %concatenate.24.place, bf16[256,1536]{1,0:T(8,128)(2,1)} %copy-done.1, bf16[256,1536]{1,0:T(8,128)(2,1)} %collective-permute-done.refs_1_, bf16[256,1536]{1,0:T(8,128)(2,1)} %collective-permute-done.1.refs_2_, ...), custom_call_target="tpu_custom_call" | custom-call | tf_op jit(solution)/shard_map/project/pallas_call | solution.py:435
  114.5 0.5 collective-permute-start.14
  115.0 0.8 slice.56
  115.8 0.8 slice.57
  116.7 0.8 slice.58
  117.5 0.8 slice.59
  118.4 0.7 pad_maximum_fusion.4
  119.2 0.2 slice_reduce_fusion.1
  119.4 0.6 pad_add_fusion.edges
  120.0 1.4 copy.11.refs_17_
  121.4 0.6 fusion.refs_15_
  122.0 0.7 copy-done.13
  122.7 0.5 copy-done.8
  123.2 38.1 %head.1 = (bf16[4,1152,128]{2,1,0:T(8,128)(2,1)}, f32[8,128]{1,0:T(8,128)}) custom-call(s32[24]{0:T(128)} %concatenate.24.place, s32[16]{0:T(128)} %pad_add_fusion.edges, bf16[256,1536]{1,0:T(8,128)(2,1)} %copy-done.1, bf16[256,1536]{1,0:T(8,128)(2,1)} %collective-permute-done.refs_1_, bf16[256,1536]{1,0:T(8,128)(2,1)} %collective-permute-done.1.refs_2_, ...), custom_call_target="tpu_custom_call" | custom-call | tf_op jit(solution)/shard_map/head/pallas_call | solution.py:462
  161.3 1.3 slice_bitcast_fusion
  162.6 0.7 collective-permute-start.15
  163.3 2.1 %collective-permute-start.16 = (bf16[1152,128]{1,0:T(8,128)(2,1)S(1)}, bf16[1152,128]{1,0:T(8,128)(2,1)S(1)}, u32[]{:S(2)}, u32[]{:S(2)}) collective-permute-start(bf16[1152,128]{1,0:T(8,128)(2,1)S(1)} %get-tuple-element.14), channel_id=1, source_target_pairs={{4,0},{20,1},{6,2},{22,3},{8,4},{24,5},{10,6},{26,7},{12,8},{28,9}... | collective-permute-start | bytes 884744 | tf_op jit(solution)/shard_map/ppermute | solution.py:493
  165.4 2.3 %collective-permute-start.17 = (bf16[1152,128]{1,0:T(8,128)(2,1)S(1)}, bf16[1152,128]{1,0:T(8,128)(2,1)S(1)}, u32[]{:S(2)}, u32[]{:S(2)}) collective-permute-start(bf16[1152,128]{1,0:T(8,128)(2,1)S(1)} %get-tuple-element.13), channel_id=1, source_target_pairs={{8,0},{24,1},{10,2},{26,3},{12,4},{28,5},{14,6},{30,7},{0,8},{16,9... | collective-permute-start | bytes 884744 | tf_op jit(solution)/shard_map/ppermute | solution.py:493
  167.7 0.7 slice.51
  168.3 3.5 %collective-permute-start.19 = (f32[1,128]{1,0:T(1,128)S(1)}, f32[1,128]{1,0:T(1,128)S(1)}, u32[]{:S(2)}, u32[]{:S(2)}) collective-permute-start(f32[1,128]{1,0:T(1,128)S(1)} %slice.51), channel_id=1, source_target_pairs={{0,1},{1,0},{2,3},{3,2},{4,5},{5,4},{6,7},{7,6},{8,9},{9,8},{10,11... | collective-permute-start | bytes 1544 | tf_op jit(solution)/shard_map/ppermute | solution.py:497
  171.9 0.8 collective-permute-done.19
  172.7 0.7 slice_add_fusion
  173.4 1.5 collective-permute-start.20
  174.9 2.1 %collective-permute-done.20 = f32[1,128]{1,0:T(1,128)S(1)} collective-permute-done((f32[1,128]{1,0:T(1,128)S(1)}, f32[1,128]{1,0:T(1,128)S(1)}, u32[]{:S(2)}, u32[]{:S(2)}) %collective-permute-start.20) | collective-permute-done | bytes 544 | tf_op jit(solution)/shard_map/ppermute | solution.py:497
  176.9 2.9 %collective-permute-start.21 = (f32[1,128]{1,0:T(1,128)S(1)}, f32[1,128]{1,0:T(1,128)S(1)}, u32[]{:S(2)}, u32[]{:S(2)}) collective-permute-start(f32[1,128]{1,0:T(1,128)S(1)} %add.103), channel_id=1, source_target_pairs={{0,4},{4,0},{8,12},{12,8},{16,20},{20,16},{24,28},{28,24},{1,5},{5... | collective-permute-start | bytes 1544 | tf_op jit(solution)/shard_map/ppermute | solution.py:501
  179.8 1.5 collective-permute-done.21
  181.3 0.6 collective-permute-start.22
  182.0 3.0 %collective-permute-done.22 = f32[1,128]{1,0:T(1,128)S(1)} collective-permute-done((f32[1,128]{1,0:T(1,128)S(1)}, f32[1,128]{1,0:T(1,128)S(1)}, u32[]{:S(2)}, u32[]{:S(2)}) %collective-permute-start.22) | collective-permute-done | bytes 544 | tf_op jit(solution)/shard_map/ppermute | solution.py:501
  185.0 2.6 %collective-permute-start.23 = (f32[1,128]{1,0:T(1,128)S(1)}, f32[1,128]{1,0:T(1,128)S(1)}, u32[]{:S(2)}, u32[]{:S(2)}) collective-permute-start(f32[1,128]{1,0:T(1,128)S(1)} %add.105), channel_id=1, source_target_pairs={{0,16},{4,20},{8,24},{12,28},{16,0},{20,4},{24,8},{28,12},{1,17},{... | collective-permute-start | bytes 1544 | tf_op jit(solution)/shard_map/ppermute | solution.py:501
  187.6 6.4 %collective-permute-done.23 = f32[1,128]{1,0:T(1,128)S(1)} collective-permute-done((f32[1,128]{1,0:T(1,128)S(1)}, f32[1,128]{1,0:T(1,128)S(1)}, u32[]{:S(2)}, u32[]{:S(2)}) %collective-permute-start.23) | collective-permute-done | bytes 544 | tf_op jit(solution)/shard_map/ppermute | solution.py:501
  194.0 0.6 add.106.refs_4_
  194.6 0.6 copy-done.9
  195.3 0.1 copy-done.10
  195.4 0.1 copy-done.11
  195.5 0.1 copy-done.12
  195.6 4.7 %finish.1 = (f32[3,384,512]{2,1,0:T(8,128)}, bf16[3,384,512]{2,1,0:T(8,128)(2,1)}) custom-call(s32[1]{0:T(128)} %bitcast.shift, bf16[1152,128]{1,0:T(8,128)(2,1)} %copy-done.9, bf16[1152,128]{1,0:T(8,128)(2,1)} %copy-done.10, bf16[1152,128]{1,0:T(8,128)(2,1)} %copy-done.11, bf16[1152,128]{1,0:T(8,128)(2,1)} %copy-done.12, f32[1,128]{1,0:T(1,128)} %add.106.refs_4_, ...), custom_call_target="tpu_custom_call" | custom-call | tf_op jit(solution)/shard_map/finish/pallas_call | solution.py:506
  (54 shorter events, 0.5 us)
Async XLA Ops:
  0.6 1.4 copy-start
  0.6 25.7 %copy-start.5 = (bf16[3,384,512]{2,1,0:T(8,128)(2,1)S(1)}, bf16[3,384,512]{2,1,0:T(8,128)(2,1)}, u32[]{:S(2)}) copy-start(bf16[3,384,512]{2,1,0:T(8,128)(2,1)} %refs_5_.1) | copy-start | bytes 3538948
  2.1 42.0 %copy-start.1 = (bf16[256,1536]{1,0:T(8,128)(2,1)}, bf16[256,1536]{1,0:T(8,128)(2,1)S(1)}, u32[]{:S(2)}) copy-start(bf16[256,1536]{1,0:T(8,128)(2,1)S(1)} %constant_dynamic-slice_fusion.10.refs_0_) | copy-start | bytes 2359300
  2.1 20.7 %collective-permute-start = (bf16[256,1536]{1,0:T(8,128)(2,1)S(1)}, bf16[256,1536]{1,0:T(8,128)(2,1)}, u32[]{:S(2)}, u32[]{:S(2)}) collective-permute-start(bf16[256,1536]{1,0:T(8,128)(2,1)S(1)} %constant_dynamic-slice_fusion.10.refs_0_), channel_id=1, source_target_pairs={{0,8},{8,16},{16,24},{24,28},{28,20},{20,12},{12,4},{4,0},{1,9},{9... | collective-permute-start | bytes 2359304 | tf_op jit(solution)/shard_map/ppermute | solution.py:403
  5.2 19.4 %collective-permute-start.1 = (bf16[256,1536]{1,0:T(8,128)(2,1)S(1)}, bf16[256,1536]{1,0:T(8,128)(2,1)}, u32[]{:S(2)}, u32[]{:S(2)}) collective-permute-start(bf16[256,1536]{1,0:T(8,128)(2,1)S(1)} %constant_dynamic-slice_fusion.10.refs_0_), channel_id=1, source_target_pairs={{8,0},{16,8},{24,16},{28,24},{20,28},{12,20},{4,12},{0,4},{9,1},{1... | collective-permute-start | bytes 2359304 | tf_op jit(solution)/shard_map/ppermute | solution.py:404
  22.8 19.0 %collective-permute-start.2 = (bf16[256,1536]{1,0:T(8,128)(2,1)}, bf16[256,1536]{1,0:T(8,128)(2,1)}, u32[]{:S(2)}, u32[]{:S(2)}) collective-permute-start(bf16[256,1536]{1,0:T(8,128)(2,1)} %collective-permute-done.refs_1_), channel_id=1, source_target_pairs={{0,8},{8,16},{16,24},{24,28},{28,20},{20,12},{12,4},{4,0},{1,9},{9... | collective-permute-start | bytes 2359304 | tf_op jit(solution)/shard_map/ppermute | solution.py:403
  24.6 21.1 %collective-permute-start.3 = (bf16[256,1536]{1,0:T(8,128)(2,1)}, bf16[256,1536]{1,0:T(8,128)(2,1)}, u32[]{:S(2)}, u32[]{:S(2)}) collective-permute-start(bf16[256,1536]{1,0:T(8,128)(2,1)} %collective-permute-done.1.refs_2_), channel_id=1, source_target_pairs={{8,0},{16,8},{24,16},{28,24},{20,28},{12,20},{4,12},{0,4},{9,1},{1... | collective-permute-start | bytes 2359304 | tf_op jit(solution)/shard_map/ppermute | solution.py:404
  41.8 19.8 %collective-permute-start.4 = (bf16[256,1536]{1,0:T(8,128)(2,1)}, bf16[256,1536]{1,0:T(8,128)(2,1)S(1)}, u32[]{:S(2)}, u32[]{:S(2)}) collective-permute-start(bf16[256,1536]{1,0:T(8,128)(2,1)} %collective-permute-done.2.refs_3_), channel_id=1, source_target_pairs={{0,8},{8,16},{16,24},{24,28},{28,20},{20,12},{12,4},{4,0},{1,9},{9... | collective-permute-start | bytes 2359304 | tf_op jit(solution)/shard_map/ppermute | solution.py:403
  44.1 44.8 %collective-permute-start.10 = (bf16[1408,128]{1,0:T(8,128)(2,1)}, bf16[1408,128]{1,0:T(8,128)(2,1)S(1)}, u32[]{:S(2)}, u32[]{:S(2)}) collective-permute-start(bf16[1408,128]{1,0:T(8,128)(2,1)} %pad_maximum_fusion.2), channel_id=1, source_target_pairs={{0,8},{1,24},{2,10},{3,26},{4,12},{5,28},{6,14},{7,30},{8,0},{9,16... | collective-permute-start | bytes 1081352 | tf_op jit(solution)/shard_map/ppermute | solution.py:393
  45.7 26.8 %collective-permute-start.5 = (bf16[256,1536]{1,0:T(8,128)(2,1)}, bf16[256,1536]{1,0:T(8,128)(2,1)S(1)}, u32[]{:S(2)}, u32[]{:S(2)}) collective-permute-start(bf16[256,1536]{1,0:T(8,128)(2,1)} %collective-permute-done.3.refs_4_), channel_id=1, source_target_pairs={{8,0},{16,8},{24,16},{28,24},{20,28},{12,20},{4,12},{0,4},{9,1},{1... | collective-permute-start | bytes 2359304 | tf_op jit(solution)/shard_map/ppermute | solution.py:404
  46.8 42.1 %collective-permute-start.11 = (bf16[1408,128]{1,0:T(8,128)(2,1)}, bf16[1408,128]{1,0:T(8,128)(2,1)}, u32[]{:S(2)}, u32[]{:S(2)}) collective-permute-start(bf16[1408,128]{1,0:T(8,128)(2,1)} %pad_maximum_fusion.3), channel_id=1, source_target_pairs={{0,12},{1,28},{2,14},{3,30},{4,0},{5,16},{6,2},{7,18},{8,4},{9,20}... | collective-permute-start | bytes 1081352 | tf_op jit(solution)/shard_map/ppermute | solution.py:393
  48.6 40.3 %collective-permute-start.8 = (bf16[1408,128]{1,0:T(8,128)(2,1)}, bf16[1408,128]{1,0:T(8,128)(2,1)}, u32[]{:S(2)}, u32[]{:S(2)}) collective-permute-start(bf16[1408,128]{1,0:T(8,128)(2,1)} %pad_maximum_fusion), channel_id=1, source_target_pairs={{0,0},{1,16},{2,2},{3,18},{4,4},{5,20},{6,6},{7,22},{8,8},{9,24},{... | collective-permute-start | bytes 1081352 | tf_op jit(solution)/shard_map/ppermute | solution.py:393
  61.6 27.2 %copy-start.2 = (bf16[256,1536]{1,0:T(8,128)(2,1)}, bf16[256,1536]{1,0:T(8,128)(2,1)S(1)}, u32[]{:S(2)}) copy-start(bf16[256,1536]{1,0:T(8,128)(2,1)S(1)} %collective-permute-done.4.refs_5_) | copy-start | bytes 2359300
  62.4 23.1 %collective-permute-start.6 = (bf16[128,1536]{1,0:T(8,128)(2,1)}, bf16[128,1536]{1,0:T(8,128)(2,1)}, u32[]{:S(2)}, u32[]{:S(2)}) collective-permute-start(bf16[128,1536]{1,0:T(8,128)(2,1)} %slice.54), channel_id=1, source_target_pairs={{0,8},{8,16},{16,24},{24,28},{28,20},{20,12},{12,4},{4,0},{1,9},{9... | collective-permute-start | bytes 1179656 | tf_op jit(solution)/shard_map/ppermute | solution.py:410
  72.4 30.5 %copy-start.3 = (bf16[256,1536]{1,0:T(8,128)(2,1)}, bf16[256,1536]{1,0:T(8,128)(2,1)S(1)}, u32[]{:S(2)}) copy-start(bf16[256,1536]{1,0:T(8,128)(2,1)S(1)} %collective-permute-done.5.refs_6_) | copy-start | bytes 2359300
  72.5 16.4 %collective-permute-start.7 = (bf16[128,1536]{1,0:T(8,128)(2,1)S(1)}, bf16[128,1536]{1,0:T(8,128)(2,1)S(1)}, u32[]{:S(2)}, u32[]{:S(2)}) collective-permute-start(bf16[128,1536]{1,0:T(8,128)(2,1)S(1)} %slice.55), channel_id=1, source_target_pairs={{8,0},{16,8},{24,16},{28,24},{20,28},{12,20},{4,12},{0,4},{9,1},{1... | collective-permute-start | bytes 1179656 | tf_op jit(solution)/shard_map/ppermute | solution.py:411
  85.5 17.4 %collective-permute-start.9 = (bf16[1408,128]{1,0:T(8,128)(2,1)S(1)}, bf16[1408,128]{1,0:T(8,128)(2,1)S(1)}, u32[]{:S(2)}, u32[]{:S(2)}) collective-permute-start(bf16[1408,128]{1,0:T(8,128)(2,1)S(1)} %pad_maximum_fusion.1), channel_id=1, source_target_pairs={{0,4},{1,20},{2,6},{3,22},{4,8},{5,24},{6,10},{7,26},{8,12},{9,28}... | collective-permute-start | bytes 1081352 | tf_op jit(solution)/shard_map/ppermute | solution.py:393
  88.9 14.1 %copy-start.4 = (bf16[256,1536]{1,0:T(8,128)(2,1)}, bf16[256,1536]{1,0:T(8,128)(2,1)S(1)}, u32[]{:S(2)}) copy-start(bf16[256,1536]{1,0:T(8,128)(2,1)S(1)} %constant_dynamic-update-slice_fusion.refs_7_) | copy-start | bytes 2359300
  88.9 25.6 %copy-start.16 = (f32[2,512]{1,0:T(2,128)S(1)}, f32[2,512]{1,0:T(2,128)}, u32[]{:S(2)}) copy-start(f32[2,512]{1,0:T(2,128)} %param.10) | copy-start | bytes 12292
  88.9 26.1 %copy-start.14 = (s32[2048]{0:T(1024)S(1)}, s32[2048]{0:T(1024)}, u32[]{:S(2)}) copy-start(s32[2048]{0:T(1024)} %param.12) | copy-start | bytes 24580
  88.9 26.1 %copy-start.15 = (s32[2048]{0:T(1024)S(1)}, s32[2048]{0:T(1024)}, u32[]{:S(2)}) copy-start(s32[2048]{0:T(1024)} %param.13) | copy-start | bytes 24580
  88.9 14.0 %copy-start.6 = (bf16[1408,128]{1,0:T(8,128)(2,1)}, bf16[1408,128]{1,0:T(8,128)(2,1)S(1)}, u32[]{:S(2)}) copy-start(bf16[1408,128]{1,0:T(8,128)(2,1)S(1)} %collective-permute-done.10.refs_10_) | copy-start | bytes 1081348
  102.9 0.7 copy-start.7
  114.4 7.6 %collective-permute-start.13 = (bf16[2048,384]{1,0:T(8,128)(2,1)}, bf16[2048,384]{1,0:T(8,128)(2,1)S(1)}, u32[]{:S(2)}, u32[]{:S(2)}) collective-permute-start(bf16[2048,384]{1,0:T(8,128)(2,1)} %get-tuple-element.7), channel_id=1, source_target_pairs={{0,1},{1,0},{2,3},{3,2},{4,5},{5,4},{6,7},{7,6},{8,9},{9,8},{10,11... | collective-permute-start | bytes 4718600 | tf_op jit(solution)/shard_map/ppermute | solution.py:452
  114.5 6.9 %collective-permute-start.14 = (f32[2,512]{1,0:T(2,128)S(1)}, f32[2,512]{1,0:T(2,128)S(1)}, u32[]{:S(2)}, u32[]{:S(2)}) collective-permute-start(f32[2,512]{1,0:T(2,128)S(1)} %copy-done.16), channel_id=1, source_target_pairs={{0,1},{1,0},{2,3},{3,2},{4,5},{5,4},{6,7},{7,6},{8,9},{9,8},{10,11... | collective-permute-start | bytes 12296 | tf_op jit(solution)/shard_map/ppermute | solution.py:382
  119.1 2.9 %collective-permute-start.12 = (bf16[1024,128]{1,0:T(8,128)(2,1)}, bf16[1024,128]{1,0:T(8,128)(2,1)S(1)}, u32[]{:S(2)}, u32[]{:S(2)}) collective-permute-start(bf16[1024,128]{1,0:T(8,128)(2,1)} %pad_maximum_fusion.4), channel_id=1, source_target_pairs={{0,1},{1,0},{2,3},{3,2},{4,5},{5,4},{6,7},{7,6},{8,9},{9,8},{10,11... | collective-permute-start | bytes 786440 | tf_op jit(solution)/shard_map/ppermute | solution.py:431
  122.0 0.7 copy-start.13
  122.0 1.2 copy-start.8
  162.6 32.0 %collective-permute-start.15 = (bf16[1152,128]{1,0:T(8,128)(2,1)S(1)}, bf16[1152,128]{1,0:T(8,128)(2,1)S(1)}, u32[]{:S(2)}, u32[]{:S(2)}) collective-permute-start(bf16[1152,128]{1,0:T(8,128)(2,1)S(1)} %get-tuple-element.15), channel_id=1, source_target_pairs={{0,0},{16,1},{2,2},{18,3},{4,4},{20,5},{6,6},{22,7},{8,8},{24,9},{... | collective-permute-start | bytes 884744 | tf_op jit(solution)/shard_map/ppermute | solution.py:493
  163.3 31.3 %collective-permute-start.16 = (bf16[1152,128]{1,0:T(8,128)(2,1)S(1)}, bf16[1152,128]{1,0:T(8,128)(2,1)S(1)}, u32[]{:S(2)}, u32[]{:S(2)}) collective-permute-start(bf16[1152,128]{1,0:T(8,128)(2,1)S(1)} %get-tuple-element.14), channel_id=1, source_target_pairs={{4,0},{20,1},{6,2},{22,3},{8,4},{24,5},{10,6},{26,7},{12,8},{28,9}... | collective-permute-start | bytes 884744 | tf_op jit(solution)/shard_map/ppermute | solution.py:493
  165.4 29.2 %collective-permute-start.17 = (bf16[1152,128]{1,0:T(8,128)(2,1)S(1)}, bf16[1152,128]{1,0:T(8,128)(2,1)S(1)}, u32[]{:S(2)}, u32[]{:S(2)}) collective-permute-start(bf16[1152,128]{1,0:T(8,128)(2,1)S(1)} %get-tuple-element.13), channel_id=1, source_target_pairs={{8,0},{24,1},{10,2},{26,3},{12,4},{28,5},{14,6},{30,7},{0,8},{16,9... | collective-permute-start | bytes 884744 | tf_op jit(solution)/shard_map/ppermute | solution.py:493
  167.7 27.0 %collective-permute-start.18 = (bf16[1152,128]{1,0:T(8,128)(2,1)S(1)}, bf16[1152,128]{1,0:T(8,128)(2,1)S(1)}, u32[]{:S(2)}, u32[]{:S(2)}) collective-permute-start(bf16[1152,128]{1,0:T(8,128)(2,1)S(1)} %get-tuple-element.12), channel_id=1, source_target_pairs={{12,0},{28,1},{14,2},{30,3},{0,4},{16,5},{2,6},{18,7},{4,8},{20,9}... | collective-permute-start | bytes 884744 | tf_op jit(solution)/shard_map/ppermute | solution.py:493
  168.3 4.4 %collective-permute-start.19 = (f32[1,128]{1,0:T(1,128)S(1)}, f32[1,128]{1,0:T(1,128)S(1)}, u32[]{:S(2)}, u32[]{:S(2)}) collective-permute-start(f32[1,128]{1,0:T(1,128)S(1)} %slice.51), channel_id=1, source_target_pairs={{0,1},{1,0},{2,3},{3,2},{4,5},{5,4},{6,7},{7,6},{8,9},{9,8},{10,11... | collective-permute-start | bytes 1544 | tf_op jit(solution)/shard_map/ppermute | solution.py:497
  173.4 3.5 %collective-permute-start.20 = (f32[1,128]{1,0:T(1,128)S(1)}, f32[1,128]{1,0:T(1,128)S(1)}, u32[]{:S(2)}, u32[]{:S(2)}) collective-permute-start(f32[1,128]{1,0:T(1,128)S(1)} %slice_add_fusion), channel_id=1, source_target_pairs={{0,2},{1,3},{2,0},{3,1},{4,6},{5,7},{6,4},{7,5},{8,10},{9,11},{10,... | collective-permute-start | bytes 1544 | tf_op jit(solution)/shard_map/ppermute | solution.py:497
  176.9 4.4 %collective-permute-start.21 = (f32[1,128]{1,0:T(1,128)S(1)}, f32[1,128]{1,0:T(1,128)S(1)}, u32[]{:S(2)}, u32[]{:S(2)}) collective-permute-start(f32[1,128]{1,0:T(1,128)S(1)} %add.103), channel_id=1, source_target_pairs={{0,4},{4,0},{8,12},{12,8},{16,20},{20,16},{24,28},{28,24},{1,5},{5... | collective-permute-start | bytes 1544 | tf_op jit(solution)/shard_map/ppermute | solution.py:501
  181.3 3.6 %collective-permute-start.22 = (f32[1,128]{1,0:T(1,128)S(1)}, f32[1,128]{1,0:T(1,128)S(1)}, u32[]{:S(2)}, u32[]{:S(2)}) collective-permute-start(f32[1,128]{1,0:T(1,128)S(1)} %add.104), channel_id=1, source_target_pairs={{0,8},{4,12},{8,0},{12,4},{16,24},{20,28},{24,16},{28,20},{1,9},{5... | collective-permute-start | bytes 1544 | tf_op jit(solution)/shard_map/ppermute | solution.py:501
  185.0 9.0 %collective-permute-start.23 = (f32[1,128]{1,0:T(1,128)S(1)}, f32[1,128]{1,0:T(1,128)S(1)}, u32[]{:S(2)}, u32[]{:S(2)}) collective-permute-start(f32[1,128]{1,0:T(1,128)S(1)} %add.105), channel_id=1, source_target_pairs={{0,16},{4,20},{8,24},{12,28},{16,0},{20,4},{24,8},{28,12},{1,17},{... | collective-permute-start | bytes 1544 | tf_op jit(solution)/shard_map/ppermute | solution.py:501
  194.6 0.7 copy-start.9
  194.6 0.8 copy-start.10
  194.6 0.9 copy-start.11
  194.6 1.0 copy-start.12

commit v2 on v1

--- a/solution.py
+++ b/solution.py
@@ -13,6 +13,7 @@
 HEADS = 16
 CLIPS = 3
 EPS = 1e-6
+VMEM_BYTES = 56 * 1024 * 1024
 AXES = ("seq", "head")
 
 
@@ -140,56 +141,95 @@
     return (fisher_ratio, dampened)
 
 
-def project_kernel(nb, tb, rows, quarter, place, *refs):
+def project_kernel(nb, tb, rows, quarter, with_cot, place, *refs):
     chunks = refs[:nb]
     pieces = refs[nb : nb + quarter]
-    out32, out16 = refs[nb + quarter : nb + quarter + 2]
-    xs, ws, xsem, wsem = refs[nb + quarter + 2 :]
-    wcopies = []
+    outs = refs[nb + quarter : -6]
+    xs, ws, cs, xsem, wsem, csem = refs[-6:]
+    copies = []
     for k in range(quarter):
-        start = pl.multiple_of(place[nb + k] * rows, rows)
+        start = pl.multiple_of(place[k] * rows, rows)
         for j in range(3):
-            wcopies.append(
+            copies.append(
                 pltpu.make_async_copy(
                     pieces[k].at[pl.ds(j * rows, rows)],
                     ws.at[pl.ds(start, rows), pl.ds(j * HD, HD)],
                     wsem.at[k, j],
                 )
             )
-    xcopies = [
-        pltpu.make_async_copy(chunks[b], xs.at[b], xsem.at[b]) for b in range(nb)
+        if with_cot:
+            copies.append(
+                pltpu.make_async_copy(
+                    pieces[k].at[pl.ds(3 * rows, tb)], cs.at[pl.ds(k * tb, tb)], csem.at[k]
+                )
+            )
+    xcopies = []
+    at = 0
+    for b, chunk in enumerate(chunks):
+        height = chunk.shape[0]
+        xcopies.append(pltpu.make_async_copy(chunk, xs.at[pl.ds(at, height)], xsem.at[b]))
+        at += height
+    for copy in copies + xcopies:
+        copy.start()
+    for copy in copies:
+        copy.wait()
+    if with_cot:
+        outs[2][...] = cs[...]
+    for copy in xcopies:
+        copy.wait()
+    part = jnp.dot(xs[...], ws[...], preferred_element_type=jnp.float32)
+    outs[0][...] = part
+    outs[1][...] = part.astype(jnp.bfloat16)
+
+
+def project(chunks, pieces, row_block, tb, with_cot):
+    nb, quarter = len(chunks), len(pieces)
+    half = chunks[0].shape[1]
+    total = sum(chunk.shape[0] for chunk in chunks)
+    rows = (pieces[0].shape[0] - tb) // 3
+    vmem = pl.BlockSpec(memory_space=pltpu.VMEM)
+    shapes = [
+        jax.ShapeDtypeStruct((total, 3 * HD), jnp.float32),
+        jax.ShapeDtypeStruct((total, 3 * HD), jnp.bfloat16),
     ]
-    for copy in wcopies:
-        copy.start()
-    for copy in xcopies:
-        copy.start()
-    for copy in wcopies:
-        copy.wait()
-    for b in range(nb):
-        xcopies[b].wait()
-        part = jnp.dot(xs[b], ws[...], preferred_element_type=jnp.float32)
-        here = pl.ds(pl.multiple_of(place[b] * tb, tb), tb)
-        out32[here, :] = part
-        out16[here, :] = part.astype(jnp.bfloat16)
-
-
-def head_kernel(nb, tb, rows, quarter, place, edges, *refs):
-    chunks = refs[:nb]
-    cots = refs[nb : nb + quarter]
-    cot_other, mine, other, gain, clip_row, key_code = refs[nb + quarter : nb + quarter + 6]
-    fisher_out, sum_out = refs[nb + quarter + 6 : nb + quarter + 8]
-    (xs, do, proj, qn, kn, vb, qn_t, kn_t, do_t, es, dps, dk, dv, dproj, grads, xsem, csem) = refs[
-        nb + quarter + 8 :
+    if with_cot:
+        shapes.append(jax.ShapeDtypeStruct((quarter * tb, HD), jnp.bfloat16))
+    return pl.pallas_call(
+        functools.partial(project_kernel, nb, tb, rows, quarter, with_cot),
+        out_shape=shapes,
+        in_specs=[pl.BlockSpec(memory_space=pltpu.SMEM)]
+        + [pl.BlockSpec(memory_space=pl.ANY)] * (nb + quarter),
+        out_specs=[vmem] * len(shapes),
+        scratch_shapes=[
+            pltpu.VMEM((total, half), jnp.bfloat16),
+            pltpu.VMEM((half, 3 * HD), jnp.bfloat16),
+            pltpu.VMEM((quarter * tb, HD), jnp.bfloat16),
+            pltpu.SemaphoreType.DMA((nb,)),
+            pltpu.SemaphoreType.DMA((quarter, 3)),
+            pltpu.SemaphoreType.DMA((quarter,)),
+        ],
+        compiler_params=pltpu.CompilerParams(vmem_limit_bytes=VMEM_BYTES),
+        name="project",
+    )(row_block, *chunks, *pieces)
+
+
+def head_kernel(nb, tb, rows, quarter, parts, place, edges, *refs):
+    chunks = refs[: 2 * nb]
+    cots = refs[2 * nb : 2 * nb + 2]
+    ends = 2 * nb + 2 + 2 * len(parts)
+    projections = refs[2 * nb + 2 : ends]
+    gain, clip_row, key_row = refs[ends : ends + 3]
+    fisher_out = refs[ends + 3 : ends + 3 + quarter]
+    sum_out = refs[ends + 3 + quarter]
+    (xs, do, proj, qn, kn, vb, qn_t, kn_t, do_t, key_code, es, dps, dk, dv, dproj, grads) = refs[
+        ends + 4 + quarter : -2
     ]
+    xsem, csem = refs[-2:]
     scale = 1.0 / math.sqrt(HD)
     cot_copies = []
     for k in range(quarter):
         for side in range(2):
-            src = (
-                cots[k].at[pl.ds(3 * rows, tb)]
-                if side == 0
-                else cot_other.at[pl.ds(k * tb, tb)]
-            )
+            src = cots[side].at[pl.ds(k * tb, tb)]
             block = place[nb + quarter * (1 + side) + k]
             cot_copies.append(
                 pltpu.make_async_copy(
@@ -198,27 +238,37 @@
             )
     xcopies = [
         pltpu.make_async_copy(
-            chunks[b], xs.at[pl.ds(pl.multiple_of(place[b] * tb, tb), tb)], xsem.at[b]
+            chunks[b],
+            xs.at[pl.ds(pl.multiple_of(place[b // 2] * tb + b % 2 * (tb // 2), tb // 2), tb // 2)],
+            xsem.at[b],
         )
-        for b in range(nb)
+        for b in range(2 * nb)
     ]
     for copy in cot_copies + xcopies:
         copy.start()
 
-    def normalise(b, carry):
-        here = pl.ds(pl.multiple_of(b * tb, tb), tb)
-        total = mine[here, :] + other[here, :].astype(jnp.float32)
-        proj[here, :] = total[:, : 2 * HD]
-        for j, (flat, turned) in enumerate(((qn, qn_t), (kn, kn_t))):
-            raw = total[:, j * HD : (j + 1) * HD]
-            inv = lax.rsqrt(jnp.mean(raw * raw, -1, keepdims=True) + EPS)
-            value = raw * inv * gain[j : j + 1, :]
-            flat[here, :] = value.astype(jnp.bfloat16)
-            turned[b] = value.T.astype(jnp.bfloat16)
-        vb[here, :] = total[:, 2 * HD :].astype(jnp.bfloat16)
-        return carry
-
-    lax.fori_loop(0, nb, normalise, 0)
+    first_block = 0
+    for part, count in enumerate(parts):
+
+        def normalise(b, carry, first_block=first_block, part=part):
+            source = pl.ds(pl.multiple_of(b * tb, tb), tb)
+            block = place[first_block + b]
+            here = pl.ds(pl.multiple_of(block * tb, tb), tb)
+            mine, other = projections[2 * part : 2 * part + 2]
+            total = mine[source, :] + other[source, :].astype(jnp.float32)
+            proj[here, :] = total[:, : 2 * HD]
+            for j, (flat, turned) in enumerate(((qn, qn_t), (kn, kn_t))):
+                raw = total[:, j * HD : (j + 1) * HD]
+                inv = lax.rsqrt(jnp.mean(raw * raw, -1, keepdims=True) + EPS)
+                value = raw * inv * gain[j : j + 1, :]
+                flat[here, :] = value.astype(jnp.bfloat16)
+                turned[block] = value.T.astype(jnp.bfloat16)
+            vb[here, :] = total[:, 2 * HD :].astype(jnp.bfloat16)
+            key_code[here, :] = jnp.broadcast_to(key_row[block], (HD, tb)).T
+            return carry
+
+        lax.fori_loop(0, count, normalise, 0)
+        first_block += count
     for copy in cot_copies:
         copy.wait()
 
@@ -238,58 +288,60 @@
         cubed = inv * inv * inv
         return inv * weighted - raw * (cubed * jnp.mean(raw * weighted, -1, keepdims=True))
 
-    offset = lax.broadcasted_iota(jnp.int32, (tb, tb), 0) - lax.broadcasted_iota(
-        jnp.int32, (tb, tb), 1
-    )
+    wide = 2 * tb
+    units = nb // 2
+    offset = lax.broadcasted_iota(jnp.int32, (wide, tb), 0) - lax.broadcasted_iota(
+        jnp.int32, (wide, tb), 1
+    )
+
+    def forward(i, unit, sums):
+        here = pl.ds(unit * wide, wide)
+        s = jnp.dot(kn[here, :], qn_t[i], preferred_element_type=jnp.float32)
+        codes = jnp.concatenate([key_code[here, :]] * (tb // HD), 1)
+        allowed = (codes == clip_row[i]) | (offset == i * tb - unit * wide)
+        e = jnp.where(allowed, jnp.exp2(s * (scale * math.log2(math.e))), 0.0)
+        dp = jnp.dot(vb[here, :], do_t[i], preferred_element_type=jnp.float32)
+        es[here, :] = e
+        dps[here, :] = dp
+        return (
+            sums[0] + jnp.sum(e.reshape(wide // 8, 8, tb), 0),
+            sums[1] + jnp.sum((e * dp).reshape(wide // 8, 8, tb), 0),
+        )
+
+    def finish_sums(sums):
+        inv_l = 1.0 / jnp.sum(sums[0], 0, keepdims=True)
+        return inv_l, jnp.sum(sums[1], 0, keepdims=True) * inv_l
+
+    def backward(i, unit, inv_l, row_dot, dq_t):
+        here = pl.ds(unit * wide, wide)
+        rows_q = pl.ds(pl.multiple_of(i * tb, tb), tb)
+        p = es[here, :] * inv_l
+        ds = (p * (dps[here, :] - row_dot)).astype(jnp.bfloat16)
+        dv[here, :] += jnp.dot(
+            p.astype(jnp.bfloat16), do[rows_q, :], preferred_element_type=jnp.float32
+        )
+        dk[here, :] += jnp.dot(ds, qn[rows_q, :], preferred_element_type=jnp.float32)
+        return (
+            dq_t
+            + jnp.dot(kn_t[2 * unit], ds[:tb], preferred_element_type=jnp.float32)
+            + jnp.dot(kn_t[2 * unit + 1], ds[tb:], preferred_element_type=jnp.float32)
+        )
+
+    def store_dq(i, dq_t):
+        rows_q = pl.ds(pl.multiple_of(i * tb, tb), tb)
+        dproj[rows_q, :HD] = backward_norm(dq_t.T * scale, rows_q, 0).astype(jnp.bfloat16)
+
+    zero = jnp.zeros((8, tb), jnp.float32)
 
     def queries(i, carry):
-        rows_q = pl.ds(pl.multiple_of(i * tb, tb), tb)
-        q_t = qn_t[i]
-        d_t = do_t[i]
-        clip_q = clip_row[i]
-        first, last = edges[i], edges[nb + i]
-
-        def overlap(j):
-            return (edges[j] <= last) & (edges[nb + j] >= first)
-
-        def forward(j, sums):
-            def tile():
-                here = pl.ds(pl.multiple_of(j * tb, tb), tb)
-                s = jnp.dot(kn[here, :], q_t, preferred_element_type=jnp.float32)
-                allowed = (key_code[here, :] == clip_q) | (offset == (i - j) * tb)
-                e = jnp.where(allowed, jnp.exp2(s * (scale * math.log2(math.e))), 0.0)
-                dp = jnp.dot(vb[here, :], d_t, preferred_element_type=jnp.float32)
-                es[here, :] = e
-                dps[here, :] = dp
-                return (
-                    sums[0] + jnp.sum(e.reshape(tb // 8, 8, tb), 0),
-                    sums[1] + jnp.sum((e * dp).reshape(tb // 8, 8, tb), 0),
-                )
-
-            return lax.cond(overlap(j), tile, lambda: sums)
-
-        zero = jnp.zeros((8, tb), jnp.float32)
-        sum_e, sum_edp = lax.fori_loop(0, nb, forward, (zero, zero))
-        inv_l = 1.0 / jnp.sum(sum_e, 0, keepdims=True)
-        row_dot = jnp.sum(sum_edp, 0, keepdims=True) * inv_l
-        q_b = qn[rows_q, :]
-        d_b = do[rows_q, :]
-
-        def backward(j, dq_t):
-            def tile():
-                here = pl.ds(pl.multiple_of(j * tb, tb), tb)
-                p = es[here, :] * inv_l
-                ds = (p * (dps[here, :] - row_dot)).astype(jnp.bfloat16)
-                dv[here, :] += jnp.dot(
-                    p.astype(jnp.bfloat16), d_b, preferred_element_type=jnp.float32
-                )
-                dk[here, :] += jnp.dot(ds, q_b, preferred_element_type=jnp.float32)
-                return dq_t + jnp.dot(kn_t[j], ds, preferred_element_type=jnp.float32)
-
-            return lax.cond(overlap(j), tile, lambda: dq_t)
-
-        dq_t = lax.fori_loop(0, nb, backward, jnp.zeros((HD, tb), jnp.float32))
-        dproj[rows_q, :HD] = backward_norm(dq_t.T * scale, rows_q, 0).astype(jnp.bfloat16)
+        sums = (zero, zero)
+        for unit in range(units):
+            sums = forward(i, unit, sums)
+        inv_l, row_dot = finish_sums(sums)
+        dq_t = jnp.zeros((HD, tb), jnp.float32)
+        for unit in range(units):
+            dq_t = backward(i, unit, inv_l, row_dot, dq_t)
+        store_dq(i, dq_t)
         return carry
 
     lax.fori_loop(0, nb, queries, 0)
@@ -306,29 +358,30 @@
         copy.wait()
 
     def gradient(b, carry):
-        here = pl.ds(pl.multiple_of(b * tb, tb), tb)
+        here = pl.ds(pl.multiple_of(b * wide, wide), wide)
         turned = dproj[here, :].astype(jnp.float32).T
+        clips = jnp.concatenate([clip_row[2 * b], clip_row[2 * b + 1]], 1)
 
         def one_clip(clip, carry):
-            part = jnp.where(clip_row[b] == clip, turned, 0.0).astype(jnp.bfloat16)
+            part = jnp.where(clips == clip, turned, 0.0).astype(jnp.bfloat16)
             grads[clip] += jnp.dot(part, xs[here, :], preferred_element_type=jnp.float32)
             return carry
 
-        lax.fori_loop(edges[b], edges[nb + b] + 1, one_clip, 0)
+        lax.fori_loop(edges[2 * b], edges[nb + 2 * b + 1] + 1, one_clip, 0)
         return carry
 
-    lax.fori_loop(0, nb, gradient, 0)
+    lax.fori_loop(0, units, gradient, 0)
     running = jnp.zeros((HD, rows), jnp.float32)
-    for block in range(quarter):
-        slot = place[nb + 3 * quarter + block]
+    for k in range(quarter):
+        block = place[nb + k]
+        columns = pl.ds(pl.multiple_of(block * rows, rows), rows)
         for j in range(3):
-            span = (pl.ds(j * HD, HD), pl.ds(block * rows, rows))
             squares = jnp.zeros((HD, rows), jnp.float32)
             for clip in range(CLIPS):
-                g = grads[clip, span[0], span[1]]
+                g = grads[clip, j * HD : (j + 1) * HD, columns]
                 squares += g * g
             running += squares
-            fisher_out[slot, j * rows : (j + 1) * rows, :] = squares.T.astype(jnp.bfloat16)
+            fisher_out[k][j * rows : (j + 1) * rows, :] = squares.T.astype(jnp.bfloat16)
     sum_out[...] = jnp.full((8, HD), jnp.sum(running), jnp.float32)
 
 
@@ -380,93 +433,81 @@
     back_perms = [[(b, a) for a, b in perm] for perm in out_perms]
 
     gains_other = lax.ppermute(gains, AXES, swap)
-    pieces = []
+    outgoing = []
     for k in range(quarter):
         col = ((k + s) % quarter) * HD
-        piece = jnp.concatenate(
-            [
-                lax.dynamic_slice_in_dim(w_qkv, col, HD, 2).reshape(3 * rows, HD),
-                lax.dynamic_slice_in_dim(cotangent, col, HD, 1),
-            ],
-            0,
+        outgoing.append(
+            jnp.concatenate(
+                [
+                    lax.dynamic_slice_in_dim(w_qkv, col, HD, 2).reshape(3 * rows, HD),
+                    lax.dynamic_slice_in_dim(cotangent, col, HD, 1),
+                ],
+                0,
+            )
         )
-        pieces.append(lax.ppermute(piece, AXES, out_perms[k]))
+    pieces = []
+    for k in range(0, quarter, 2):
+        pair = outgoing[k : k + 2]
+        if k:
+            barred = lax.optimization_barrier((*pair, *pieces))
+            pair, pieces = list(barred[: len(pair)]), list(barred[len(pair) :])
+        pieces += [lax.ppermute(piece, AXES, out_perms[k + i]) for i, piece in enumerate(pair)]
 
     ring = list(range(0, ns, 2)) + list(range(1, ns, 2))[::-1]
     forth = [(ring[i], ring[(i + 1) % ns]) for i in range(ns)]
     back = [(b, a) for a, b in forth]
     position = [ring.index(i) for i in range(ns)]
     mine = lax.dynamic_slice_in_dim(tokens, core * half, half, 1)
-    chunks, steps = [mine], [0]
-    ahead = behind = mine
+    halves = [mine[: tb // 2], mine[tb // 2 :]]
+    chunks, steps = list(halves), [0]
+    ahead, behind = list(halves), list(halves)
     for step in range(1, ns // 2):
-        ahead = lax.ppermute(ahead, "seq", forth)
-        behind = lax.ppermute(behind, "seq", back)
-        chunks += [ahead, behind]
+        ahead = [lax.ppermute(part, "seq", forth) for part in ahead]
+        behind = [lax.ppermute(part, "seq", back) for part in behind]
+        chunks += ahead + behind
         steps += [-step, step]
-    chunks.append(
-        jnp.concatenate(
-            [
-                lax.ppermute(ahead[: tb // 2], "seq", forth),
-                lax.ppermute(behind[tb // 2 :], "seq", back),
-            ],
-            0,
-        )
-    )
+    chunks += [lax.ppermute(ahead[0], "seq", forth), lax.ppermute(behind[1], "seq", back)]
     steps.append(ns // 2)
     order = jnp.array([[ring[(position[i] + d) % ns] for d in steps] for i in range(ns)], jnp.int32)
     ks = jnp.arange(quarter, dtype=jnp.int32)
-    row_block = (s - ks) % quarter
+    row_block = ((s - ks) % quarter).astype(jnp.int32)
     place = jnp.concatenate(
         [
             lax.dynamic_index_in_dim(order, s, 0, False),
             row_block,
             row_block + core * quarter,
             row_block + (1 - core) * quarter,
-            (s - ks) % quarter,
         ]
     ).astype(jnp.int32)
 
-    cot_mine = jnp.concatenate([p[3 * rows :] for p in pieces], 0)
-    cot_other = lax.ppermute(cot_mine, AXES, swap)
-
-    params = pltpu.CompilerParams(vmem_limit_bytes=56 * 1024 * 1024)
+    params = pltpu.CompilerParams(vmem_limit_bytes=VMEM_BYTES)
     bf16, f32 = jnp.bfloat16, jnp.float32
-    part32, part16 = pl.pallas_call(
-        functools.partial(project_kernel, ns, tb, rows, quarter),
-        out_shape=(
-            jax.ShapeDtypeStruct((all_tokens, 3 * HD), f32),
-            jax.ShapeDtypeStruct((all_tokens, 3 * HD), bf16),
-        ),
-        in_specs=[smem] + [hbm] * (ns + quarter),
-        out_specs=(vmem, vmem),
-        scratch_shapes=[
-            pltpu.VMEM((ns, tb, half), bf16),
-            pltpu.VMEM((half, 3 * HD), bf16),
-            pltpu.SemaphoreType.DMA((ns,)),
-            pltpu.SemaphoreType.DMA((quarter, 3)),
-        ],
-        compiler_params=params,
-        name="project",
-    )(place, *chunks, *pieces)
-    other = lax.ppermute(part16, AXES, swap)
-
     own_gain = (s // quarter) == core
     gain = lax.dynamic_slice_in_dim(
         jnp.where(own_gain, gains, gains_other), (s % quarter) * HD, HD, 1
     )
     clip_row = token_clip.reshape(ns, 1, tb)
-    key_code = jnp.where(key_live == 1, token_clip, -1)[:, None]
+    key_row = jnp.where(key_live == 1, token_clip, -1).reshape(ns, 1, tb)
     blocks = token_clip.reshape(ns, tb)
     edges = jnp.concatenate([blocks[:, 0], blocks[:, -1]])
-    fisher, part_sum = pl.pallas_call(
-        functools.partial(head_kernel, ns, tb, rows, quarter),
+    place, row_block, edges, gain, clip_row, key_row, *pieces = lax.optimization_barrier(
+        (place, row_block, edges, gain, clip_row, key_row, *pieces)
+    )
+    early = ns - 3
+    first32, first16, cot_mine = project(chunks[: 2 * early], pieces, row_block, tb, True)
+    first_other = lax.ppermute(first16, AXES, swap)
+    cot_other = lax.ppermute(cot_mine, AXES, swap)
+    last32, last16 = project(chunks[2 * early :], pieces, row_block, tb, False)
+    last_other = lax.ppermute(last16, AXES, swap)
+
+    *fisher, part_sum = pl.pallas_call(
+        functools.partial(head_kernel, ns, tb, rows, quarter, (early, ns - early)),
         out_shape=(
-            jax.ShapeDtypeStruct((quarter, 3 * rows, HD), bf16),
+            *[jax.ShapeDtypeStruct((3 * rows, HD), bf16)] * quarter,
             jax.ShapeDtypeStruct((8, HD), f32),
         ),
-        in_specs=[smem, smem] + [hbm] * (ns + quarter + 1) + [vmem] * 5,
-        out_specs=(vmem, vmem),
+        in_specs=[smem, smem] + [hbm] * (2 * ns + 2) + [vmem] * 7,
+        out_specs=[vmem] * (quarter + 1),
         scratch_shapes=[
             pltpu.VMEM((all_tokens, half), bf16),
             pltpu.VMEM((all_tokens, HD), bf16),
@@ -477,18 +518,32 @@
             pltpu.VMEM((ns, HD, tb), bf16),
             pltpu.VMEM((ns, HD, tb), bf16),
             pltpu.VMEM((ns, HD, tb), bf16),
+            pltpu.VMEM((all_tokens, HD), jnp.int32),
             pltpu.VMEM((all_tokens, tb), f32),
             pltpu.VMEM((all_tokens, tb), f32),
             pltpu.VMEM((all_tokens, HD), f32),
             pltpu.VMEM((all_tokens, HD), f32),
             pltpu.VMEM((all_tokens, 3 * HD), bf16),
             pltpu.VMEM((CLIPS, 3 * HD, half), f32),
-            pltpu.SemaphoreType.DMA((ns,)),
+            pltpu.SemaphoreType.DMA((2 * ns,)),
             pltpu.SemaphoreType.DMA((2, quarter)),
         ],
         compiler_params=params,
         name="head",
-    )(place, edges, *chunks, *pieces, cot_other, part32, other, gain, clip_row, key_code)
+    )(
+        place,
+        edges,
+        *chunks,
+        cot_mine,
+        cot_other,
+        first32,
+        first_other,
+        last32,
+        last_other,
+        gain,
+        clip_row,
+        key_row,
+    )
 
     returned = [lax.ppermute(fisher[k], AXES, back_perms[k]) for k in range(quarter)]
     total = part_sum[:1]

time: 201 us -> 179 us (0.89)
  waiting for transfers between devices: 84 us -> 51 us
  starting transfers between devices: 38.1 us -> 62.3 us
  local copies, waits for them, and re-layouts: 17 us -> 8.1 us
  Pallas kernels: 53.5 us -> 48.4 us
    ppermute x13 -> x20, waiting for transfers between devices: 70.2 us -> 33.3 us  [the longest x4 13.5 us: chip_per_head(): lax.ppermute(piece, AXES, out_perms[k + i])]
    ppermute x13 -> x20, starting transfers between devices: 21.3 us -> 45.8 us  [the longest x6 15 us: chip_per_head(): ahead = [lax.ppermute(part, 'seq', forth) for part in ahead]]
    pallas_call x2 -> x3, Pallas kernels: 48.8 us -> 43.7 us  [the longest x1 30.9 us: chip_per_head(): pl.pallas_call(functools.partial(head_kernel, ns, tb, rows, quarter, (ear...]
    ppermute x3, starting transfers between devices: 6.12 us -> 2.47 us  [chip_per_head(): lax.ppermute(total, 'seq', [(i, i ^ bit) for i in range(ns)])]
    ppermute x4, starting transfers between devices: 5.06 us -> 8.28 us  [chip_per_head(): lax.ppermute(fisher[k], AXES, back_perms[k])]
    slice x6 -> x1, local copies, waits for them, and re-layouts: 4.21 us -> 1.17 us  [chip_per_head(): halves = [mine[:tb // 2], mine[tb // 2:]]]
    unnamed x35 -> x60, local copies, waits for them, and re-layouts: 5.39 us -> 4.58 us
  transfers between devices with their start and end apart: 24 -> 31, of which waited for: 12 -> 11; matrix products, arithmetic and copies ran while one was open for 9% -> 6% of each run, Pallas kernels for 0% -> 7%
where the time goes in v2:
time: 179 us; the launch traced here: 178 us
  starting transfers between devices  62.3 us (35%)
  waiting for transfers between devices  51 us (28%)
  Pallas kernels  48.4 us (27%)
  local copies, waits for them, and re-layouts  8.1 us (5%)
  other arithmetic  7.26 us (4%)
    pallas_call x1, Pallas kernels, chip_per_head(): pl.pallas_call(functools.partial(head_kernel, ns, tb, rows, quarter, (ear...  30.9 us
    ppermute x6, starting transfers between devices, chip_per_head(): ahead = [lax.ppermute(part, 'seq', forth) for part in ahead]  15 us
    ppermute x4, waiting for transfers between devices, chip_per_head(): lax.ppermute(piece, AXES, out_perms[k + i])  13.5 us
    ppermute x4, starting transfers between devices, chip_per_head(): lax.ppermute(piece, AXES, out_perms[k + i])  13.1 us
    ppermute x3, waiting for transfers between devices, chip_per_head(): lax.ppermute(total, 'seq', [(i, i ^ bit) for i in range(ns)])  12.9 us
    pallas_call x2, Pallas kernels, project(): pl.pallas_call(functools.partial(project_kernel, nb, tb, rows, quarter, w...  12.8 us
    ppermute x6, waiting for transfers between devices, chip_per_head(): behind = [lax.ppermute(part, 'seq', back) for part in behind]  12.2 us
    ppermute x6, starting transfers between devices, chip_per_head(): behind = [lax.ppermute(part, 'seq', back) for part in behind]  9.81 us
  transfers between devices with their start and end apart: 31, of which 11 were waited for; matrix products, arithmetic and copies ran while one was open for 6% of the time, Pallas kernels for 7%

profile of v2, /device:TPU:0, one launch (start us, length us, event | category | flops | bytes accessed | tf_op | source)
XLA Modules:
  0.0 178.0 jit_solution(15537126541421602931)
XLA Ops:
  0.6 0.0 copy-start
  0.7 0.5 collective-permute-start
  1.2 1.2 fusion.3
  2.4 2.7 %collective-permute-start.8 = (bf16[128,1536]{1,0:T(8,128)(2,1)S(1)}, bf16[128,1536]{1,0:T(8,128)(2,1)S(1)}, u32[]{:S(2)}, u32[]{:S(2)}) collective-permute-start(bf16[128,1536]{1,0:T(8,128)(2,1)S(1)} %get-tuple-element.52.refs_1_), channel_id=1, source_target_pairs={{8,0},{16,8},{24,16},{28,24},{20,28},{12,20},{4,12},{0,4},{9,1},{1... | collective-permute-start | bytes 1179656 | tf_op jit(solution)/shard_map/ppermute | solution.py:466
  5.1 0.1 collective-permute-start.5
  5.3 0.2 constant_dynamic-slice_fusion.3
  5.5 0.0 copy-start.27
  5.5 0.7 collective-permute-start.1
  6.2 0.8 pad_maximum_fusion.3
  7.0 1.9 %collective-permute-start.2 = (bf16[1408,128]{1,0:T(8,128)(2,1)}, bf16[1408,128]{1,0:T(8,128)(2,1)S(1)}, u32[]{:S(2)}, u32[]{:S(2)}) collective-permute-start(bf16[1408,128]{1,0:T(8,128)(2,1)} %pad_maximum_fusion.3), channel_id=1, source_target_pairs={{0,4},{1,20},{2,6},{3,22},{4,8},{5,24},{6,10},{7,26},{8,12},{9,28}... | collective-permute-start | bytes 1081352 | tf_op jit(solution)/shard_map/ppermute | solution.py:454
  8.9 0.9 pad_maximum_fusion
  9.8 1.6 collective-permute-start.6
  11.5 13.5 %collective-permute-done.2.refs_11_.refs_7_ = bf16[1408,128]{1,0:T(8,128)(2,1)S(1)} collective-permute-done((bf16[1408,128]{1,0:T(8,128)(2,1)}, bf16[1408,128]{1,0:T(8,128)(2,1)S(1)}, u32[]{:S(2)}, u32[]{:S(2)}) %collective-permute-start.2) | collective-permute-done | bytes 360480 | tf_op jit(solution)/shard_map/ppermute | solution.py:454
  25.0 2.8 %collective-permute-start.3 = (bf16[1408,128]{1,0:T(8,128)(2,1)}, bf16[1408,128]{1,0:T(8,128)(2,1)}, u32[]{:S(2)}, u32[]{:S(2)}) collective-permute-start(bf16[1408,128]{1,0:T(8,128)(2,1)} %get-tuple-element.28), channel_id=1, source_target_pairs={{0,8},{1,24},{2,10},{3,26},{4,12},{5,28},{6,14},{7,30},{8,0},{9,16... | collective-permute-start | bytes 1081352 | tf_op jit(solution)/shard_map/ppermute | solution.py:454
  27.8 5.8 %collective-permute-start.12 = (bf16[128,1536]{1,0:T(8,128)(2,1)S(1)}, bf16[128,1536]{1,0:T(8,128)(2,1)S(1)}, u32[]{:S(2)}, u32[]{:S(2)}) collective-permute-start(bf16[128,1536]{1,0:T(8,128)(2,1)S(1)} %collective-permute-done.8.refs_5_), channel_id=1, source_target_pairs={{8,0},{16,8},{24,16},{28,24},{20,28},{12,20},{4,12},{0,4},{9,1},{1... | collective-permute-start | bytes 1179656 | tf_op jit(solution)/shard_map/ppermute | solution.py:466
  33.7 1.2 fusion.2
  34.9 0.2 slice_reduce_fusion.1
  35.1 0.6 pad_add_fusion.1.edges
  35.7 7.7 %collective-permute-start.4 = (bf16[1408,128]{1,0:T(8,128)(2,1)}, bf16[1408,128]{1,0:T(8,128)(2,1)}, u32[]{:S(2)}, u32[]{:S(2)}) collective-permute-start(bf16[1408,128]{1,0:T(8,128)(2,1)} %get-tuple-element.29), channel_id=1, source_target_pairs={{0,12},{1,28},{2,14},{3,30},{4,0},{5,16},{6,2},{7,18},{8,4},{9,20}... | collective-permute-start | bytes 1081352 | tf_op jit(solution)/shard_map/ppermute | solution.py:454
  43.4 0.8 collective-permute-start.10
  44.2 1.3 collective-permute-start.11
  45.5 7.8 %collective-permute-done.12.refs_9_ = bf16[128,1536]{1,0:T(8,128)(2,1)S(1)} collective-permute-done((bf16[128,1536]{1,0:T(8,128)(2,1)S(1)}, bf16[128,1536]{1,0:T(8,128)(2,1)S(1)}, u32[]{:S(2)}, u32[]{:S(2)}) %collective-permute-start.12) | collective-permute-done | bytes 393248 | tf_op jit(solution)/shard_map/ppermute | solution.py:466
  53.3 10.5 %collective-permute-start.13 = (bf16[128,1536]{1,0:T(8,128)(2,1)}, bf16[128,1536]{1,0:T(8,128)(2,1)S(1)}, u32[]{:S(2)}, u32[]{:S(2)}) collective-permute-start(bf16[128,1536]{1,0:T(8,128)(2,1)} %collective-permute-done.9.refs_6_), channel_id=1, source_target_pairs={{0,8},{8,16},{16,24},{24,28},{28,20},{20,12},{12,4},{4,0},{1,9},{9... | collective-permute-start | bytes 1179656 | tf_op jit(solution)/shard_map/ppermute | solution.py:465
  63.8 1.2 pad_add_fusion.place
  65.0 1.3 compare_select_fusion
  66.3 1.2 fusion.refs_22_
  67.5 2.0 %collective-permute-start.14 = (bf16[128,1536]{1,0:T(8,128)(2,1)S(1)}, bf16[128,1536]{1,0:T(8,128)(2,1)S(1)}, u32[]{:S(2)}, u32[]{:S(2)}) collective-permute-start(bf16[128,1536]{1,0:T(8,128)(2,1)S(1)} %collective-permute-done.10.refs_7_), channel_id=1, source_target_pairs={{0,8},{8,16},{16,24},{24,28},{28,20},{20,12},{12,4},{4,0},{1,9},{9... | collective-permute-start | bytes 1179656 | tf_op jit(solution)/shard_map/ppermute | solution.py:465
  69.5 3.8 %collective-permute-done.11.refs_8_ = bf16[128,1536]{1,0:T(8,128)(2,1)S(1)} collective-permute-done((bf16[128,1536]{1,0:T(8,128)(2,1)S(1)}, bf16[128,1536]{1,0:T(8,128)(2,1)S(1)}, u32[]{:S(2)}, u32[]{:S(2)}) %collective-permute-start.11) | collective-permute-done | bytes 393248 | tf_op jit(solution)/shard_map/ppermute | solution.py:466
  73.4 0.7 copy-done.15
  74.1 7.3 %project.2 = (f32[1280,384]{1,0:T(8,128)}, bf16[1280,384]{1,0:T(8,128)(2,1)}, bf16[1024,128]{1,0:T(8,128)(2,1)}) custom-call(s32[4]{0:T(128)} %copy-done.28, bf16[128,1536]{1,0:T(8,128)(2,1)} %copy-done.2, bf16[128,1536]{1,0:T(8,128)(2,1)} %copy-done.1, bf16[128,1536]{1,0:T(8,128)(2,1)} %copy-done.10, bf16[128,1536]{1,0:T(8,128)(2,1)} %copy-done.11, ...), custom_call_target="tpu_custom_call" | custom-call | tf_op jit(solution)/shard_map/project/pallas_call | solution.py:197
  81.4 7.3 %collective-permute-start.18 = (bf16[128,1536]{1,0:T(8,128)(2,1)S(1)}, bf16[128,1536]{1,0:T(8,128)(2,1)S(1)}, u32[]{:S(2)}, u32[]{:S(2)}) collective-permute-start(bf16[128,1536]{1,0:T(8,128)(2,1)S(1)} %collective-permute-done.16.refs_3_.refs_13_), channel_id=1, source_target_pairs={{8,0},{16,8},{24,16},{28,24},{20,28},{12,20},{4,12},{0,4},{9,1},{1... | collective-permute-start | bytes 1179656 | tf_op jit(solution)/shard_map/ppermute | solution.py:469
  88.7 0.6 collective-permute-start.17
  89.3 0.6 collective-permute-done.15.refs_2_.refs_12_
  89.9 7.6 %collective-permute-done.18.refs_5_.refs_15_ = bf16[128,1536]{1,0:T(8,128)(2,1)S(1)} collective-permute-done((bf16[128,1536]{1,0:T(8,128)(2,1)S(1)}, bf16[128,1536]{1,0:T(8,128)(2,1)S(1)}, u32[]{:S(2)}, u32[]{:S(2)}) %collective-permute-start.18) | collective-permute-done | bytes 393248 | tf_op jit(solution)/shard_map/ppermute | solution.py:469
  97.5 0.7 copy-done.7
  98.2 0.8 copy-done.8
  99.0 5.5 %project.3 = (f32[768,384]{1,0:T(8,128)}, bf16[768,384]{1,0:T(8,128)(2,1)}) custom-call(s32[4]{0:T(128)} %copy-done.28, bf16[128,1536]{1,0:T(8,128)(2,1)} %copy-done.4, bf16[128,1536]{1,0:T(8,128)(2,1)} %copy-done.5, bf16[128,1536]{1,0:T(8,128)(2,1)} %copy-done.6, bf16[128,1536]{1,0:T(8,128)(2,1)} %copy-done.3, bf16[128,1536]{1,0:T(8,128)(2,1)} %copy-done.8, ...), custom_call_target="tpu_custom_call" | custom-call | tf_op jit(solution)/shard_map/project/pallas_call | solution.py:197
  104.5 0.1 collective-permute-start.21
  104.6 0.5 collective-permute-start.19
  105.1 1.9 %collective-permute-done.19.refs_17_ = bf16[1024,128]{1,0:T(8,128)(2,1)S(1)} collective-permute-done((bf16[1024,128]{1,0:T(8,128)(2,1)S(1)}, bf16[1024,128]{1,0:T(8,128)(2,1)S(1)}, u32[]{:S(2)}, u32[]{:S(2)}) %collective-permute-start.19) | collective-permute-done | bytes 262176 | tf_op jit(solution)/shard_map/ppermute | solution.py:499
  107.0 0.7 copy-done.25
  107.7 0.4 copy-done.18
  108.1 0.2 copy-done.19
  108.3 30.9 %head.1 = (bf16[1152,128]{1,0:T(8,128)(2,1)}, bf16[1152,128]{1,0:T(8,128)(2,1)}, bf16[1152,128]{1,0:T(8,128)(2,1)}, bf16[1152,128]{1,0:T(8,128)(2,1)}, f32[8,128]{1,0:T(8,128)}) custom-call(s32[20]{0:T(128)} %pad_add_fusion.place, s32[16]{0:T(128)} %pad_add_fusion.1.edges, bf16[128,1536]{1,0:T(8,128)(2,1)} %copy-done.2, bf16[128,1536]{1,0:T(8,128)(2,1)} %copy-done.1, ...), custom_call_target="tpu_custom_call" | custom-call | tf_op jit(solution)/shard_map/head/pallas_call | solution.py:503
  139.1 1.6 collective-permute-start.22
  140.8 2.1 %collective-permute-start.23 = (bf16[1152,128]{1,0:T(8,128)(2,1)}, bf16[1152,128]{1,0:T(8,128)(2,1)S(1)}, u32[]{:S(2)}, u32[]{:S(2)}) collective-permute-start(bf16[1152,128]{1,0:T(8,128)(2,1)} %get-tuple-element.46), channel_id=1, source_target_pairs={{4,0},{20,1},{6,2},{22,3},{8,4},{24,5},{10,6},{26,7},{12,8},{28,9}... | collective-permute-start | bytes 884744 | tf_op jit(solution)/shard_map/ppermute | solution.py:548
  142.8 2.6 %collective-permute-start.24 = (bf16[1152,128]{1,0:T(8,128)(2,1)}, bf16[1152,128]{1,0:T(8,128)(2,1)S(1)}, u32[]{:S(2)}, u32[]{:S(2)}) collective-permute-start(bf16[1152,128]{1,0:T(8,128)(2,1)} %get-tuple-element.47), channel_id=1, source_target_pairs={{8,0},{24,1},{10,2},{26,3},{12,4},{28,5},{14,6},{30,7},{0,8},{16,9... | collective-permute-start | bytes 884744 | tf_op jit(solution)/shard_map/ppermute | solution.py:548
  145.4 2.0 %collective-permute-start.25 = (bf16[1152,128]{1,0:T(8,128)(2,1)}, bf16[1152,128]{1,0:T(8,128)(2,1)S(1)}, u32[]{:S(2)}, u32[]{:S(2)}) collective-permute-start(bf16[1152,128]{1,0:T(8,128)(2,1)} %get-tuple-element.48), channel_id=1, source_target_pairs={{12,0},{28,1},{14,2},{30,3},{0,4},{16,5},{2,6},{18,7},{4,8},{20,9}... | collective-permute-start | bytes 884744 | tf_op jit(solution)/shard_map/ppermute | solution.py:548
  147.4 0.7 slice.19
  148.1 3.2 %collective-permute-start.26 = (f32[1,128]{1,0:T(1,128)S(1)}, f32[1,128]{1,0:T(1,128)S(1)}, u32[]{:S(2)}, u32[]{:S(2)}) collective-permute-start(f32[1,128]{1,0:T(1,128)S(1)} %slice.19), channel_id=1, source_target_pairs={{0,1},{1,0},{2,3},{3,2},{4,5},{5,4},{6,7},{7,6},{8,9},{9,8},{10,11... | collective-permute-start | bytes 1544 | tf_op jit(solution)/shard_map/ppermute | solution.py:552
  151.3 0.8 collective-permute-done.26
  152.1 0.7 slice_add_fusion
  152.8 1.5 collective-permute-start.27
  154.3 2.0 %collective-permute-done.27 = f32[1,128]{1,0:T(1,128)S(1)} collective-permute-done((f32[1,128]{1,0:T(1,128)S(1)}, f32[1,128]{1,0:T(1,128)S(1)}, u32[]{:S(2)}, u32[]{:S(2)}) %collective-permute-start.27) | collective-permute-done | bytes 544 | tf_op jit(solution)/shard_map/ppermute | solution.py:552
  156.3 3.5 %collective-permute-done.28 = f32[1,128]{1,0:T(1,128)S(1)} collective-permute-done((f32[1,128]{1,0:T(1,128)S(1)}, f32[1,128]{1,0:T(1,128)S(1)}, u32[]{:S(2)}, u32[]{:S(2)}) %collective-permute-start.28) | collective-permute-done | bytes 544 | tf_op jit(solution)/shard_map/ppermute | solution.py:556
  159.9 3.5 %collective-permute-done.29 = f32[1,128]{1,0:T(1,128)S(1)} collective-permute-done((f32[1,128]{1,0:T(1,128)S(1)}, f32[1,128]{1,0:T(1,128)S(1)}, u32[]{:S(2)}, u32[]{:S(2)}) %collective-permute-start.29) | collective-permute-done | bytes 544 | tf_op jit(solution)/shard_map/ppermute | solution.py:556
  163.4 2.5 %collective-permute-start.30 = (f32[1,128]{1,0:T(1,128)S(1)}, f32[1,128]{1,0:T(1,128)S(1)}, u32[]{:S(2)}, u32[]{:S(2)}) collective-permute-start(f32[1,128]{1,0:T(1,128)S(1)} %add.103), channel_id=1, source_target_pairs={{0,16},{4,20},{8,24},{12,28},{16,0},{20,4},{24,8},{28,12},{1,17},{... | collective-permute-start | bytes 1544 | tf_op jit(solution)/shard_map/ppermute | solution.py:556
  165.9 5.8 %collective-permute-done.30 = f32[1,128]{1,0:T(1,128)S(1)} collective-permute-done((f32[1,128]{1,0:T(1,128)S(1)}, f32[1,128]{1,0:T(1,128)S(1)}, u32[]{:S(2)}, u32[]{:S(2)}) %collective-permute-start.30) | collective-permute-done | bytes 544 | tf_op jit(solution)/shard_map/ppermute | solution.py:556
  171.7 0.5 add.104.refs_4_
  172.3 0.7 copy-done.20
  173.0 0.1 copy-done.21
  173.1 0.1 copy-done.22
  173.2 0.1 copy-done.23
  173.3 4.7 %finish.1 = (f32[3,384,512]{2,1,0:T(8,128)}, bf16[3,384,512]{2,1,0:T(8,128)(2,1)}) custom-call(s32[1]{0:T(128)} %bitcast.shift, bf16[1152,128]{1,0:T(8,128)(2,1)} %copy-done.20, bf16[1152,128]{1,0:T(8,128)(2,1)} %copy-done.21, bf16[1152,128]{1,0:T(8,128)(2,1)} %copy-done.22, bf16[1152,128]{1,0:T(8,128)(2,1)} %copy-done.23, f32[1,128]{1,0:T(1,128)} %add.104.refs_4_, ...), custom_call_target="tpu_custom_call" | custom-call | tf_op jit(solution)/shard_map/finish/pallas_call | solution.py:561
  (83 shorter events, 0.3 us)
Async XLA Ops:
  0.6 4.6 %copy-start.26 = (bf16[256,512]{1,0:T(8,128)(2,1)S(1)}, bf16[256,512]{1,0:T(8,128)(2,1)}, u32[]{:S(2)}) copy-start(bf16[256,512]{1,0:T(8,128)(2,1)} %param.11) | copy-start | bytes 786436
  0.6 4.6 %copy-start = (bf16[3,384,512]{2,1,0:T(8,128)(2,1)S(1)}, bf16[3,384,512]{2,1,0:T(8,128)(2,1)}, u32[]{:S(2)}) copy-start(bf16[3,384,512]{2,1,0:T(8,128)(2,1)} %refs_5_.1) | copy-start | bytes 3538948
  0.7 24.3 %collective-permute-start = (f32[2,512]{1,0:T(2,128)}, f32[2,512]{1,0:T(2,128)S(1)}, u32[]{:S(2)}, u32[]{:S(2)}) collective-permute-start(f32[2,512]{1,0:T(2,128)} %param.10), channel_id=1, source_target_pairs={{0,1},{1,0},{2,3},{3,2},{4,5},{5,4},{6,7},{7,6},{8,9},{9,8},{10,11... | collective-permute-start | bytes 12296 | tf_op jit(solution)/shard_map/ppermute | solution.py:435
  2.3 7.5 %copy-start.1 = (bf16[128,1536]{1,0:T(8,128)(2,1)}, bf16[128,1536]{1,0:T(8,128)(2,1)S(1)}, u32[]{:S(2)}) copy-start(bf16[128,1536]{1,0:T(8,128)(2,1)S(1)} %get-tuple-element.52.refs_1_) | copy-start | bytes 1179652
  2.3 22.6 %copy-start.2 = (bf16[128,1536]{1,0:T(8,128)(2,1)}, bf16[128,1536]{1,0:T(8,128)(2,1)S(1)}, u32[]{:S(2)}) copy-start(bf16[128,1536]{1,0:T(8,128)(2,1)S(1)} %get-tuple-element.53.refs_0_) | copy-start | bytes 1179652
  2.4 25.4 %collective-permute-start.8 = (bf16[128,1536]{1,0:T(8,128)(2,1)S(1)}, bf16[128,1536]{1,0:T(8,128)(2,1)S(1)}, u32[]{:S(2)}, u32[]{:S(2)}) collective-permute-start(bf16[128,1536]{1,0:T(8,128)(2,1)S(1)} %get-tuple-element.52.refs_1_), channel_id=1, source_target_pairs={{8,0},{16,8},{24,16},{28,24},{20,28},{12,20},{4,12},{0,4},{9,1},{1... | collective-permute-start | bytes 1179656 | tf_op jit(solution)/shard_map/ppermute | solution.py:466
  5.1 28.6 %collective-permute-start.5 = (bf16[128,1536]{1,0:T(8,128)(2,1)S(1)}, bf16[128,1536]{1,0:T(8,128)(2,1)S(1)}, u32[]{:S(2)}, u32[]{:S(2)}) collective-permute-start(bf16[128,1536]{1,0:T(8,128)(2,1)S(1)} %get-tuple-element.53.refs_0_), channel_id=1, source_target_pairs={{0,8},{8,16},{16,24},{24,28},{28,20},{20,12},{12,4},{4,0},{1,9},{9... | collective-permute-start | bytes 1179656 | tf_op jit(solution)/shard_map/ppermute | solution.py:465
  5.5 29.4 %copy-start.27 = (s32[2048]{0:T(1024)S(1)}, s32[2048]{0:T(1024)}, u32[]{:S(2)}) copy-start(s32[2048]{0:T(1024)} %param.12) | copy-start | bytes 24580
  5.5 4.3 %collective-permute-start.1 = (bf16[1408,128]{1,0:T(8,128)(2,1)S(1)}, bf16[1408,128]{1,0:T(8,128)(2,1)S(1)}, u32[]{:S(2)}, u32[]{:S(2)}) collective-permute-start(bf16[1408,128]{1,0:T(8,128)(2,1)S(1)} %pad_maximum_fusion.2), channel_id=1, source_target_pairs={{0,0},{1,16},{2,2},{3,18},{4,4},{5,20},{6,6},{7,22},{8,8},{9,24},{... | collective-permute-start | bytes 1081352 | tf_op jit(solution)/shard_map/ppermute | solution.py:454
  7.0 18.0 %collective-permute-start.2 = (bf16[1408,128]{1,0:T(8,128)(2,1)}, bf16[1408,128]{1,0:T(8,128)(2,1)S(1)}, u32[]{:S(2)}, u32[]{:S(2)}) collective-permute-start(bf16[1408,128]{1,0:T(8,128)(2,1)} %pad_maximum_fusion.3), channel_id=1, source_target_pairs={{0,4},{1,20},{2,6},{3,22},{4,8},{5,24},{6,10},{7,26},{8,12},{9,28}... | collective-permute-start | bytes 1081352 | tf_op jit(solution)/shard_map/ppermute | solution.py:454
  9.8 35.6 %copy-start.16 = (bf16[1408,128]{1,0:T(8,128)(2,1)}, bf16[1408,128]{1,0:T(8,128)(2,1)S(1)}, u32[]{:S(2)}) copy-start(bf16[1408,128]{1,0:T(8,128)(2,1)S(1)} %collective-permute-done.1.refs_10_.refs_6_) | copy-start | bytes 1081348
  9.8 25.9 %collective-permute-start.6 = (bf16[128,1536]{1,0:T(8,128)(2,1)S(1)}, bf16[128,1536]{1,0:T(8,128)(2,1)S(1)}, u32[]{:S(2)}, u32[]{:S(2)}) collective-permute-start(bf16[128,1536]{1,0:T(8,128)(2,1)S(1)} %get-tuple-element.52.refs_1_), channel_id=1, source_target_pairs={{0,8},{8,16},{16,24},{24,28},{28,20},{20,12},{12,4},{4,0},{1,9},{9... | collective-permute-start | bytes 1179656 | tf_op jit(solution)/shard_map/ppermute | solution.py:465
  25.0 20.5 %copy-start.17 = (bf16[1408,128]{1,0:T(8,128)(2,1)}, bf16[1408,128]{1,0:T(8,128)(2,1)S(1)}, u32[]{:S(2)}) copy-start(bf16[1408,128]{1,0:T(8,128)(2,1)S(1)} %collective-permute-done.2.refs_11_.refs_7_) | copy-start | bytes 1081348
  25.0 18.5 %collective-permute-start.7 = (bf16[128,1536]{1,0:T(8,128)(2,1)S(1)}, bf16[128,1536]{1,0:T(8,128)(2,1)S(1)}, u32[]{:S(2)}, u32[]{:S(2)}) collective-permute-start(bf16[128,1536]{1,0:T(8,128)(2,1)S(1)} %get-tuple-element.53.refs_0_), channel_id=1, source_target_pairs={{8,0},{16,8},{24,16},{28,24},{20,28},{12,20},{4,12},{0,4},{9,1},{1... | collective-permute-start | bytes 1179656 | tf_op jit(solution)/shard_map/ppermute | solution.py:466
  25.0 9.9 %copy-start.29 = (f32[2,512]{1,0:T(2,128)}, f32[2,512]{1,0:T(2,128)S(1)}, u32[]{:S(2)}) copy-start(f32[2,512]{1,0:T(2,128)S(1)} %collective-permute-done) | copy-start | bytes 12292
  25.0 19.2 %collective-permute-start.3 = (bf16[1408,128]{1,0:T(8,128)(2,1)}, bf16[1408,128]{1,0:T(8,128)(2,1)}, u32[]{:S(2)}, u32[]{:S(2)}) collective-permute-start(bf16[1408,128]{1,0:T(8,128)(2,1)} %get-tuple-element.28), channel_id=1, source_target_pairs={{0,8},{1,24},{2,10},{3,26},{4,12},{5,28},{6,14},{7,30},{8,0},{9,16... | collective-permute-start | bytes 1081352 | tf_op jit(solution)/shard_map/ppermute | solution.py:454
  27.8 45.5 %copy-start.9 = (bf16[128,1536]{1,0:T(8,128)(2,1)}, bf16[128,1536]{1,0:T(8,128)(2,1)S(1)}, u32[]{:S(2)}) copy-start(bf16[128,1536]{1,0:T(8,128)(2,1)S(1)} %collective-permute-done.8.refs_5_) | copy-start | bytes 1179652
  27.8 25.5 %collective-permute-start.12 = (bf16[128,1536]{1,0:T(8,128)(2,1)S(1)}, bf16[128,1536]{1,0:T(8,128)(2,1)S(1)}, u32[]{:S(2)}, u32[]{:S(2)}) collective-permute-start(bf16[128,1536]{1,0:T(8,128)(2,1)S(1)} %collective-permute-done.8.refs_5_), channel_id=1, source_target_pairs={{8,0},{16,8},{24,16},{28,24},{20,28},{12,20},{4,12},{0,4},{9,1},{1... | collective-permute-start | bytes 1179656 | tf_op jit(solution)/shard_map/ppermute | solution.py:466
  33.6 39.7 %copy-start.10 = (bf16[128,1536]{1,0:T(8,128)(2,1)}, bf16[128,1536]{1,0:T(8,128)(2,1)S(1)}, u32[]{:S(2)}) copy-start(bf16[128,1536]{1,0:T(8,128)(2,1)S(1)} %collective-permute-done.5.refs_2_) | copy-start | bytes 1179652
  33.7 19.7 %collective-permute-start.9 = (bf16[128,1536]{1,0:T(8,128)(2,1)S(1)}, bf16[128,1536]{1,0:T(8,128)(2,1)}, u32[]{:S(2)}, u32[]{:S(2)}) collective-permute-start(bf16[128,1536]{1,0:T(8,128)(2,1)S(1)} %collective-permute-done.5.refs_2_), channel_id=1, source_target_pairs={{0,8},{8,16},{16,24},{24,28},{28,20},{20,12},{12,4},{4,0},{1,9},{9... | collective-permute-start | bytes 1179656 | tf_op jit(solution)/shard_map/ppermute | solution.py:465
  35.7 37.6 %copy-start.28 = (s32[4]{0:T(128)}, s32[4]{0:T(128)S(1)}, u32[]{:S(2)}) copy-start(s32[4]{0:T(128)S(1)} %get-tuple-element.32.place) | copy-start | bytes 52
  35.7 37.6 %copy-start.11 = (bf16[128,1536]{1,0:T(8,128)(2,1)}, bf16[128,1536]{1,0:T(8,128)(2,1)S(1)}, u32[]{:S(2)}) copy-start(bf16[128,1536]{1,0:T(8,128)(2,1)S(1)} %collective-permute-done.6.refs_3_) | copy-start | bytes 1179652
  35.7 31.7 %collective-permute-start.4 = (bf16[1408,128]{1,0:T(8,128)(2,1)}, bf16[1408,128]{1,0:T(8,128)(2,1)}, u32[]{:S(2)}, u32[]{:S(2)}) collective-permute-start(bf16[1408,128]{1,0:T(8,128)(2,1)} %get-tuple-element.29), channel_id=1, source_target_pairs={{0,12},{1,28},{2,14},{3,30},{4,0},{5,16},{6,2},{7,18},{8,4},{9,20}... | collective-permute-start | bytes 1081352 | tf_op jit(solution)/shard_map/ppermute | solution.py:454
  43.4 29.9 %copy-start.12 = (bf16[128,1536]{1,0:T(8,128)(2,1)}, bf16[128,1536]{1,0:T(8,128)(2,1)S(1)}, u32[]{:S(2)}) copy-start(bf16[128,1536]{1,0:T(8,128)(2,1)S(1)} %collective-permute-done.7.refs_4_) | copy-start | bytes 1179652
  43.4 24.0 %collective-permute-start.10 = (bf16[128,1536]{1,0:T(8,128)(2,1)S(1)}, bf16[128,1536]{1,0:T(8,128)(2,1)S(1)}, u32[]{:S(2)}, u32[]{:S(2)}) collective-permute-start(bf16[128,1536]{1,0:T(8,128)(2,1)S(1)} %collective-permute-done.6.refs_3_), channel_id=1, source_target_pairs={{0,8},{8,16},{16,24},{24,28},{28,20},{20,12},{12,4},{4,0},{1,9},{9... | collective-permute-start | bytes 1179656 | tf_op jit(solution)/shard_map/ppermute | solution.py:465
  44.2 29.1 %collective-permute-start.11 = (bf16[128,1536]{1,0:T(8,128)(2,1)S(1)}, bf16[128,1536]{1,0:T(8,128)(2,1)S(1)}, u32[]{:S(2)}, u32[]{:S(2)}) collective-permute-start(bf16[128,1536]{1,0:T(8,128)(2,1)S(1)} %collective-permute-done.7.refs_4_), channel_id=1, source_target_pairs={{8,0},{16,8},{24,16},{28,24},{20,28},{12,20},{4,12},{0,4},{9,1},{1... | collective-permute-start | bytes 1179656 | tf_op jit(solution)/shard_map/ppermute | solution.py:466
  53.3 20.1 %copy-start.13 = (bf16[128,1536]{1,0:T(8,128)(2,1)}, bf16[128,1536]{1,0:T(8,128)(2,1)S(1)}, u32[]{:S(2)}) copy-start(bf16[128,1536]{1,0:T(8,128)(2,1)S(1)} %collective-permute-done.12.refs_9_) | copy-start | bytes 1179652
  53.3 28.1 %collective-permute-start.16 = (bf16[128,1536]{1,0:T(8,128)(2,1)S(1)}, bf16[128,1536]{1,0:T(8,128)(2,1)S(1)}, u32[]{:S(2)}, u32[]{:S(2)}) collective-permute-start(bf16[128,1536]{1,0:T(8,128)(2,1)S(1)} %collective-permute-done.12.refs_9_), channel_id=1, source_target_pairs={{8,0},{16,8},{24,16},{28,24},{20,28},{12,20},{4,12},{0,4},{9,1},{1... | collective-permute-start | bytes 1179656 | tf_op jit(solution)/shard_map/ppermute | solution.py:466
  53.3 35.4 %collective-permute-start.13 = (bf16[128,1536]{1,0:T(8,128)(2,1)}, bf16[128,1536]{1,0:T(8,128)(2,1)S(1)}, u32[]{:S(2)}, u32[]{:S(2)}) collective-permute-start(bf16[128,1536]{1,0:T(8,128)(2,1)} %collective-permute-done.9.refs_6_), channel_id=1, source_target_pairs={{0,8},{8,16},{16,24},{24,28},{28,20},{20,12},{12,4},{4,0},{1,9},{9... | collective-permute-start | bytes 1179656 | tf_op jit(solution)/shard_map/ppermute | solution.py:465
  67.5 5.9 %copy-start.14 = (bf16[128,1536]{1,0:T(8,128)(2,1)}, bf16[128,1536]{1,0:T(8,128)(2,1)S(1)}, u32[]{:S(2)}) copy-start(bf16[128,1536]{1,0:T(8,128)(2,1)S(1)} %collective-permute-done.10.refs_7_) | copy-start | bytes 1179652
  67.5 21.8 %collective-permute-start.14 = (bf16[128,1536]{1,0:T(8,128)(2,1)S(1)}, bf16[128,1536]{1,0:T(8,128)(2,1)S(1)}, u32[]{:S(2)}, u32[]{:S(2)}) collective-permute-start(bf16[128,1536]{1,0:T(8,128)(2,1)S(1)} %collective-permute-done.10.refs_7_), channel_id=1, source_target_pairs={{0,8},{8,16},{16,24},{24,28},{28,20},{20,12},{12,4},{4,0},{1,9},{9... | collective-permute-start | bytes 1179656 | tf_op jit(solution)/shard_map/ppermute | solution.py:465
  73.3 0.8 copy-start.15
  73.3 16.5 %collective-permute-start.15 = (bf16[128,1536]{1,0:T(8,128)(2,1)S(1)}, bf16[128,1536]{1,0:T(8,128)(2,1)S(1)}, u32[]{:S(2)}, u32[]{:S(2)}) collective-permute-start(bf16[128,1536]{1,0:T(8,128)(2,1)S(1)} %collective-permute-done.11.refs_8_), channel_id=1, source_target_pairs={{8,0},{16,8},{24,16},{28,24},{20,28},{12,20},{4,12},{0,4},{9,1},{1... | collective-permute-start | bytes 1179656 | tf_op jit(solution)/shard_map/ppermute | solution.py:466
  81.4 16.1 %copy-start.3 = (bf16[128,1536]{1,0:T(8,128)(2,1)}, bf16[128,1536]{1,0:T(8,128)(2,1)S(1)}, u32[]{:S(2)}) copy-start(bf16[128,1536]{1,0:T(8,128)(2,1)S(1)} %collective-permute-done.16.refs_3_.refs_13_) | copy-start | bytes 1179652
  81.4 16.0 %collective-permute-start.18 = (bf16[128,1536]{1,0:T(8,128)(2,1)S(1)}, bf16[128,1536]{1,0:T(8,128)(2,1)S(1)}, u32[]{:S(2)}, u32[]{:S(2)}) collective-permute-start(bf16[128,1536]{1,0:T(8,128)(2,1)S(1)} %collective-permute-done.16.refs_3_.refs_13_), channel_id=1, source_target_pairs={{8,0},{16,8},{24,16},{28,24},{20,28},{12,20},{4,12},{0,4},{9,1},{1... | collective-permute-start | bytes 1179656 | tf_op jit(solution)/shard_map/ppermute | solution.py:469
  88.7 8.8 %copy-start.4 = (bf16[128,1536]{1,0:T(8,128)(2,1)}, bf16[128,1536]{1,0:T(8,128)(2,1)S(1)}, u32[]{:S(2)}) copy-start(bf16[128,1536]{1,0:T(8,128)(2,1)S(1)} %collective-permute-done.13.refs_0_.refs_10_) | copy-start | bytes 1179652
  88.7 8.8 %collective-permute-start.17 = (bf16[128,1536]{1,0:T(8,128)(2,1)S(1)}, bf16[128,1536]{1,0:T(8,128)(2,1)S(1)}, u32[]{:S(2)}, u32[]{:S(2)}) collective-permute-start(bf16[128,1536]{1,0:T(8,128)(2,1)S(1)} %collective-permute-done.13.refs_0_.refs_10_), channel_id=1, source_target_pairs={{0,8},{8,16},{16,24},{24,28},{28,20},{20,12},{12,4},{4,0},{1,9},{9... | collective-permute-start | bytes 1179656 | tf_op jit(solution)/shard_map/ppermute | solution.py:469
  89.3 15.4 %copy-start.24 = (bf16[1024,128]{1,0:T(8,128)(2,1)S(1)}, bf16[1024,128]{1,0:T(8,128)(2,1)}, u32[]{:S(2)}) copy-start(bf16[1024,128]{1,0:T(8,128)(2,1)} %get-tuple-element.37.refs_16_) | copy-start | bytes 786436
  89.3 17.7 %collective-permute-start.20 = (bf16[1280,384]{1,0:T(8,128)(2,1)}, bf16[1280,384]{1,0:T(8,128)(2,1)S(1)}, u32[]{:S(2)}, u32[]{:S(2)}) collective-permute-start(bf16[1280,384]{1,0:T(8,128)(2,1)} %get-tuple-element.39), channel_id=1, source_target_pairs={{0,1},{1,0},{2,3},{3,2},{4,5},{5,4},{6,7},{7,6},{8,9},{9,8},{10,11... | collective-permute-start | bytes 2949128 | tf_op jit(solution)/shard_map/ppermute | solution.py:498
  89.3 8.2 %copy-start.5 = (bf16[128,1536]{1,0:T(8,128)(2,1)}, bf16[128,1536]{1,0:T(8,128)(2,1)S(1)}, u32[]{:S(2)}) copy-start(bf16[128,1536]{1,0:T(8,128)(2,1)S(1)} %collective-permute-done.14.refs_1_.refs_11_) | copy-start | bytes 1179652
  89.9 7.6 %copy-start.6 = (bf16[128,1536]{1,0:T(8,128)(2,1)}, bf16[128,1536]{1,0:T(8,128)(2,1)S(1)}, u32[]{:S(2)}) copy-start(bf16[128,1536]{1,0:T(8,128)(2,1)S(1)} %collective-permute-done.15.refs_2_.refs_12_) | copy-start | bytes 1179652
  97.5 0.8 copy-start.7
  98.2 0.8 copy-start.8
  104.5 2.5 %collective-permute-start.21 = (bf16[768,384]{1,0:T(8,128)(2,1)}, bf16[768,384]{1,0:T(8,128)(2,1)S(1)}, u32[]{:S(2)}, u32[]{:S(2)}) collective-permute-start(bf16[768,384]{1,0:T(8,128)(2,1)} %get-tuple-element.41), channel_id=1, source_target_pairs={{0,1},{1,0},{2,3},{3,2},{4,5},{5,4},{6,7},{7,6},{8,9},{9,8},{10,11... | collective-permute-start | bytes 1769480 | tf_op jit(solution)/shard_map/ppermute | solution.py:501
  104.6 2.4 %collective-permute-start.19 = (bf16[1024,128]{1,0:T(8,128)(2,1)S(1)}, bf16[1024,128]{1,0:T(8,128)(2,1)S(1)}, u32[]{:S(2)}, u32[]{:S(2)}) collective-permute-start(bf16[1024,128]{1,0:T(8,128)(2,1)S(1)} %copy-done.24), channel_id=1, source_target_pairs={{0,1},{1,0},{2,3},{3,2},{4,5},{5,4},{6,7},{7,6},{8,9},{9,8},{10,11... | collective-permute-start | bytes 786440 | tf_op jit(solution)/shard_map/ppermute | solution.py:499
  107.0 0.7 copy-start.25
  107.0 1.1 copy-start.18
  107.0 1.3 copy-start.19
  139.1 33.1 %collective-permute-start.22 = (bf16[1152,128]{1,0:T(8,128)(2,1)}, bf16[1152,128]{1,0:T(8,128)(2,1)S(1)}, u32[]{:S(2)}, u32[]{:S(2)}) collective-permute-start(bf16[1152,128]{1,0:T(8,128)(2,1)} %get-tuple-element.45), channel_id=1, source_target_pairs={{0,0},{16,1},{2,2},{18,3},{4,4},{20,5},{6,6},{22,7},{8,8},{24,9},{... | collective-permute-start | bytes 884744 | tf_op jit(solution)/shard_map/ppermute | solution.py:548
  140.8 31.5 %collective-permute-start.23 = (bf16[1152,128]{1,0:T(8,128)(2,1)}, bf16[1152,128]{1,0:T(8,128)(2,1)S(1)}, u32[]{:S(2)}, u32[]{:S(2)}) collective-permute-start(bf16[1152,128]{1,0:T(8,128)(2,1)} %get-tuple-element.46), channel_id=1, source_target_pairs={{4,0},{20,1},{6,2},{22,3},{8,4},{24,5},{10,6},{26,7},{12,8},{28,9}... | collective-permute-start | bytes 884744 | tf_op jit(solution)/shard_map/ppermute | solution.py:548
  142.8 29.4 %collective-permute-start.24 = (bf16[1152,128]{1,0:T(8,128)(2,1)}, bf16[1152,128]{1,0:T(8,128)(2,1)S(1)}, u32[]{:S(2)}, u32[]{:S(2)}) collective-permute-start(bf16[1152,128]{1,0:T(8,128)(2,1)} %get-tuple-element.47), channel_id=1, source_target_pairs={{8,0},{24,1},{10,2},{26,3},{12,4},{28,5},{14,6},{30,7},{0,8},{16,9... | collective-permute-start | bytes 884744 | tf_op jit(solution)/shard_map/ppermute | solution.py:548
  145.4 26.9 %collective-permute-start.25 = (bf16[1152,128]{1,0:T(8,128)(2,1)}, bf16[1152,128]{1,0:T(8,128)(2,1)S(1)}, u32[]{:S(2)}, u32[]{:S(2)}) collective-permute-start(bf16[1152,128]{1,0:T(8,128)(2,1)} %get-tuple-element.48), channel_id=1, source_target_pairs={{12,0},{28,1},{14,2},{30,3},{0,4},{16,5},{2,6},{18,7},{4,8},{20,9}... | collective-permute-start | bytes 884744 | tf_op jit(solution)/shard_map/ppermute | solution.py:548
  148.1 4.0 %collective-permute-start.26 = (f32[1,128]{1,0:T(1,128)S(1)}, f32[1,128]{1,0:T(1,128)S(1)}, u32[]{:S(2)}, u32[]{:S(2)}) collective-permute-start(f32[1,128]{1,0:T(1,128)S(1)} %slice.19), channel_id=1, source_target_pairs={{0,1},{1,0},{2,3},{3,2},{4,5},{5,4},{6,7},{7,6},{8,9},{9,8},{10,11... | collective-permute-start | bytes 1544 | tf_op jit(solution)/shard_map/ppermute | solution.py:552
  152.8 3.5 %collective-permute-start.27 = (f32[1,128]{1,0:T(1,128)S(1)}, f32[1,128]{1,0:T(1,128)S(1)}, u32[]{:S(2)}, u32[]{:S(2)}) collective-permute-start(f32[1,128]{1,0:T(1,128)S(1)} %slice_add_fusion), channel_id=1, source_target_pairs={{0,2},{1,3},{2,0},{3,1},{4,6},{5,7},{6,4},{7,5},{8,10},{9,11},{10,... | collective-permute-start | bytes 1544 | tf_op jit(solution)/shard_map/ppermute | solution.py:552
  156.3 3.5 %collective-permute-start.28 = (f32[1,128]{1,0:T(1,128)S(1)}, f32[1,128]{1,0:T(1,128)S(1)}, u32[]{:S(2)}, u32[]{:S(2)}) collective-permute-start(f32[1,128]{1,0:T(1,128)S(1)} %add.101), channel_id=1, source_target_pairs={{0,4},{4,0},{8,12},{12,8},{16,20},{20,16},{24,28},{28,24},{1,5},{5... | collective-permute-start | bytes 1544 | tf_op jit(solution)/shard_map/ppermute | solution.py:556
  159.9 3.5 %collective-permute-start.29 = (f32[1,128]{1,0:T(1,128)S(1)}, f32[1,128]{1,0:T(1,128)S(1)}, u32[]{:S(2)}, u32[]{:S(2)}) collective-permute-start(f32[1,128]{1,0:T(1,128)S(1)} %add.102), channel_id=1, source_target_pairs={{0,8},{4,12},{8,0},{12,4},{16,24},{20,28},{24,16},{28,20},{1,9},{5... | collective-permute-start | bytes 1544 | tf_op jit(solution)/shard_map/ppermute | solution.py:556
  163.4 8.3 %collective-permute-start.30 = (f32[1,128]{1,0:T(1,128)S(1)}, f32[1,128]{1,0:T(1,128)S(1)}, u32[]{:S(2)}, u32[]{:S(2)}) collective-permute-start(f32[1,128]{1,0:T(1,128)S(1)} %add.103), channel_id=1, source_target_pairs={{0,16},{4,20},{8,24},{12,28},{16,0},{20,4},{24,8},{28,12},{1,17},{... | collective-permute-start | bytes 1544 | tf_op jit(solution)/shard_map/ppermute | solution.py:556
  172.3 0.7 copy-start.20
  172.3 0.8 copy-start.21
  172.3 0.9 copy-start.22
  172.3 1.0 copy-start.23

commit v3 on v2

--- a/solution.py
+++ b/solution.py
@@ -174,12 +174,11 @@
     for copy in copies:
         copy.wait()
     if with_cot:
-        outs[2][...] = cs[...]
+        outs[1][...] = cs[...]
     for copy in xcopies:
         copy.wait()
     part = jnp.dot(xs[...], ws[...], preferred_element_type=jnp.float32)
-    outs[0][...] = part
-    outs[1][...] = part.astype(jnp.bfloat16)
+    outs[0][...] = part.astype(jnp.bfloat16)
 
 
 def project(chunks, pieces, row_block, tb, with_cot):
@@ -189,7 +188,6 @@
     rows = (pieces[0].shape[0] - tb) // 3
     vmem = pl.BlockSpec(memory_space=pltpu.VMEM)
     shapes = [
-        jax.ShapeDtypeStruct((total, 3 * HD), jnp.float32),
         jax.ShapeDtypeStruct((total, 3 * HD), jnp.bfloat16),
     ]
     if with_cot:
@@ -209,22 +207,29 @@
             pltpu.SemaphoreType.DMA((quarter,)),
         ],
         compiler_params=pltpu.CompilerParams(vmem_limit_bytes=VMEM_BYTES),
+        cost_estimate=pl.CostEstimate(flops=8800000000, bytes_accessed=28800000, transcendentals=0),
         name="project",
     )(row_block, *chunks, *pieces)
 
 
-def head_kernel(nb, tb, rows, quarter, parts, place, edges, *refs):
-    chunks = refs[: 2 * nb]
-    cots = refs[2 * nb : 2 * nb + 2]
-    ends = 2 * nb + 2 + 2 * len(parts)
-    projections = refs[2 * nb + 2 : ends]
-    gain, clip_row, key_row = refs[ends : ends + 3]
-    fisher_out = refs[ends + 3 : ends + 3 + quarter]
-    sum_out = refs[ends + 3 + quarter]
-    (xs, do, proj, qn, kn, vb, qn_t, kn_t, do_t, key_code, es, dps, dk, dv, dproj, grads) = refs[
-        ends + 4 + quarter : -2
+def cover(total, unit):
+    count = max(1, total // unit)
+    return (unit,) * (count - 1) + (total - unit * (count - 1),)
+
+
+def head_kernel(nb, tb, rows, quarter, parts, layout, spans, place, windows, *refs):
+    nc = len(layout)
+    chunks = refs[:nc]
+    cots = refs[nc : nc + 2]
+    ends = nc + 2 + 2 * len(parts)
+    projections = refs[nc + 2 : ends]
+    gain, clip_row, key_row, clips = refs[ends : ends + 4]
+    fisher_out = refs[ends + 4 : ends + 4 + quarter]
+    sum_out = refs[ends + 4 + quarter]
+    (do, q_raw_t, k_raw, qn, kn, vb, qn_t, kn_t, do_t, key_code, es, dps, dk, dv) = refs[
+        ends + 5 + quarter : -5
     ]
-    xsem, csem = refs[-2:]
+    dproj_t, xs, squares, xsem, csem = refs[-5:]
     scale = 1.0 / math.sqrt(HD)
     cot_copies = []
     for k in range(quarter):
@@ -236,16 +241,13 @@
                     src, do.at[pl.ds(pl.multiple_of(block * tb, tb), tb)], csem.at[side, k]
                 )
             )
-    xcopies = [
-        pltpu.make_async_copy(
-            chunks[b],
-            xs.at[pl.ds(pl.multiple_of(place[b // 2] * tb + b % 2 * (tb // 2), tb // 2), tb // 2)],
-            xsem.at[b],
-        )
-        for b in range(2 * nb)
-    ]
+    xcopies = []
+    for b, (block, offset, count) in enumerate(layout):
+        start = pl.multiple_of(place[block] * tb + offset, count)
+        xcopies.append(pltpu.make_async_copy(chunks[b], xs.at[pl.ds(start, count)], xsem.at[b]))
     for copy in cot_copies + xcopies:
         copy.start()
+    q_gain_t = jnp.concatenate([jnp.broadcast_to(gain[0:1, :], (HD, HD)).T] * (tb // HD), 1)
 
     first_block = 0
     for part, count in enumerate(parts):
@@ -255,14 +257,22 @@
             block = place[first_block + b]
             here = pl.ds(pl.multiple_of(block * tb, tb), tb)
             mine, other = projections[2 * part : 2 * part + 2]
-            total = mine[source, :] + other[source, :].astype(jnp.float32)
-            proj[here, :] = total[:, : 2 * HD]
-            for j, (flat, turned) in enumerate(((qn, qn_t), (kn, kn_t))):
-                raw = total[:, j * HD : (j + 1) * HD]
-                inv = lax.rsqrt(jnp.mean(raw * raw, -1, keepdims=True) + EPS)
-                value = raw * inv * gain[j : j + 1, :]
-                flat[here, :] = value.astype(jnp.bfloat16)
-                turned[block] = value.T.astype(jnp.bfloat16)
+            total = mine[source, :].astype(jnp.float32) + other[source, :].astype(jnp.float32)
+            raw = total[:, :HD]
+            inv = lax.rsqrt(jnp.mean(raw * raw, -1, keepdims=True) + EPS)
+            qn[here, :] = (raw * inv * gain[0:1, :]).astype(jnp.bfloat16)
+            raw_t = raw.T
+            inv = lax.rsqrt(jnp.mean(raw_t * raw_t, 0, keepdims=True) + EPS)
+            q_raw_t[block] = raw_t
+            qn_t[block] = (raw_t * inv * q_gain_t).astype(jnp.bfloat16)
+            raw = total[:, HD : 2 * HD]
+            k_raw[here, :] = raw
+            inv = lax.rsqrt(jnp.mean(raw * raw, -1, keepdims=True) + EPS)
+            value = raw * inv * gain[1:2, :]
+            kn[here, :] = value.astype(jnp.bfloat16)
+            value_t = value.T.astype(jnp.bfloat16)
+            for u in range(tb // HD):
+                kn_t[block * (tb // HD) + u] = value_t[:, u * HD : (u + 1) * HD]
             vb[here, :] = total[:, 2 * HD :].astype(jnp.bfloat16)
             key_code[here, :] = jnp.broadcast_to(key_row[block], (HD, tb)).T
             return carry
@@ -281,107 +291,124 @@
 
     lax.fori_loop(0, nb, prepare, 0)
 
-    def backward_norm(upstream, here, j):
-        raw = proj[here, j * HD : (j + 1) * HD]
-        inv = lax.rsqrt(jnp.mean(raw * raw, -1, keepdims=True) + EPS)
-        weighted = gain[j : j + 1, :] * upstream
+    def backward_norm(upstream, raw, weight, axis):
+        inv = lax.rsqrt(jnp.mean(raw * raw, axis, keepdims=True) + EPS)
+        weighted = weight * upstream
         cubed = inv * inv * inv
-        return inv * weighted - raw * (cubed * jnp.mean(raw * weighted, -1, keepdims=True))
-
-    wide = 2 * tb
-    units = nb // 2
-    offset = lax.broadcasted_iota(jnp.int32, (wide, tb), 0) - lax.broadcasted_iota(
-        jnp.int32, (wide, tb), 1
-    )
-
-    def forward(i, unit, sums):
-        here = pl.ds(unit * wide, wide)
+        return inv * weighted - raw * (cubed * jnp.mean(raw * weighted, axis, keepdims=True))
+
+    def tile(start, length):
+        here = pl.ds(pl.multiple_of(start, HD), length)
+        offset = lax.broadcasted_iota(jnp.int32, (length, tb), 0) - lax.broadcasted_iota(
+            jnp.int32, (length, tb), 1
+        )
+        return here, offset
+
+    def forward(i, start, at, length, sums):
+        here, offset = tile(start + at, length)
         s = jnp.dot(kn[here, :], qn_t[i], preferred_element_type=jnp.float32)
         codes = jnp.concatenate([key_code[here, :]] * (tb // HD), 1)
-        allowed = (codes == clip_row[i]) | (offset == i * tb - unit * wide)
+        allowed = (codes == clip_row[i]) | (offset == i * tb - start - at)
         e = jnp.where(allowed, jnp.exp2(s * (scale * math.log2(math.e))), 0.0)
         dp = jnp.dot(vb[here, :], do_t[i], preferred_element_type=jnp.float32)
-        es[here, :] = e
-        dps[here, :] = dp
+        es[at : at + length, :] = e
+        dps[at : at + length, :] = dp
         return (
-            sums[0] + jnp.sum(e.reshape(wide // 8, 8, tb), 0),
-            sums[1] + jnp.sum((e * dp).reshape(wide // 8, 8, tb), 0),
+            sums[0] + jnp.sum(e.reshape(length // 8, 8, tb), 0),
+            sums[1] + jnp.sum((e * dp).reshape(length // 8, 8, tb), 0),
         )
 
     def finish_sums(sums):
         inv_l = 1.0 / jnp.sum(sums[0], 0, keepdims=True)
         return inv_l, jnp.sum(sums[1], 0, keepdims=True) * inv_l
 
-    def backward(i, unit, inv_l, row_dot, dq_t):
-        here = pl.ds(unit * wide, wide)
-        rows_q = pl.ds(pl.multiple_of(i * tb, tb), tb)
-        p = es[here, :] * inv_l
-        ds = (p * (dps[here, :] - row_dot)).astype(jnp.bfloat16)
+    def backward(i, start, at, length, inv_l, row_dot, dq_t):
+        here, _ = tile(start + at, length)
+        rows_q = columns(i)
+        p = es[at : at + length, :] * inv_l
+        ds = (p * (dps[at : at + length, :] - row_dot)).astype(jnp.bfloat16)
         dv[here, :] += jnp.dot(
             p.astype(jnp.bfloat16), do[rows_q, :], preferred_element_type=jnp.float32
         )
         dk[here, :] += jnp.dot(ds, qn[rows_q, :], preferred_element_type=jnp.float32)
-        return (
-            dq_t
-            + jnp.dot(kn_t[2 * unit], ds[:tb], preferred_element_type=jnp.float32)
-            + jnp.dot(kn_t[2 * unit + 1], ds[tb:], preferred_element_type=jnp.float32)
-        )
+        first = (start + at) // HD
+        for u in range(0, length, tb):
+            keys_t = jnp.concatenate(
+                [kn_t[first + (u + v) // HD] for v in range(0, min(tb, length - u), HD)], 1
+            )
+            dq_t += jnp.dot(keys_t, ds[u : u + tb], preferred_element_type=jnp.float32)
+        return dq_t
+
+    def columns(i):
+        return pl.ds(pl.multiple_of(i * tb, tb), tb)
 
     def store_dq(i, dq_t):
-        rows_q = pl.ds(pl.multiple_of(i * tb, tb), tb)
-        dproj[rows_q, :HD] = backward_norm(dq_t.T * scale, rows_q, 0).astype(jnp.bfloat16)
+        dproj_t[:HD, columns(i)] = backward_norm(dq_t * scale, q_raw_t[i], q_gain_t, 0).astype(
+            jnp.bfloat16
+        )
 
     zero = jnp.zeros((8, tb), jnp.float32)
 
-    def queries(i, carry):
+    def query_block(i, start, lengths):
         sums = (zero, zero)
-        for unit in range(units):
-            sums = forward(i, unit, sums)
+        at = 0
+        for length in lengths:
+            sums = forward(i, start, at, length, sums)
+            at += length
         inv_l, row_dot = finish_sums(sums)
         dq_t = jnp.zeros((HD, tb), jnp.float32)
-        for unit in range(units):
-            dq_t = backward(i, unit, inv_l, row_dot, dq_t)
+        at = 0
+        for length in lengths:
+            dq_t = backward(i, start, at, length, inv_l, row_dot, dq_t)
+            at += length
         store_dq(i, dq_t)
+
+    def queries(i, carry):
+        inside = (place[nb + 3 * quarter + i] == windows[len(spans)]) & (
+            place[2 * nb + 3 * quarter + i] == windows[len(spans)]
+        )
+
+        @pl.when(inside)
+        def _():
+            query_block(i, windows[0], cover(spans[0], 2 * tb))
+
+        @pl.when(jnp.logical_not(inside))
+        def _():
+            query_block(i, 0, cover(nb * tb, 2 * tb))
+
         return carry
 
     lax.fori_loop(0, nb, queries, 0)
 
     def keys(b, carry):
-        here = pl.ds(pl.multiple_of(b * tb, tb), tb)
-        dproj[here, HD : 2 * HD] = backward_norm(dk[here, :] * scale, here, 1).astype(jnp.bfloat16)
-        dproj[here, 2 * HD :] = dv[here, :].astype(jnp.bfloat16)
+        here = columns(b)
+        value = backward_norm(dk[here, :] * scale, k_raw[here, :], gain[1:2, :], -1)
+        dproj_t[HD : 2 * HD, here] = value.T.astype(jnp.bfloat16)
+        dproj_t[2 * HD :, here] = dv[here, :].T.astype(jnp.bfloat16)
         return carry
 
     lax.fori_loop(0, nb, keys, 0)
-    grads[...] = jnp.zeros_like(grads)
+
     for copy in xcopies:
         copy.wait()
-
-    def gradient(b, carry):
-        here = pl.ds(pl.multiple_of(b * wide, wide), wide)
-        turned = dproj[here, :].astype(jnp.float32).T
-        clips = jnp.concatenate([clip_row[2 * b], clip_row[2 * b + 1]], 1)
-
-        def one_clip(clip, carry):
-            part = jnp.where(clips == clip, turned, 0.0).astype(jnp.bfloat16)
-            grads[clip] += jnp.dot(part, xs[here, :], preferred_element_type=jnp.float32)
-            return carry
-
-        lax.fori_loop(edges[2 * b], edges[nb + 2 * b + 1] + 1, one_clip, 0)
-        return carry
-
-    lax.fori_loop(0, units, gradient, 0)
-    running = jnp.zeros((HD, rows), jnp.float32)
+    for i, length in enumerate(spans):
+        span = pl.ds(pl.multiple_of(windows[i], HD), length)
+        mask = (clips[:, span] == windows[len(spans) + i]).astype(jnp.float32)
+        part = jnp.dot(
+            dproj_t[:, span] * mask.astype(jnp.bfloat16),
+            xs[span, :],
+            preferred_element_type=jnp.float32,
+        )
+        squares[...] = part * part if i == 0 else squares[...] + part * part
+    running = jnp.zeros((3 * HD, rows), jnp.float32)
     for k in range(quarter):
-        block = place[nb + k]
-        columns = pl.ds(pl.multiple_of(block * rows, rows), rows)
+        lanes = pl.ds(pl.multiple_of(place[nb + k] * rows, rows), rows)
+        piece = squares[:, lanes]
+        running += piece
         for j in range(3):
-            squares = jnp.zeros((HD, rows), jnp.float32)
-            for clip in range(CLIPS):
-                g = grads[clip, j * HD : (j + 1) * HD, columns]
-                squares += g * g
-            running += squares
-            fisher_out[k][j * rows : (j + 1) * rows, :] = squares.T.astype(jnp.bfloat16)
+            fisher_out[k][j * rows : (j + 1) * rows, :] = (
+                piece[j * HD : (j + 1) * HD, :].T.astype(jnp.bfloat16)
+            )
     sum_out[...] = jnp.full((8, HD), jnp.sum(running), jnp.float32)
 
 
@@ -458,16 +485,22 @@
     back = [(b, a) for a, b in forth]
     position = [ring.index(i) for i in range(ns)]
     mine = lax.dynamic_slice_in_dim(tokens, core * half, half, 1)
-    halves = [mine[: tb // 2], mine[tb // 2 :]]
-    chunks, steps = list(halves), [0]
-    ahead, behind = list(halves), list(halves)
+    def halved(parts):
+        return [half for part in parts for half in (part[: tb // 2], part[tb // 2 :])]
+
+    ahead, behind = [mine], [mine]
+    chunks, steps = [[mine]], [0]
     for step in range(1, ns // 2):
+        if step == 3:
+            ahead, behind = halved(ahead), halved(behind)
         ahead = [lax.ppermute(part, "seq", forth) for part in ahead]
         behind = [lax.ppermute(part, "seq", back) for part in behind]
-        chunks += ahead + behind
+        chunks += [ahead, behind]
         steps += [-step, step]
-    chunks += [lax.ppermute(ahead[0], "seq", forth), lax.ppermute(behind[1], "seq", back)]
+    chunks.append([lax.ppermute(ahead[0], "seq", forth), lax.ppermute(behind[1], "seq", back)])
     steps.append(ns // 2)
+    blocks = token_clip.reshape(ns, tb)
+    edges = (blocks[:, 0], blocks[:, -1])
     order = jnp.array([[ring[(position[i] + d) % ns] for d in steps] for i in range(ns)], jnp.int32)
     ks = jnp.arange(quarter, dtype=jnp.int32)
     row_block = ((s - ks) % quarter).astype(jnp.int32)
@@ -477,6 +510,7 @@
             row_block,
             row_block + core * quarter,
             row_block + (1 - core) * quarter,
+            *edges,
         ]
     ).astype(jnp.int32)
 
@@ -488,61 +522,78 @@
     )
     clip_row = token_clip.reshape(ns, 1, tb)
     key_row = jnp.where(key_live == 1, token_clip, -1).reshape(ns, 1, tb)
-    blocks = token_clip.reshape(ns, tb)
-    edges = jnp.concatenate([blocks[:, 0], blocks[:, -1]])
-    place, row_block, edges, gain, clip_row, key_row, *pieces = lax.optimization_barrier(
-        (place, row_block, edges, gain, clip_row, key_row, *pieces)
-    )
-    early = ns - 3
-    first32, first16, cot_mine = project(chunks[: 2 * early], pieces, row_block, tb, True)
-    first_other = lax.ppermute(first16, AXES, swap)
-    cot_other = lax.ppermute(cot_mine, AXES, swap)
-    last32, last16 = project(chunks[2 * early :], pieces, row_block, tb, False)
-    last_other = lax.ppermute(last16, AXES, swap)
-
+    clip_ids = jnp.arange(CLIPS, dtype=jnp.int32)
+    starts = jnp.sum(token_clip[None] < clip_ids[:, None], 1, dtype=jnp.int32)
+    sizes = jnp.sum(token_clip[None] == clip_ids[:, None], 1, dtype=jnp.int32)
+    longest = jnp.argmax(sizes).astype(jnp.int32)
+    ordered = jnp.stack([longest] + [(longest + i) % CLIPS for i in range(1, CLIPS)])
+    spans = (3 * all_tokens // 4 + HD,) + (all_tokens // 4 + HD,) * (CLIPS - 1)
+    windows = jnp.minimum(starts[ordered] // HD * HD, all_tokens - jnp.array(spans, jnp.int32))
+    windows = jnp.concatenate([windows, ordered]).astype(jnp.int32)
+    place, row_block, windows, gain, clip_row, key_row, *pieces = lax.optimization_barrier(
+        (place, row_block, windows, gain, clip_row, key_row, *pieces)
+    )
+    layout = []
+    for block, group in enumerate(chunks):
+        offset = 0
+        for part in group:
+            layout.append((block, offset, part.shape[0]))
+            offset += part.shape[0]
+    parts = (ns - 3, 3)
+    projections = []
+    at = 0
+    for part, count in enumerate(parts):
+        group = [array for block in chunks[at : at + count] for array in block]
+        partial, *cot = project(group, pieces, row_block, tb, part == 0)
+        projections += [partial, lax.ppermute(partial, AXES, swap)]
+        at += count
+        if part == 0:
+            cot_mine = cot[0]
+            cot_other = lax.ppermute(cot_mine, AXES, swap)
+    arrays = [array for block in chunks for array in block]
     *fisher, part_sum = pl.pallas_call(
-        functools.partial(head_kernel, ns, tb, rows, quarter, (early, ns - early)),
+        functools.partial(head_kernel, ns, tb, rows, quarter, parts, tuple(layout), spans),
         out_shape=(
             *[jax.ShapeDtypeStruct((3 * rows, HD), bf16)] * quarter,
             jax.ShapeDtypeStruct((8, HD), f32),
         ),
-        in_specs=[smem, smem] + [hbm] * (2 * ns + 2) + [vmem] * 7,
+        in_specs=[smem, smem] + [hbm] * (len(arrays) + 2) + [vmem] * (len(projections) + 4),
         out_specs=[vmem] * (quarter + 1),
         scratch_shapes=[
-            pltpu.VMEM((all_tokens, half), bf16),
             pltpu.VMEM((all_tokens, HD), bf16),
-            pltpu.VMEM((all_tokens, 2 * HD), f32),
+            pltpu.VMEM((ns, HD, tb), f32),
+            pltpu.VMEM((all_tokens, HD), f32),
             pltpu.VMEM((all_tokens, HD), bf16),
             pltpu.VMEM((all_tokens, HD), bf16),
             pltpu.VMEM((all_tokens, HD), bf16),
             pltpu.VMEM((ns, HD, tb), bf16),
-            pltpu.VMEM((ns, HD, tb), bf16),
+            pltpu.VMEM((all_tokens // HD, HD, HD), bf16),
             pltpu.VMEM((ns, HD, tb), bf16),
             pltpu.VMEM((all_tokens, HD), jnp.int32),
             pltpu.VMEM((all_tokens, tb), f32),
             pltpu.VMEM((all_tokens, tb), f32),
             pltpu.VMEM((all_tokens, HD), f32),
             pltpu.VMEM((all_tokens, HD), f32),
-            pltpu.VMEM((all_tokens, 3 * HD), bf16),
-            pltpu.VMEM((CLIPS, 3 * HD, half), f32),
-            pltpu.SemaphoreType.DMA((2 * ns,)),
+            pltpu.VMEM((3 * HD, all_tokens), bf16),
+            pltpu.VMEM((all_tokens, half), bf16),
+            pltpu.VMEM((3 * HD, half), f32),
+            pltpu.SemaphoreType.DMA((len(arrays),)),
             pltpu.SemaphoreType.DMA((2, quarter)),
         ],
         compiler_params=params,
+        cost_estimate=pl.CostEstimate(flops=34100000000, bytes_accessed=111600000, transcendentals=0),
         name="head",
     )(
         place,
-        edges,
-        *chunks,
+        windows,
+        *arrays,
         cot_mine,
         cot_other,
-        first32,
-        first_other,
-        last32,
-        last_other,
+        *projections,
         gain,
         clip_row,
         key_row,
+        token_clip[None],
     )
 
     returned = [lax.ppermute(fisher[k], AXES, back_perms[k]) for k in range(quarter)]
@@ -579,6 +630,7 @@
             ),
         ),
         compiler_params=params,
+        cost_estimate=pl.CostEstimate(flops=5500000000, bytes_accessed=18000000, transcendentals=0),
         name="finish",
     )(shift, *returned, total, w_qkv, damp_mask)
 
@@ -587,7 +639,7 @@
     ns, nh = mesh.shape["seq"], mesh.shape["head"]
 
     def on_device(*args):
-        if ns == 2 * (args[1].shape[2] // HD) and ns & (ns - 1) == 0 and nh % 2 == 0:
+        if ns == 2 * (args[1].shape[2] // HD) and ns & (ns - 1) == 0 and nh % 2 == 0 and args[4].shape[0] % (4 * HD) == 0:
             return chip_per_head(*args, ns=ns, nh=nh)
         return row_sharded(*args)
 

time: 179 us -> 171 us (0.955)
  waiting for transfers between devices: 51 us -> 39.6 us
  Pallas kernels: 48.4 us -> 42 us
  local copies, waits for them, and re-layouts: 8.1 us -> 11.7 us
  starting transfers between devices: 62.3 us -> 65.3 us
  other arithmetic: 7.26 us -> 9.31 us
    ppermute x4, waiting for transfers between devices: 13.5 us -> 1.17 us  [chip_per_head(): lax.ppermute(piece, AXES, out_perms[k + i])]
    ppermute x1, starting transfers between devices: 0.59 us -> 10.8 us  [chip_per_head(): lax.ppermute(ahead[0], 'seq', forth)]
    ppermute x6 -> x4, waiting for transfers between devices: 12.2 us -> 21.4 us  [chip_per_head(): behind = [lax.ppermute(part, 'seq', back) for part in behind]]
    ppermute x4, starting transfers between devices: 13.1 us -> 4.69 us  [chip_per_head(): lax.ppermute(piece, AXES, out_perms[k + i])]
    ppermute x6 -> x4, starting transfers between devices: 15 us -> 23.4 us  [chip_per_head(): ahead = [lax.ppermute(part, 'seq', forth) for part in ahead]]
    ppermute x1, starting transfers between devices: 7.25 us -> 0.06 us  [chip_per_head(): lax.ppermute(behind[1], 'seq', back)]
    ppermute x1, waiting for transfers between devices: 7.6 us -> 1.07 us  [chip_per_head(): lax.ppermute(behind[1], 'seq', back)]
    pallas_call x1, Pallas kernels: 30.9 us -> 25.6 us  [chip_per_head(): pl.pallas_call(functools.partial(head_kernel, ns, tb, rows, quarter, part...]
  transfers between devices with their start and end apart: 31 -> 27, of which waited for: 11 -> 12; matrix products, arithmetic and copies ran while one was open for 6% -> 9% of each run, Pallas kernels for 7% -> 7%
where the time goes in v3:
time: 171 us; the launch traced here: 170 us
  starting transfers between devices  65.3 us (38%)
  Pallas kernels  42 us (25%)
  waiting for transfers between devices  39.6 us (23%)
  local copies, waits for them, and re-layouts  11.7 us (7%)
  other arithmetic  9.31 us (5%)
  between operations  2.19 us (1%)
    pallas_call x1, Pallas kernels, chip_per_head(): pl.pallas_call(functools.partial(head_kernel, ns, tb, rows, quarter, part...  25.6 us
    ppermute x4, starting transfers between devices, chip_per_head(): ahead = [lax.ppermute(part, 'seq', forth) for part in ahead]  23.4 us
    ppermute x4, waiting for transfers between devices, chip_per_head(): behind = [lax.ppermute(part, 'seq', back) for part in behind]  21.4 us
    pallas_call x2, Pallas kernels, project(): pl.pallas_call(functools.partial(project_kernel, nb, tb, rows, quarter, w...  11.8 us
    ppermute x1, starting transfers between devices, chip_per_head(): lax.ppermute(ahead[0], 'seq', forth)  10.8 us
    ppermute x3, waiting for transfers between devices, chip_per_head(): lax.ppermute(total, 'seq', [(i, i ^ bit) for i in range(ns)])  9.29 us
    ppermute x4, starting transfers between devices, chip_per_head(): lax.ppermute(fisher[k], AXES, back_perms[k])  7.5 us
    ppermute x3, starting transfers between devices, chip_per_head(): lax.ppermute(total, 'seq', [(i, i ^ bit) for i in range(ns)])  7.31 us
  transfers between devices with their start and end apart: 27, of which 12 were waited for; matrix products, arithmetic and copies ran while one was open for 9% of the time, Pallas kernels for 7%

profile of v3, /device:TPU:0, one launch (start us, length us, event | category | flops | bytes accessed | tf_op | source)
XLA Modules:
  0.0 170.1 jit_solution(16042920835326909896)
XLA Ops:
  0.7 1.4 copy-done
  2.0 0.9 constant_dynamic-slice_fusion.1.refs_0_
  3.0 3.0 %collective-permute-start.6 = (bf16[256,1536]{1,0:T(8,128)(2,1)}, bf16[256,1536]{1,0:T(8,128)(2,1)}, u32[]{:S(2)}, u32[]{:S(2)}) collective-permute-start(bf16[256,1536]{1,0:T(8,128)(2,1)} %constant_dynamic-slice_fusion.1.refs_0_), channel_id=1, source_target_pairs={{8,0},{16,8},{24,16},{28,24},{20,28},{12,20},{4,12},{0,4},{9,1},{1... | collective-permute-start | bytes 2359304 | tf_op jit(solution)/shard_map/ppermute | solution.py:497
  6.1 0.2 constant_dynamic-slice_fusion.3
  6.4 1.4 collective-permute-start.1
  7.8 0.8 pad_maximum_fusion.3
  8.5 2.0 %collective-permute-start.2 = (bf16[1408,128]{1,0:T(8,128)(2,1)}, bf16[1408,128]{1,0:T(8,128)(2,1)}, u32[]{:S(2)}, u32[]{:S(2)}) collective-permute-start(bf16[1408,128]{1,0:T(8,128)(2,1)} %pad_maximum_fusion.3), channel_id=1, source_target_pairs={{0,4},{1,20},{2,6},{3,22},{4,8},{5,24},{6,10},{7,26},{8,12},{9,28}... | collective-permute-start | bytes 1081352 | tf_op jit(solution)/shard_map/ppermute | solution.py:481
  10.5 0.2 convert_reduce_fusion.1
  10.7 0.7 iota_reduce_fusion
  12.6 0.7 fusion.2
  13.3 0.6 gather_fusion
  14.0 9.9 %collective-permute-done.6.refs_2_ = bf16[256,1536]{1,0:T(8,128)(2,1)} collective-permute-done((bf16[256,1536]{1,0:T(8,128)(2,1)}, bf16[256,1536]{1,0:T(8,128)(2,1)}, u32[]{:S(2)}, u32[]{:S(2)}) %collective-permute-start.6) | collective-permute-done | bytes 786464 | tf_op jit(solution)/shard_map/ppermute | solution.py:497
  23.9 1.9 %collective-permute-start.8 = (bf16[256,1536]{1,0:T(8,128)(2,1)}, bf16[256,1536]{1,0:T(8,128)(2,1)S(1)}, u32[]{:S(2)}, u32[]{:S(2)}) collective-permute-start(bf16[256,1536]{1,0:T(8,128)(2,1)} %collective-permute-done.6.refs_2_), channel_id=1, source_target_pairs={{8,0},{16,8},{24,16},{28,24},{20,28},{12,20},{4,12},{0,4},{9,1},{1... | collective-permute-start | bytes 2359304 | tf_op jit(solution)/shard_map/ppermute | solution.py:497
  25.8 0.6 multiply_minimum_fusion
  26.4 0.6 compare_select_fusion
  27.0 7.1 %collective-permute-start.7 = (bf16[256,1536]{1,0:T(8,128)(2,1)}, bf16[256,1536]{1,0:T(8,128)(2,1)}, u32[]{:S(2)}, u32[]{:S(2)}) collective-permute-start(bf16[256,1536]{1,0:T(8,128)(2,1)} %collective-permute-done.5.refs_1_), channel_id=1, source_target_pairs={{0,8},{8,16},{16,24},{24,28},{28,20},{20,12},{12,4},{4,0},{1,9},{9... | collective-permute-start | bytes 2359304 | tf_op jit(solution)/shard_map/ppermute | solution.py:496
  34.1 0.5 broadcast_add_fusion.1
  34.6 0.9 pad_maximum_fusion
  35.5 1.2 collective-permute-done.2.refs_6_.refs_7_
  36.7 1.3 collective-permute-start.3
  38.0 11.5 %collective-permute-done.8.refs_4_ = bf16[256,1536]{1,0:T(8,128)(2,1)S(1)} collective-permute-done((bf16[256,1536]{1,0:T(8,128)(2,1)}, bf16[256,1536]{1,0:T(8,128)(2,1)S(1)}, u32[]{:S(2)}, u32[]{:S(2)}) %collective-permute-start.8) | collective-permute-done | bytes 786464 | tf_op jit(solution)/shard_map/ppermute | solution.py:497
  49.6 0.9 collective-permute-start.12
  50.5 1.3 collective-permute-done.7.refs_3_
  51.8 1.9 %fusion.5 = (bf16[128,1536]{1,0:T(8,128)(2,1)S(1)}, bf16[128,1536]{1,0:T(8,128)(2,1)}) fusion(bf16[256,1536]{1,0:T(8,128)(2,1)} %collective-permute-done.7.refs_3_), kind=kLoop, calls=%fused_computation.44 | loop fusion | bytes 1572864 | tf_op jit(solution)/shard_map/slice | solution.py:489
  53.7 14.2 %collective-permute-start.9 = (bf16[128,1536]{1,0:T(8,128)(2,1)}, bf16[128,1536]{1,0:T(8,128)(2,1)S(1)}, u32[]{:S(2)}, u32[]{:S(2)}) collective-permute-start(bf16[128,1536]{1,0:T(8,128)(2,1)} %get-tuple-element.57), channel_id=1, source_target_pairs={{0,8},{8,16},{16,24},{24,28},{28,20},{20,12},{12,4},{4,0},{1,9},{9... | collective-permute-start | bytes 1179656 | tf_op jit(solution)/shard_map/ppermute | solution.py:496
  68.0 0.7 fusion.3
  68.7 0.2 slice_reduce_fusion
  68.8 1.9 %pad_add_fusion.windows = s32[6]{0:T(128)} fusion(s32[1]{0:T(128)} %bitcast.8, s32[1]{0:T(128)} %bitcast.7, s32[1]{0:T(128)} %bitcast.6, s32[3]{0:T(128)} %multiply_minimum_fusion), kind=kLoop, calls=%fused_computation.37 | loop fusion | flops 18 | bytes 48 | tf_op jit(solution)/shard_map/concatenate | solution.py:532
  70.7 1.2 concatenate.38.place
  72.0 1.2 fusion.refs_17_
  73.2 2.0 %collective-permute-start.10 = (bf16[128,1536]{1,0:T(8,128)(2,1)S(1)}, bf16[128,1536]{1,0:T(8,128)(2,1)S(1)}, u32[]{:S(2)}, u32[]{:S(2)}) collective-permute-start(bf16[128,1536]{1,0:T(8,128)(2,1)S(1)} %get-tuple-element.56), channel_id=1, source_target_pairs={{0,8},{8,16},{16,24},{24,28},{28,20},{20,12},{12,4},{4,0},{1,9},{9... | collective-permute-start | bytes 1179656 | tf_op jit(solution)/shard_map/ppermute | solution.py:496
  75.3 0.5 collective-permute-done.9.refs_0_.refs_5_
  75.8 10.8 %collective-permute-start.13 = (bf16[128,1536]{1,0:T(8,128)(2,1)S(1)}, bf16[128,1536]{1,0:T(8,128)(2,1)S(1)}, u32[]{:S(2)}, u32[]{:S(2)}) collective-permute-start(bf16[128,1536]{1,0:T(8,128)(2,1)S(1)} %collective-permute-done.9.refs_0_.refs_5_), channel_id=1, source_target_pairs={{0,8},{8,16},{16,24},{24,28},{28,20},{20,12},{12,4},{4,0},{1,9},{9... | collective-permute-start | bytes 1179656 | tf_op jit(solution)/shard_map/ppermute | solution.py:500
  86.6 6.6 %project.2 = (bf16[1280,384]{1,0:T(8,128)(2,1)}, bf16[1024,128]{1,0:T(8,128)(2,1)}) custom-call(s32[4]{0:T(128)} %copy-done.6, bf16[256,1536]{1,0:T(8,128)(2,1)} %constant_dynamic-slice_fusion.1.refs_0_, bf16[256,1536]{1,0:T(8,128)(2,1)} %collective-permute-done.5.refs_1_, bf16[256,1536]{1,0:T(8,128)(2,1)} %collective-permute-done.6.refs_2_, ...), custom_call_target="tpu_custom_call" | custom-call | flops 8800000000 | bytes 28800000 | tf_op jit(solution)/shard_map/project/pallas_call | solution.py:195
  93.4 1.1 collective-permute-done.14.refs_5_.refs_10_
  94.5 0.7 copy-done.12
  95.2 0.8 copy-done.13
  96.0 5.1 %project.3.refs_15_ = bf16[768,384]{1,0:T(8,128)(2,1)} custom-call(s32[4]{0:T(128)} %copy-done.6, bf16[128,1536]{1,0:T(8,128)(2,1)} %copy-done.9, bf16[128,1536]{1,0:T(8,128)(2,1)} %copy-done.11, bf16[128,1536]{1,0:T(8,128)(2,1)} %copy-done.10, bf16[128,1536]{1,0:T(8,128)(2,1)} %collective-permute-done.12.refs_3_.refs_8_, bf16[128,1536]{1,0:T(8,128)(2,1)} %copy-done.13, ...), custom_call_target="tpu_custom_call" | custom-call | flops 8800000000 | bytes 28800000 | tf_op jit(solution)/shard_map/project/pallas_call | solution.py:195
  101.1 0.7 collective-permute-start.17
  101.9 1.9 %collective-permute-done.15.refs_12_ = bf16[1024,128]{1,0:T(8,128)(2,1)S(1)} collective-permute-done((bf16[1024,128]{1,0:T(8,128)(2,1)S(1)}, bf16[1024,128]{1,0:T(8,128)(2,1)S(1)}, u32[]{:S(2)}, u32[]{:S(2)}) %collective-permute-start.15) | collective-permute-done | bytes 262176 | tf_op jit(solution)/shard_map/ppermute | solution.py:552
  103.9 0.7 copy-done.19
  104.5 0.3 copy-done.7
  104.9 0.2 copy-done.8
  105.1 25.6 %head.1 = (bf16[1152,128]{1,0:T(8,128)(2,1)}, bf16[1152,128]{1,0:T(8,128)(2,1)}, bf16[1152,128]{1,0:T(8,128)(2,1)}, bf16[1152,128]{1,0:T(8,128)(2,1)}, f32[8,128]{1,0:T(8,128)}) custom-call(s32[36]{0:T(128)} %concatenate.38.place, s32[6]{0:T(128)} %pad_add_fusion.windows, bf16[256,1536]{1,0:T(8,128)(2,1)} %constant_dynamic-slice_fusion.1.refs_0_, ...), custom_call_target="tpu_custom_call" | custom-call | flops 34100000768 | bytes 111600000 | tf_op jit(solution)/shard_map/head/pallas_call | solution.py:554
  130.6 1.6 collective-permute-start.18
  132.3 5.3 %collective-permute-start.19 = (bf16[1152,128]{1,0:T(8,128)(2,1)}, bf16[1152,128]{1,0:T(8,128)(2,1)S(1)}, u32[]{:S(2)}, u32[]{:S(2)}) collective-permute-start(bf16[1152,128]{1,0:T(8,128)(2,1)} %get-tuple-element.42), channel_id=1, source_target_pairs={{4,0},{20,1},{6,2},{22,3},{8,4},{24,5},{10,6},{26,7},{12,8},{28,9}... | collective-permute-start | bytes 884744 | tf_op jit(solution)/shard_map/ppermute | solution.py:599
  137.6 0.6 collective-permute-start.21
  138.1 0.7 slice.27
  138.8 3.4 %collective-permute-start.22 = (f32[1,128]{1,0:T(1,128)S(1)}, f32[1,128]{1,0:T(1,128)S(1)}, u32[]{:S(2)}, u32[]{:S(2)}) collective-permute-start(f32[1,128]{1,0:T(1,128)S(1)} %slice.27), channel_id=1, source_target_pairs={{0,1},{1,0},{2,3},{3,2},{4,5},{5,4},{6,7},{7,6},{8,9},{9,8},{10,11... | collective-permute-start | bytes 1544 | tf_op jit(solution)/shard_map/ppermute | solution.py:603
  142.2 0.8 collective-permute-done.22
  143.0 0.7 slice_add_fusion
  143.7 1.5 collective-permute-start.23
  145.2 2.1 %collective-permute-done.23 = f32[1,128]{1,0:T(1,128)S(1)} collective-permute-done((f32[1,128]{1,0:T(1,128)S(1)}, f32[1,128]{1,0:T(1,128)S(1)}, u32[]{:S(2)}, u32[]{:S(2)}) %collective-permute-start.23) | collective-permute-done | bytes 544 | tf_op jit(solution)/shard_map/ppermute | solution.py:603
  147.3 3.6 %collective-permute-start.24 = (f32[1,128]{1,0:T(1,128)S(1)}, f32[1,128]{1,0:T(1,128)S(1)}, u32[]{:S(2)}, u32[]{:S(2)}) collective-permute-start(f32[1,128]{1,0:T(1,128)S(1)} %add.133), channel_id=1, source_target_pairs={{0,4},{4,0},{8,12},{12,8},{16,20},{20,16},{24,28},{28,24},{1,5},{5... | collective-permute-start | bytes 1544 | tf_op jit(solution)/shard_map/ppermute | solution.py:607
  150.9 1.5 collective-permute-done.24
  152.4 3.5 %collective-permute-done.25 = f32[1,128]{1,0:T(1,128)S(1)} collective-permute-done((f32[1,128]{1,0:T(1,128)S(1)}, f32[1,128]{1,0:T(1,128)S(1)}, u32[]{:S(2)}, u32[]{:S(2)}) %collective-permute-start.25) | collective-permute-done | bytes 544 | tf_op jit(solution)/shard_map/ppermute | solution.py:607
  155.9 3.7 %collective-permute-start.26 = (f32[1,128]{1,0:T(1,128)S(1)}, f32[1,128]{1,0:T(1,128)S(1)}, u32[]{:S(2)}, u32[]{:S(2)}) collective-permute-start(f32[1,128]{1,0:T(1,128)S(1)} %add.135), channel_id=1, source_target_pairs={{0,16},{4,20},{8,24},{12,28},{16,0},{20,4},{24,8},{28,12},{1,17},{... | collective-permute-start | bytes 1544 | tf_op jit(solution)/shard_map/ppermute | solution.py:607
  159.6 4.2 %collective-permute-done.26 = f32[1,128]{1,0:T(1,128)S(1)} collective-permute-done((f32[1,128]{1,0:T(1,128)S(1)}, f32[1,128]{1,0:T(1,128)S(1)}, u32[]{:S(2)}, u32[]{:S(2)}) %collective-permute-start.26) | collective-permute-done | bytes 544 | tf_op jit(solution)/shard_map/ppermute | solution.py:607
  163.9 0.5 add.136.refs_4_
  164.4 0.7 copy-done.14
  165.1 0.1 copy-done.15
  165.2 0.1 copy-done.16
  165.3 0.1 copy-done.17
  165.4 4.7 %finish.1 = (f32[3,384,512]{2,1,0:T(8,128)}, bf16[3,384,512]{2,1,0:T(8,128)(2,1)}) custom-call(s32[1]{0:T(128)} %bitcast.shift, bf16[1152,128]{1,0:T(8,128)(2,1)} %copy-done.14, bf16[1152,128]{1,0:T(8,128)(2,1)} %copy-done.15, bf16[1152,128]{1,0:T(8,128)(2,1)} %copy-done.16, bf16[1152,128]{1,0:T(8,128)(2,1)} %copy-done.17, f32[1,128]{1,0:T(1,128)} %add.136.refs_4_, ...), custom_call_target="tpu_custom_call" | custom-call | flops 5500000256 | bytes 18000000 | tf_op jit(solution)/shard_map/finish/pallas_call | solution.py:612
  (65 shorter events, 0.6 us)
Async XLA Ops:
  0.6 1.4 copy-start
  0.6 5.4 %copy-start.3 = (bf16[256,512]{1,0:T(8,128)(2,1)S(1)}, bf16[256,512]{1,0:T(8,128)(2,1)}, u32[]{:S(2)}) copy-start(bf16[256,512]{1,0:T(8,128)(2,1)} %param.12) | copy-start | bytes 786436
  0.7 5.4 %copy-start.1 = (bf16[3,384,512]{2,1,0:T(8,128)(2,1)S(1)}, bf16[3,384,512]{2,1,0:T(8,128)(2,1)}, u32[]{:S(2)}) copy-start(bf16[3,384,512]{2,1,0:T(8,128)(2,1)} %refs_5_.1) | copy-start | bytes 3538948
  3.0 20.9 %collective-permute-start.6 = (bf16[256,1536]{1,0:T(8,128)(2,1)}, bf16[256,1536]{1,0:T(8,128)(2,1)}, u32[]{:S(2)}, u32[]{:S(2)}) collective-permute-start(bf16[256,1536]{1,0:T(8,128)(2,1)} %constant_dynamic-slice_fusion.1.refs_0_), channel_id=1, source_target_pairs={{8,0},{16,8},{24,16},{28,24},{20,28},{12,20},{4,12},{0,4},{9,1},{1... | collective-permute-start | bytes 2359304 | tf_op jit(solution)/shard_map/ppermute | solution.py:497
  6.0 21.0 %collective-permute-start.5 = (bf16[256,1536]{1,0:T(8,128)(2,1)}, bf16[256,1536]{1,0:T(8,128)(2,1)}, u32[]{:S(2)}, u32[]{:S(2)}) collective-permute-start(bf16[256,1536]{1,0:T(8,128)(2,1)} %constant_dynamic-slice_fusion.1.refs_0_), channel_id=1, source_target_pairs={{0,8},{8,16},{16,24},{24,28},{28,20},{20,12},{12,4},{4,0},{1,9},{9... | collective-permute-start | bytes 2359304 | tf_op jit(solution)/shard_map/ppermute | solution.py:496
  6.0 66.0 %collective-permute-start = (f32[2,512]{1,0:T(2,128)}, f32[2,512]{1,0:T(2,128)}, u32[]{:S(2)}, u32[]{:S(2)}) collective-permute-start(f32[2,512]{1,0:T(2,128)} %param.11), channel_id=1, source_target_pairs={{0,1},{1,0},{2,3},{3,2},{4,5},{5,4},{6,7},{7,6},{8,9},{9,8},{10,11... | collective-permute-start | bytes 12296 | tf_op jit(solution)/shard_map/ppermute | solution.py:462
  6.1 4.4 %copy-start.4 = (s32[2048]{0:T(1024)S(1)}, s32[2048]{0:T(1024)}, u32[]{:S(2)}) copy-start(s32[2048]{0:T(1024)} %param.13) | copy-start | bytes 24580
  6.3 19.5 %copy-start.20 = (s32[3]{0:T(128)S(1)}, s32[3]{0:T(128)}, u32[]{:S(2)}) copy-start(s32[3]{0:T(128)} %constant.121) | copy-start | bytes 40
  6.3 20.1 %copy-start.5 = (s32[2048]{0:T(1024)S(1)}, s32[2048]{0:T(1024)}, u32[]{:S(2)}) copy-start(s32[2048]{0:T(1024)} %param.14) | copy-start | bytes 24580
  6.4 29.2 %collective-permute-start.1 = (bf16[1408,128]{1,0:T(8,128)(2,1)S(1)}, bf16[1408,128]{1,0:T(8,128)(2,1)}, u32[]{:S(2)}, u32[]{:S(2)}) collective-permute-start(bf16[1408,128]{1,0:T(8,128)(2,1)S(1)} %pad_maximum_fusion.2), channel_id=1, source_target_pairs={{0,0},{1,16},{2,2},{3,18},{4,4},{5,20},{6,6},{7,22},{8,8},{9,24},{... | collective-permute-start | bytes 1081352 | tf_op jit(solution)/shard_map/ppermute | solution.py:481
  8.5 28.2 %collective-permute-start.2 = (bf16[1408,128]{1,0:T(8,128)(2,1)}, bf16[1408,128]{1,0:T(8,128)(2,1)}, u32[]{:S(2)}, u32[]{:S(2)}) collective-permute-start(bf16[1408,128]{1,0:T(8,128)(2,1)} %pad_maximum_fusion.3), channel_id=1, source_target_pairs={{0,4},{1,20},{2,6},{3,22},{4,8},{5,24},{6,10},{7,26},{8,12},{9,28}... | collective-permute-start | bytes 1081352 | tf_op jit(solution)/shard_map/ppermute | solution.py:481
  14.0 56.8 %copy-start.6 = (s32[4]{0:T(128)}, s32[4]{0:T(128)S(1)}, u32[]{:S(2)}) copy-start(s32[4]{0:T(128)S(1)} %get-tuple-element.31.place) | copy-start | bytes 52
  23.9 25.7 %collective-permute-start.8 = (bf16[256,1536]{1,0:T(8,128)(2,1)}, bf16[256,1536]{1,0:T(8,128)(2,1)S(1)}, u32[]{:S(2)}, u32[]{:S(2)}) collective-permute-start(bf16[256,1536]{1,0:T(8,128)(2,1)} %collective-permute-done.6.refs_2_), channel_id=1, source_target_pairs={{8,0},{16,8},{24,16},{28,24},{20,28},{12,20},{4,12},{0,4},{9,1},{1... | collective-permute-start | bytes 2359304 | tf_op jit(solution)/shard_map/ppermute | solution.py:497
  27.0 24.8 %collective-permute-start.7 = (bf16[256,1536]{1,0:T(8,128)(2,1)}, bf16[256,1536]{1,0:T(8,128)(2,1)}, u32[]{:S(2)}, u32[]{:S(2)}) collective-permute-start(bf16[256,1536]{1,0:T(8,128)(2,1)} %collective-permute-done.5.refs_1_), channel_id=1, source_target_pairs={{0,8},{8,16},{16,24},{24,28},{28,20},{20,12},{12,4},{4,0},{1,9},{9... | collective-permute-start | bytes 2359304 | tf_op jit(solution)/shard_map/ppermute | solution.py:496
  36.7 36.5 %collective-permute-start.3 = (bf16[1408,128]{1,0:T(8,128)(2,1)}, bf16[1408,128]{1,0:T(8,128)(2,1)}, u32[]{:S(2)}, u32[]{:S(2)}) collective-permute-start(bf16[1408,128]{1,0:T(8,128)(2,1)} %get-tuple-element.27), channel_id=1, source_target_pairs={{0,8},{1,24},{2,10},{3,26},{4,12},{5,28},{6,14},{7,30},{8,0},{9,16... | collective-permute-start | bytes 1081352 | tf_op jit(solution)/shard_map/ppermute | solution.py:481
  38.0 35.2 %collective-permute-start.4 = (bf16[1408,128]{1,0:T(8,128)(2,1)}, bf16[1408,128]{1,0:T(8,128)(2,1)}, u32[]{:S(2)}, u32[]{:S(2)}) collective-permute-start(bf16[1408,128]{1,0:T(8,128)(2,1)} %get-tuple-element.28), channel_id=1, source_target_pairs={{0,12},{1,28},{2,14},{3,30},{4,0},{5,16},{6,2},{7,18},{8,4},{9,20}... | collective-permute-start | bytes 1081352 | tf_op jit(solution)/shard_map/ppermute | solution.py:481
  49.5 4.2 %copy-start.2 = (bf16[256,1536]{1,0:T(8,128)(2,1)}, bf16[256,1536]{1,0:T(8,128)(2,1)S(1)}, u32[]{:S(2)}) copy-start(bf16[256,1536]{1,0:T(8,128)(2,1)S(1)} %collective-permute-done.8.refs_4_) | copy-start | bytes 2359300
  49.6 25.7 %collective-permute-start.12 = (bf16[128,1536]{1,0:T(8,128)(2,1)S(1)}, bf16[128,1536]{1,0:T(8,128)(2,1)}, u32[]{:S(2)}, u32[]{:S(2)}) collective-permute-start(bf16[128,1536]{1,0:T(8,128)(2,1)S(1)} %get-tuple-element.54), channel_id=1, source_target_pairs={{8,0},{16,8},{24,16},{28,24},{20,28},{12,20},{4,12},{0,4},{9,1},{1... | collective-permute-start | bytes 1179656 | tf_op jit(solution)/shard_map/ppermute | solution.py:497
  53.7 22.1 %collective-permute-start.9 = (bf16[128,1536]{1,0:T(8,128)(2,1)}, bf16[128,1536]{1,0:T(8,128)(2,1)S(1)}, u32[]{:S(2)}, u32[]{:S(2)}) collective-permute-start(bf16[128,1536]{1,0:T(8,128)(2,1)} %get-tuple-element.57), channel_id=1, source_target_pairs={{0,8},{8,16},{16,24},{24,28},{28,20},{20,12},{12,4},{4,0},{1,9},{9... | collective-permute-start | bytes 1179656 | tf_op jit(solution)/shard_map/ppermute | solution.py:496
  73.2 20.1 %collective-permute-start.11 = (bf16[128,1536]{1,0:T(8,128)(2,1)S(1)}, bf16[128,1536]{1,0:T(8,128)(2,1)S(1)}, u32[]{:S(2)}, u32[]{:S(2)}) collective-permute-start(bf16[128,1536]{1,0:T(8,128)(2,1)S(1)} %get-tuple-element.55), channel_id=1, source_target_pairs={{8,0},{16,8},{24,16},{28,24},{20,28},{12,20},{4,12},{0,4},{9,1},{1... | collective-permute-start | bytes 1179656 | tf_op jit(solution)/shard_map/ppermute | solution.py:497
  73.2 20.2 %collective-permute-start.10 = (bf16[128,1536]{1,0:T(8,128)(2,1)S(1)}, bf16[128,1536]{1,0:T(8,128)(2,1)S(1)}, u32[]{:S(2)}, u32[]{:S(2)}) collective-permute-start(bf16[128,1536]{1,0:T(8,128)(2,1)S(1)} %get-tuple-element.56), channel_id=1, source_target_pairs={{0,8},{8,16},{16,24},{24,28},{28,20},{20,12},{12,4},{4,0},{1,9},{9... | collective-permute-start | bytes 1179656 | tf_op jit(solution)/shard_map/ppermute | solution.py:496
  75.3 19.2 %collective-permute-start.14 = (bf16[128,1536]{1,0:T(8,128)(2,1)}, bf16[128,1536]{1,0:T(8,128)(2,1)S(1)}, u32[]{:S(2)}, u32[]{:S(2)}) collective-permute-start(bf16[128,1536]{1,0:T(8,128)(2,1)} %collective-permute-done.12.refs_3_.refs_8_), channel_id=1, source_target_pairs={{8,0},{16,8},{24,16},{28,24},{20,28},{12,20},{4,12},{0,4},{9,1},{1... | collective-permute-start | bytes 1179656 | tf_op jit(solution)/shard_map/ppermute | solution.py:500
  75.8 17.4 %copy-start.9 = (bf16[128,1536]{1,0:T(8,128)(2,1)}, bf16[128,1536]{1,0:T(8,128)(2,1)S(1)}, u32[]{:S(2)}) copy-start(bf16[128,1536]{1,0:T(8,128)(2,1)S(1)} %collective-permute-done.9.refs_0_.refs_5_) | copy-start | bytes 1179652
  75.8 18.6 %collective-permute-start.13 = (bf16[128,1536]{1,0:T(8,128)(2,1)S(1)}, bf16[128,1536]{1,0:T(8,128)(2,1)S(1)}, u32[]{:S(2)}, u32[]{:S(2)}) collective-permute-start(bf16[128,1536]{1,0:T(8,128)(2,1)S(1)} %collective-permute-done.9.refs_0_.refs_5_), channel_id=1, source_target_pairs={{0,8},{8,16},{16,24},{24,28},{28,20},{20,12},{12,4},{4,0},{1,9},{9... | collective-permute-start | bytes 1179656 | tf_op jit(solution)/shard_map/ppermute | solution.py:500
  93.3 8.6 %copy-start.18 = (bf16[1024,128]{1,0:T(8,128)(2,1)S(1)}, bf16[1024,128]{1,0:T(8,128)(2,1)}, u32[]{:S(2)}) copy-start(bf16[1024,128]{1,0:T(8,128)(2,1)} %get-tuple-element.36.refs_11_) | copy-start | bytes 786436
  93.3 10.6 %collective-permute-start.16 = (bf16[1280,384]{1,0:T(8,128)(2,1)}, bf16[1280,384]{1,0:T(8,128)(2,1)S(1)}, u32[]{:S(2)}, u32[]{:S(2)}) collective-permute-start(bf16[1280,384]{1,0:T(8,128)(2,1)} %get-tuple-element.37.refs_13_), channel_id=1, source_target_pairs={{0,1},{1,0},{2,3},{3,2},{4,5},{5,4},{6,7},{7,6},{8,9},{9,8},{10,11... | collective-permute-start | bytes 2949128 | tf_op jit(solution)/shard_map/ppermute | solution.py:548
  93.4 1.1 copy-start.10
  93.4 1.1 copy-start.11
  94.5 0.8 copy-start.12
  95.2 0.8 copy-start.13
  101.1 2.7 %collective-permute-start.17 = (bf16[768,384]{1,0:T(8,128)(2,1)}, bf16[768,384]{1,0:T(8,128)(2,1)S(1)}, u32[]{:S(2)}, u32[]{:S(2)}) collective-permute-start(bf16[768,384]{1,0:T(8,128)(2,1)} %project.3.refs_15_), channel_id=1, source_target_pairs={{0,1},{1,0},{2,3},{3,2},{4,5},{5,4},{6,7},{7,6},{8,9},{9,8},{10,11... | collective-permute-start | bytes 1769480 | tf_op jit(solution)/shard_map/ppermute | solution.py:548
  101.8 2.0 %collective-permute-start.15 = (bf16[1024,128]{1,0:T(8,128)(2,1)S(1)}, bf16[1024,128]{1,0:T(8,128)(2,1)S(1)}, u32[]{:S(2)}, u32[]{:S(2)}) collective-permute-start(bf16[1024,128]{1,0:T(8,128)(2,1)S(1)} %copy-done.18), channel_id=1, source_target_pairs={{0,1},{1,0},{2,3},{3,2},{4,5},{5,4},{6,7},{7,6},{8,9},{9,8},{10,11... | collective-permute-start | bytes 786440 | tf_op jit(solution)/shard_map/ppermute | solution.py:552
  103.8 0.7 copy-start.19
  103.9 1.0 copy-start.7
  103.9 1.2 copy-start.8
  130.6 33.7 %collective-permute-start.18 = (bf16[1152,128]{1,0:T(8,128)(2,1)}, bf16[1152,128]{1,0:T(8,128)(2,1)S(1)}, u32[]{:S(2)}, u32[]{:S(2)}) collective-permute-start(bf16[1152,128]{1,0:T(8,128)(2,1)} %get-tuple-element.41), channel_id=1, source_target_pairs={{0,0},{16,1},{2,2},{18,3},{4,4},{20,5},{6,6},{22,7},{8,8},{24,9},{... | collective-permute-start | bytes 884744 | tf_op jit(solution)/shard_map/ppermute | solution.py:599
  132.3 32.1 %collective-permute-start.19 = (bf16[1152,128]{1,0:T(8,128)(2,1)}, bf16[1152,128]{1,0:T(8,128)(2,1)S(1)}, u32[]{:S(2)}, u32[]{:S(2)}) collective-permute-start(bf16[1152,128]{1,0:T(8,128)(2,1)} %get-tuple-element.42), channel_id=1, source_target_pairs={{4,0},{20,1},{6,2},{22,3},{8,4},{24,5},{10,6},{26,7},{12,8},{28,9}... | collective-permute-start | bytes 884744 | tf_op jit(solution)/shard_map/ppermute | solution.py:599
  137.6 26.8 %collective-permute-start.20 = (bf16[1152,128]{1,0:T(8,128)(2,1)}, bf16[1152,128]{1,0:T(8,128)(2,1)S(1)}, u32[]{:S(2)}, u32[]{:S(2)}) collective-permute-start(bf16[1152,128]{1,0:T(8,128)(2,1)} %get-tuple-element.43), channel_id=1, source_target_pairs={{8,0},{24,1},{10,2},{26,3},{12,4},{28,5},{14,6},{30,7},{0,8},{16,9... | collective-permute-start | bytes 884744 | tf_op jit(solution)/shard_map/ppermute | solution.py:599
  137.6 26.8 %collective-permute-start.21 = (bf16[1152,128]{1,0:T(8,128)(2,1)}, bf16[1152,128]{1,0:T(8,128)(2,1)S(1)}, u32[]{:S(2)}, u32[]{:S(2)}) collective-permute-start(bf16[1152,128]{1,0:T(8,128)(2,1)} %get-tuple-element.44), channel_id=1, source_target_pairs={{12,0},{28,1},{14,2},{30,3},{0,4},{16,5},{2,6},{18,7},{4,8},{20,9}... | collective-permute-start | bytes 884744 | tf_op jit(solution)/shard_map/ppermute | solution.py:599
  138.8 4.2 %collective-permute-start.22 = (f32[1,128]{1,0:T(1,128)S(1)}, f32[1,128]{1,0:T(1,128)S(1)}, u32[]{:S(2)}, u32[]{:S(2)}) collective-permute-start(f32[1,128]{1,0:T(1,128)S(1)} %slice.27), channel_id=1, source_target_pairs={{0,1},{1,0},{2,3},{3,2},{4,5},{5,4},{6,7},{7,6},{8,9},{9,8},{10,11... | collective-permute-start | bytes 1544 | tf_op jit(solution)/shard_map/ppermute | solution.py:603
  143.7 3.5 %collective-permute-start.23 = (f32[1,128]{1,0:T(1,128)S(1)}, f32[1,128]{1,0:T(1,128)S(1)}, u32[]{:S(2)}, u32[]{:S(2)}) collective-permute-start(f32[1,128]{1,0:T(1,128)S(1)} %slice_add_fusion), channel_id=1, source_target_pairs={{0,2},{1,3},{2,0},{3,1},{4,6},{5,7},{6,4},{7,5},{8,10},{9,11},{10,... | collective-permute-start | bytes 1544 | tf_op jit(solution)/shard_map/ppermute | solution.py:603
  147.3 5.1 %collective-permute-start.24 = (f32[1,128]{1,0:T(1,128)S(1)}, f32[1,128]{1,0:T(1,128)S(1)}, u32[]{:S(2)}, u32[]{:S(2)}) collective-permute-start(f32[1,128]{1,0:T(1,128)S(1)} %add.133), channel_id=1, source_target_pairs={{0,4},{4,0},{8,12},{12,8},{16,20},{20,16},{24,28},{28,24},{1,5},{5... | collective-permute-start | bytes 1544 | tf_op jit(solution)/shard_map/ppermute | solution.py:607
  152.4 3.5 %collective-permute-start.25 = (f32[1,128]{1,0:T(1,128)S(1)}, f32[1,128]{1,0:T(1,128)S(1)}, u32[]{:S(2)}, u32[]{:S(2)}) collective-permute-start(f32[1,128]{1,0:T(1,128)S(1)} %add.134), channel_id=1, source_target_pairs={{0,8},{4,12},{8,0},{12,4},{16,24},{20,28},{24,16},{28,20},{1,9},{5... | collective-permute-start | bytes 1544 | tf_op jit(solution)/shard_map/ppermute | solution.py:607
  155.9 7.9 %collective-permute-start.26 = (f32[1,128]{1,0:T(1,128)S(1)}, f32[1,128]{1,0:T(1,128)S(1)}, u32[]{:S(2)}, u32[]{:S(2)}) collective-permute-start(f32[1,128]{1,0:T(1,128)S(1)} %add.135), channel_id=1, source_target_pairs={{0,16},{4,20},{8,24},{12,28},{16,0},{20,4},{24,8},{28,12},{1,17},{... | collective-permute-start | bytes 1544 | tf_op jit(solution)/shard_map/ppermute | solution.py:607
  164.4 0.7 copy-start.14
  164.4 0.8 copy-start.15
  164.4 0.9 copy-start.16
  164.4 1.0 copy-start.17

commit v4 on v3

--- a/solution.py
+++ b/solution.py
@@ -412,23 +412,44 @@
     sum_out[...] = jnp.full((8, HD), jnp.sum(running), jnp.float32)
 
 
-def finish_kernel(quarter, rows, shift, *refs):
+def finish_kernel(quarter, rows, shift, total, w, mask, *refs):
     pieces = refs[:quarter]
-    total, w, mask, ratio_out, damp_out = refs[quarter:]
-    lane = pl.program_id(0)
+    ratio_out, damp_out, w_in, mask_in, ratio_buf, damp_buf, in_sem, out_sem = refs[quarter:]
+    loads, stores = [], []
+    for k in range(quarter):
+        lanes = pl.ds(pl.multiple_of(lax.rem(shift[0] + k, quarter) * HD, HD), HD)
+        loads.append(
+            (
+                pltpu.make_async_copy(w.at[:, :, lanes], w_in.at[k], in_sem.at[0, k]),
+                pltpu.make_async_copy(mask.at[:, lanes], mask_in.at[k], in_sem.at[1, k]),
+            )
+        )
+        stores.append(
+            (
+                pltpu.make_async_copy(ratio_buf.at[k], ratio_out.at[:, :, lanes], out_sem.at[0, k]),
+                pltpu.make_async_copy(damp_buf.at[k], damp_out.at[:, :, lanes], out_sem.at[1, k]),
+            )
+        )
+    for pair in loads:
+        for copy in pair:
+            copy.start()
     mean = total[0, 0] * (1.0 / (3 * D * HEADS * HD))
     factor = 1.0 / jnp.full((1, HD), mean + EPS, jnp.float32)
-    damp = mask[...].astype(jnp.float32)
     for k in range(quarter):
-
-        @pl.when(lax.rem(shift[0] + k, quarter) == lane)
-        def _():
-            for j in range(3):
-                ratio = pieces[k][j * rows : (j + 1) * rows, :].astype(jnp.float32) * factor
-                ratio_out[j] = ratio
-                damp_out[j] = (w[j].astype(jnp.float32) / (1.0 + damp * ratio)).astype(
-                    jnp.bfloat16
-                )
+        for copy in loads[k]:
+            copy.wait()
+        damp = mask_in[k].astype(jnp.float32)
+        for j in range(3):
+            ratio = pieces[k][j * rows : (j + 1) * rows, :].astype(jnp.float32) * factor
+            ratio_buf[k, j] = ratio
+            damp_buf[k, j] = (w_in[k, j].astype(jnp.float32) / (1.0 + damp * ratio)).astype(
+                jnp.bfloat16
+            )
+        for copy in stores[k]:
+            copy.start()
+    for pair in stores:
+        for copy in pair:
+            copy.wait()
 
 
 def chip_per_head(tokens, w_qkv, gains, cotangent, token_clip, key_live, damp_mask, *, ns, nh):
@@ -607,32 +628,27 @@
         total = total + lax.ppermute(total, "seq", [(i, i ^ bit) for i in range(ns)])
         bit *= 2
     shift = (s % quarter).astype(jnp.int32).reshape(1)
-    full = lambda i, shift: (0, 0)
-    lanes = lambda i, shift: (0, 0, i)
+    hbm_only = pl.BlockSpec(memory_space=pltpu.HBM)
     return pl.pallas_call(
         functools.partial(finish_kernel, quarter, rows),
         out_shape=(
             jax.ShapeDtypeStruct((3, rows, cols), f32),
             jax.ShapeDtypeStruct((3, rows, cols), bf16),
         ),
-        grid_spec=pltpu.PrefetchScalarGridSpec(
-            num_scalar_prefetch=1,
-            grid=(quarter,),
-            in_specs=[pl.BlockSpec((3 * rows, HD), full)] * quarter
-            + [
-                pl.BlockSpec((1, HD), full, memory_space=pltpu.SMEM),
-                pl.BlockSpec((3, rows, HD), lanes),
-                pl.BlockSpec((rows, HD), lambda i, shift: (0, i)),
-            ],
-            out_specs=(
-                pl.BlockSpec((3, rows, HD), lanes),
-                pl.BlockSpec((3, rows, HD), lanes),
-            ),
-        ),
+        in_specs=[smem, smem, hbm_only, hbm_only] + [vmem] * quarter,
+        out_specs=[hbm_only] * 2,
+        scratch_shapes=[
+            pltpu.VMEM((quarter, 3, rows, HD), bf16),
+            pltpu.VMEM((quarter, rows, HD), jnp.int32),
+            pltpu.VMEM((quarter, 3, rows, HD), f32),
+            pltpu.VMEM((quarter, 3, rows, HD), bf16),
+            pltpu.SemaphoreType.DMA((2, quarter)),
+            pltpu.SemaphoreType.DMA((2, quarter)),
+        ],
         compiler_params=params,
         cost_estimate=pl.CostEstimate(flops=5500000000, bytes_accessed=18000000, transcendentals=0),
         name="finish",
-    )(shift, *returned, total, w_qkv, damp_mask)
+    )(shift, total, w_qkv, damp_mask, *returned)
 
 
 def solution(mesh):

time: 171 us -> 170 us (level)
  no operation moved by 1% of the time
where the time goes in v4:
time: 170 us
  starting transfers between devices  65.3 us (38%)
  Pallas kernels  41.6 us (24%)
  waiting for transfers between devices  39.6 us (23%)
  local copies, waits for them, and re-layouts  11.7 us (7%)
  other arithmetic  9.31 us (5%)
  between operations  2.35 us (1%)
    pallas_call x1, Pallas kernels, chip_per_head(): pl.pallas_call(functools.partial(head_kernel, ns, tb, rows, quarter, part...  25.6 us
    ppermute x4, starting transfers between devices, chip_per_head(): ahead = [lax.ppermute(part, 'seq', forth) for part in ahead]  23.4 us
    ppermute x4, waiting for transfers between devices, chip_per_head(): behind = [lax.ppermute(part, 'seq', back) for part in behind]  21.4 us
    pallas_call x2, Pallas kernels, project(): pl.pallas_call(functools.partial(project_kernel, nb, tb, rows, quarter, w...  11.8 us
    ppermute x1, starting transfers between devices, chip_per_head(): lax.ppermute(ahead[0], 'seq', forth)  10.8 us
    ppermute x3, waiting for transfers between devices, chip_per_head(): lax.ppermute(total, 'seq', [(i, i ^ bit) for i in range(ns)])  9.28 us
    ppermute x4, starting transfers between devices, chip_per_head(): lax.ppermute(fisher[k], AXES, back_perms[k])  7.49 us
    ppermute x3, starting transfers between devices, chip_per_head(): lax.ppermute(total, 'seq', [(i, i ^ bit) for i in range(ns)])  7.31 us
  transfers between devices with their start and end apart: 27, of which 12 were waited for; matrix products, arithmetic and copies ran while one was open for 9% of the time, Pallas kernels for 7%

profile of v4, /device:TPU:0, one launch (start us, length us, event | category | flops | bytes accessed | tf_op | source)
XLA Modules:
  0.0 169.9 jit_solution(7187549120875178286)
XLA Ops:
  0.7 1.4 copy-done
  2.0 0.9 constant_dynamic-slice_fusion.1.refs_0_
  3.0 3.0 %collective-permute-start.6 = (bf16[256,1536]{1,0:T(8,128)(2,1)}, bf16[256,1536]{1,0:T(8,128)(2,1)}, u32[]{:S(2)}, u32[]{:S(2)}) collective-permute-start(bf16[256,1536]{1,0:T(8,128)(2,1)} %constant_dynamic-slice_fusion.1.refs_0_), channel_id=1, source_target_pairs={{8,0},{16,8},{24,16},{28,24},{20,28},{12,20},{4,12},{0,4},{9,1},{1... | collective-permute-start | bytes 2359304 | tf_op jit(solution)/shard_map/ppermute | solution.py:518
  6.1 0.2 constant_dynamic-slice_fusion.3
  6.4 1.4 collective-permute-start.1
  7.8 0.8 pad_maximum_fusion.3
  8.5 2.0 %collective-permute-start.2 = (bf16[1408,128]{1,0:T(8,128)(2,1)}, bf16[1408,128]{1,0:T(8,128)(2,1)}, u32[]{:S(2)}, u32[]{:S(2)}) collective-permute-start(bf16[1408,128]{1,0:T(8,128)(2,1)} %pad_maximum_fusion.3), channel_id=1, source_target_pairs={{0,4},{1,20},{2,6},{3,22},{4,8},{5,24},{6,10},{7,26},{8,12},{9,28}... | collective-permute-start | bytes 1081352 | tf_op jit(solution)/shard_map/ppermute | solution.py:502
  10.5 0.2 convert_reduce_fusion.1
  10.7 0.7 iota_reduce_fusion
  12.6 0.7 fusion.2
  13.3 0.6 gather_fusion
  14.0 9.9 %collective-permute-done.6.refs_2_ = bf16[256,1536]{1,0:T(8,128)(2,1)} collective-permute-done((bf16[256,1536]{1,0:T(8,128)(2,1)}, bf16[256,1536]{1,0:T(8,128)(2,1)}, u32[]{:S(2)}, u32[]{:S(2)}) %collective-permute-start.6) | collective-permute-done | bytes 786464 | tf_op jit(solution)/shard_map/ppermute | solution.py:518
  23.9 1.9 %collective-permute-start.8 = (bf16[256,1536]{1,0:T(8,128)(2,1)}, bf16[256,1536]{1,0:T(8,128)(2,1)S(1)}, u32[]{:S(2)}, u32[]{:S(2)}) collective-permute-start(bf16[256,1536]{1,0:T(8,128)(2,1)} %collective-permute-done.6.refs_2_), channel_id=1, source_target_pairs={{8,0},{16,8},{24,16},{28,24},{20,28},{12,20},{4,12},{0,4},{9,1},{1... | collective-permute-start | bytes 2359304 | tf_op jit(solution)/shard_map/ppermute | solution.py:518
  25.8 0.6 multiply_minimum_fusion
  26.4 0.6 compare_select_fusion
  27.0 7.1 %collective-permute-start.7 = (bf16[256,1536]{1,0:T(8,128)(2,1)}, bf16[256,1536]{1,0:T(8,128)(2,1)}, u32[]{:S(2)}, u32[]{:S(2)}) collective-permute-start(bf16[256,1536]{1,0:T(8,128)(2,1)} %collective-permute-done.5.refs_1_), channel_id=1, source_target_pairs={{0,8},{8,16},{16,24},{24,28},{28,20},{20,12},{12,4},{4,0},{1,9},{9... | collective-permute-start | bytes 2359304 | tf_op jit(solution)/shard_map/ppermute | solution.py:517
  34.1 0.5 broadcast_add_fusion.1
  34.6 0.9 pad_maximum_fusion
  35.5 1.2 collective-permute-done.2.refs_6_.refs_7_
  36.7 1.3 collective-permute-start.3
  38.0 11.5 %collective-permute-done.8.refs_4_ = bf16[256,1536]{1,0:T(8,128)(2,1)S(1)} collective-permute-done((bf16[256,1536]{1,0:T(8,128)(2,1)}, bf16[256,1536]{1,0:T(8,128)(2,1)S(1)}, u32[]{:S(2)}, u32[]{:S(2)}) %collective-permute-start.8) | collective-permute-done | bytes 786464 | tf_op jit(solution)/shard_map/ppermute | solution.py:518
  49.6 0.9 collective-permute-start.12
  50.5 1.3 collective-permute-done.7.refs_3_
  51.8 1.9 %fusion.5 = (bf16[128,1536]{1,0:T(8,128)(2,1)S(1)}, bf16[128,1536]{1,0:T(8,128)(2,1)}) fusion(bf16[256,1536]{1,0:T(8,128)(2,1)} %collective-permute-done.7.refs_3_), kind=kLoop, calls=%fused_computation.44 | loop fusion | bytes 1572864 | tf_op jit(solution)/shard_map/slice | solution.py:510
  53.7 14.2 %collective-permute-start.9 = (bf16[128,1536]{1,0:T(8,128)(2,1)}, bf16[128,1536]{1,0:T(8,128)(2,1)S(1)}, u32[]{:S(2)}, u32[]{:S(2)}) collective-permute-start(bf16[128,1536]{1,0:T(8,128)(2,1)} %get-tuple-element.57), channel_id=1, source_target_pairs={{0,8},{8,16},{16,24},{24,28},{28,20},{20,12},{12,4},{4,0},{1,9},{9... | collective-permute-start | bytes 1179656 | tf_op jit(solution)/shard_map/ppermute | solution.py:517
  68.0 0.7 fusion.3
  68.7 0.2 slice_reduce_fusion
  68.8 1.9 %pad_add_fusion.windows = s32[6]{0:T(128)} fusion(s32[1]{0:T(128)} %bitcast.8, s32[1]{0:T(128)} %bitcast.7, s32[1]{0:T(128)} %bitcast.6, s32[3]{0:T(128)} %multiply_minimum_fusion), kind=kLoop, calls=%fused_computation.37 | loop fusion | flops 18 | bytes 48 | tf_op jit(solution)/shard_map/concatenate | solution.py:553
  70.7 1.2 concatenate.38.place
  72.0 1.2 fusion.refs_17_
  73.2 2.0 %collective-permute-start.10 = (bf16[128,1536]{1,0:T(8,128)(2,1)S(1)}, bf16[128,1536]{1,0:T(8,128)(2,1)S(1)}, u32[]{:S(2)}, u32[]{:S(2)}) collective-permute-start(bf16[128,1536]{1,0:T(8,128)(2,1)S(1)} %get-tuple-element.56), channel_id=1, source_target_pairs={{0,8},{8,16},{16,24},{24,28},{28,20},{20,12},{12,4},{4,0},{1,9},{9... | collective-permute-start | bytes 1179656 | tf_op jit(solution)/shard_map/ppermute | solution.py:517
  75.3 0.5 collective-permute-done.9.refs_0_.refs_5_
  75.8 10.8 %collective-permute-start.13 = (bf16[128,1536]{1,0:T(8,128)(2,1)S(1)}, bf16[128,1536]{1,0:T(8,128)(2,1)S(1)}, u32[]{:S(2)}, u32[]{:S(2)}) collective-permute-start(bf16[128,1536]{1,0:T(8,128)(2,1)S(1)} %collective-permute-done.9.refs_0_.refs_5_), channel_id=1, source_target_pairs={{0,8},{8,16},{16,24},{24,28},{28,20},{20,12},{12,4},{4,0},{1,9},{9... | collective-permute-start | bytes 1179656 | tf_op jit(solution)/shard_map/ppermute | solution.py:521
  86.6 6.6 %project.2 = (bf16[1280,384]{1,0:T(8,128)(2,1)}, bf16[1024,128]{1,0:T(8,128)(2,1)}) custom-call(s32[4]{0:T(128)} %copy-done.6, bf16[256,1536]{1,0:T(8,128)(2,1)} %constant_dynamic-slice_fusion.1.refs_0_, bf16[256,1536]{1,0:T(8,128)(2,1)} %collective-permute-done.5.refs_1_, bf16[256,1536]{1,0:T(8,128)(2,1)} %collective-permute-done.6.refs_2_, ...), custom_call_target="tpu_custom_call" | custom-call | flops 8800000000 | bytes 28800000 | tf_op jit(solution)/shard_map/project/pallas_call | solution.py:195
  93.4 1.1 collective-permute-done.14.refs_5_.refs_10_
  94.5 0.7 copy-done.12
  95.2 0.8 copy-done.13
  96.0 5.1 %project.3.refs_15_ = bf16[768,384]{1,0:T(8,128)(2,1)} custom-call(s32[4]{0:T(128)} %copy-done.6, bf16[128,1536]{1,0:T(8,128)(2,1)} %copy-done.9, bf16[128,1536]{1,0:T(8,128)(2,1)} %copy-done.11, bf16[128,1536]{1,0:T(8,128)(2,1)} %copy-done.10, bf16[128,1536]{1,0:T(8,128)(2,1)} %collective-permute-done.12.refs_3_.refs_8_, bf16[128,1536]{1,0:T(8,128)(2,1)} %copy-done.13, ...), custom_call_target="tpu_custom_call" | custom-call | flops 8800000000 | bytes 28800000 | tf_op jit(solution)/shard_map/project/pallas_call | solution.py:195
  101.1 0.7 collective-permute-start.17
  101.9 1.9 %collective-permute-done.15.refs_12_ = bf16[1024,128]{1,0:T(8,128)(2,1)S(1)} collective-permute-done((bf16[1024,128]{1,0:T(8,128)(2,1)S(1)}, bf16[1024,128]{1,0:T(8,128)(2,1)S(1)}, u32[]{:S(2)}, u32[]{:S(2)}) %collective-permute-start.15) | collective-permute-done | bytes 262176 | tf_op jit(solution)/shard_map/ppermute | solution.py:573
  103.9 0.7 copy-done.19
  104.5 0.3 copy-done.7
  104.9 0.2 copy-done.8
  105.1 25.6 %head.1 = (bf16[1152,128]{1,0:T(8,128)(2,1)}, bf16[1152,128]{1,0:T(8,128)(2,1)}, bf16[1152,128]{1,0:T(8,128)(2,1)}, bf16[1152,128]{1,0:T(8,128)(2,1)}, f32[8,128]{1,0:T(8,128)}) custom-call(s32[36]{0:T(128)} %concatenate.38.place, s32[6]{0:T(128)} %pad_add_fusion.windows, bf16[256,1536]{1,0:T(8,128)(2,1)} %constant_dynamic-slice_fusion.1.refs_0_, ...), custom_call_target="tpu_custom_call" | custom-call | flops 34100000768 | bytes 111600000 | tf_op jit(solution)/shard_map/head/pallas_call | solution.py:575
  130.7 1.6 collective-permute-start.23
  132.3 5.3 %collective-permute-start.24 = (bf16[1152,128]{1,0:T(8,128)(2,1)}, bf16[1152,128]{1,0:T(8,128)(2,1)S(1)}, u32[]{:S(2)}, u32[]{:S(2)}) collective-permute-start(bf16[1152,128]{1,0:T(8,128)(2,1)} %get-tuple-element.43), channel_id=1, source_target_pairs={{4,0},{20,1},{6,2},{22,3},{8,4},{24,5},{10,6},{26,7},{12,8},{28,9}... | collective-permute-start | bytes 884744 | tf_op jit(solution)/shard_map/ppermute | solution.py:620
  137.6 0.6 collective-permute-start.26
  138.2 0.7 slice.27
  138.8 3.4 %collective-permute-start.18 = (f32[1,128]{1,0:T(1,128)S(1)}, f32[1,128]{1,0:T(1,128)S(1)}, u32[]{:S(2)}, u32[]{:S(2)}) collective-permute-start(f32[1,128]{1,0:T(1,128)S(1)} %slice.27), channel_id=1, source_target_pairs={{0,1},{1,0},{2,3},{3,2},{4,5},{5,4},{6,7},{7,6},{8,9},{9,8},{10,11... | collective-permute-start | bytes 1544 | tf_op jit(solution)/shard_map/ppermute | solution.py:624
  142.3 0.8 collective-permute-done.18
  143.1 0.7 slice_add_fusion
  143.8 1.5 collective-permute-start.19
  145.2 2.0 %collective-permute-done.19 = f32[1,128]{1,0:T(1,128)S(1)} collective-permute-done((f32[1,128]{1,0:T(1,128)S(1)}, f32[1,128]{1,0:T(1,128)S(1)}, u32[]{:S(2)}, u32[]{:S(2)}) %collective-permute-start.19) | collective-permute-done | bytes 544 | tf_op jit(solution)/shard_map/ppermute | solution.py:624
  147.3 3.6 %collective-permute-start.20 = (f32[1,128]{1,0:T(1,128)S(1)}, f32[1,128]{1,0:T(1,128)S(1)}, u32[]{:S(2)}, u32[]{:S(2)}) collective-permute-start(f32[1,128]{1,0:T(1,128)S(1)} %add.133), channel_id=1, source_target_pairs={{0,4},{4,0},{8,12},{12,8},{16,20},{20,16},{24,28},{28,24},{1,5},{5... | collective-permute-start | bytes 1544 | tf_op jit(solution)/shard_map/ppermute | solution.py:628
  150.9 1.5 collective-permute-done.20
  152.4 3.5 %collective-permute-done.21 = f32[1,128]{1,0:T(1,128)S(1)} collective-permute-done((f32[1,128]{1,0:T(1,128)S(1)}, f32[1,128]{1,0:T(1,128)S(1)}, u32[]{:S(2)}, u32[]{:S(2)}) %collective-permute-start.21) | collective-permute-done | bytes 544 | tf_op jit(solution)/shard_map/ppermute | solution.py:628
  156.0 3.7 %collective-permute-start.22 = (f32[1,128]{1,0:T(1,128)S(1)}, f32[1,128]{1,0:T(1,128)S(1)}, u32[]{:S(2)}, u32[]{:S(2)}) collective-permute-start(f32[1,128]{1,0:T(1,128)S(1)} %add.135), channel_id=1, source_target_pairs={{0,16},{4,20},{8,24},{12,28},{16,0},{20,4},{24,8},{28,12},{1,17},{... | collective-permute-start | bytes 1544 | tf_op jit(solution)/shard_map/ppermute | solution.py:628
  159.7 4.2 %collective-permute-done.22 = f32[1,128]{1,0:T(1,128)S(1)} collective-permute-done((f32[1,128]{1,0:T(1,128)S(1)}, f32[1,128]{1,0:T(1,128)S(1)}, u32[]{:S(2)}, u32[]{:S(2)}) %collective-permute-start.22) | collective-permute-done | bytes 544 | tf_op jit(solution)/shard_map/ppermute | solution.py:628
  163.9 0.5 add.136.total
  164.5 0.7 copy-done.14
  165.1 0.1 copy-done.15
  165.2 0.1 copy-done.16
  165.3 0.1 copy-done.17
  165.4 4.3 %finish.1 = (f32[3,384,512]{2,1,0:T(8,128)}, bf16[3,384,512]{2,1,0:T(8,128)(2,1)}) custom-call(s32[1]{0:T(128)} %bitcast.shift, f32[1,128]{1,0:T(1,128)} %add.136.total, bf16[3,384,512]{2,1,0:T(8,128)(2,1)} %w.1, s32[384,512]{1,0:T(8,128)} %mask.1, bf16[1152,128]{1,0:T(8,128)(2,1)} %copy-done.14, bf16[1152,128]{1,0:T(8,128)(2,1)} %copy-done.15, ...), custom_call_target="tpu_custom_call" | custom-call | flops 5500000256 | bytes 18000000 | tf_op jit(solution)/shard_map/finish/pallas_call | solution.py:632
  (65 shorter events, 0.6 us)
Async XLA Ops:
  0.6 1.4 copy-start
  0.6 5.4 %copy-start.3 = (bf16[256,512]{1,0:T(8,128)(2,1)S(1)}, bf16[256,512]{1,0:T(8,128)(2,1)}, u32[]{:S(2)}) copy-start(bf16[256,512]{1,0:T(8,128)(2,1)} %param.12) | copy-start | bytes 786436
  0.7 5.4 %copy-start.1 = (bf16[3,384,512]{2,1,0:T(8,128)(2,1)S(1)}, bf16[3,384,512]{2,1,0:T(8,128)(2,1)}, u32[]{:S(2)}) copy-start(bf16[3,384,512]{2,1,0:T(8,128)(2,1)} %w.1) | copy-start | bytes 3538948
  3.0 20.9 %collective-permute-start.6 = (bf16[256,1536]{1,0:T(8,128)(2,1)}, bf16[256,1536]{1,0:T(8,128)(2,1)}, u32[]{:S(2)}, u32[]{:S(2)}) collective-permute-start(bf16[256,1536]{1,0:T(8,128)(2,1)} %constant_dynamic-slice_fusion.1.refs_0_), channel_id=1, source_target_pairs={{8,0},{16,8},{24,16},{28,24},{20,28},{12,20},{4,12},{0,4},{9,1},{1... | collective-permute-start | bytes 2359304 | tf_op jit(solution)/shard_map/ppermute | solution.py:518
  6.0 21.0 %collective-permute-start.5 = (bf16[256,1536]{1,0:T(8,128)(2,1)}, bf16[256,1536]{1,0:T(8,128)(2,1)}, u32[]{:S(2)}, u32[]{:S(2)}) collective-permute-start(bf16[256,1536]{1,0:T(8,128)(2,1)} %constant_dynamic-slice_fusion.1.refs_0_), channel_id=1, source_target_pairs={{0,8},{8,16},{16,24},{24,28},{28,20},{20,12},{12,4},{4,0},{1,9},{9... | collective-permute-start | bytes 2359304 | tf_op jit(solution)/shard_map/ppermute | solution.py:517
  6.0 66.0 %collective-permute-start = (f32[2,512]{1,0:T(2,128)}, f32[2,512]{1,0:T(2,128)}, u32[]{:S(2)}, u32[]{:S(2)}) collective-permute-start(f32[2,512]{1,0:T(2,128)} %param.11), channel_id=1, source_target_pairs={{0,1},{1,0},{2,3},{3,2},{4,5},{5,4},{6,7},{7,6},{8,9},{9,8},{10,11... | collective-permute-start | bytes 12296 | tf_op jit(solution)/shard_map/ppermute | solution.py:483
  6.1 4.4 %copy-start.4 = (s32[2048]{0:T(1024)S(1)}, s32[2048]{0:T(1024)}, u32[]{:S(2)}) copy-start(s32[2048]{0:T(1024)} %param.13) | copy-start | bytes 24580
  6.3 19.5 %copy-start.20 = (s32[3]{0:T(128)S(1)}, s32[3]{0:T(128)}, u32[]{:S(2)}) copy-start(s32[3]{0:T(128)} %constant.121) | copy-start | bytes 40
  6.3 20.1 %copy-start.5 = (s32[2048]{0:T(1024)S(1)}, s32[2048]{0:T(1024)}, u32[]{:S(2)}) copy-start(s32[2048]{0:T(1024)} %param.14) | copy-start | bytes 24580
  6.4 29.2 %collective-permute-start.1 = (bf16[1408,128]{1,0:T(8,128)(2,1)S(1)}, bf16[1408,128]{1,0:T(8,128)(2,1)}, u32[]{:S(2)}, u32[]{:S(2)}) collective-permute-start(bf16[1408,128]{1,0:T(8,128)(2,1)S(1)} %pad_maximum_fusion.2), channel_id=1, source_target_pairs={{0,0},{1,16},{2,2},{3,18},{4,4},{5,20},{6,6},{7,22},{8,8},{9,24},{... | collective-permute-start | bytes 1081352 | tf_op jit(solution)/shard_map/ppermute | solution.py:502
  8.5 28.2 %collective-permute-start.2 = (bf16[1408,128]{1,0:T(8,128)(2,1)}, bf16[1408,128]{1,0:T(8,128)(2,1)}, u32[]{:S(2)}, u32[]{:S(2)}) collective-permute-start(bf16[1408,128]{1,0:T(8,128)(2,1)} %pad_maximum_fusion.3), channel_id=1, source_target_pairs={{0,4},{1,20},{2,6},{3,22},{4,8},{5,24},{6,10},{7,26},{8,12},{9,28}... | collective-permute-start | bytes 1081352 | tf_op jit(solution)/shard_map/ppermute | solution.py:502
  14.0 56.8 %copy-start.6 = (s32[4]{0:T(128)}, s32[4]{0:T(128)S(1)}, u32[]{:S(2)}) copy-start(s32[4]{0:T(128)S(1)} %get-tuple-element.31.place) | copy-start | bytes 52
  23.9 25.7 %collective-permute-start.8 = (bf16[256,1536]{1,0:T(8,128)(2,1)}, bf16[256,1536]{1,0:T(8,128)(2,1)S(1)}, u32[]{:S(2)}, u32[]{:S(2)}) collective-permute-start(bf16[256,1536]{1,0:T(8,128)(2,1)} %collective-permute-done.6.refs_2_), channel_id=1, source_target_pairs={{8,0},{16,8},{24,16},{28,24},{20,28},{12,20},{4,12},{0,4},{9,1},{1... | collective-permute-start | bytes 2359304 | tf_op jit(solution)/shard_map/ppermute | solution.py:518
  27.0 24.8 %collective-permute-start.7 = (bf16[256,1536]{1,0:T(8,128)(2,1)}, bf16[256,1536]{1,0:T(8,128)(2,1)}, u32[]{:S(2)}, u32[]{:S(2)}) collective-permute-start(bf16[256,1536]{1,0:T(8,128)(2,1)} %collective-permute-done.5.refs_1_), channel_id=1, source_target_pairs={{0,8},{8,16},{16,24},{24,28},{28,20},{20,12},{12,4},{4,0},{1,9},{9... | collective-permute-start | bytes 2359304 | tf_op jit(solution)/shard_map/ppermute | solution.py:517
  36.7 36.5 %collective-permute-start.3 = (bf16[1408,128]{1,0:T(8,128)(2,1)}, bf16[1408,128]{1,0:T(8,128)(2,1)}, u32[]{:S(2)}, u32[]{:S(2)}) collective-permute-start(bf16[1408,128]{1,0:T(8,128)(2,1)} %get-tuple-element.27), channel_id=1, source_target_pairs={{0,8},{1,24},{2,10},{3,26},{4,12},{5,28},{6,14},{7,30},{8,0},{9,16... | collective-permute-start | bytes 1081352 | tf_op jit(solution)/shard_map/ppermute | solution.py:502
  38.0 35.2 %collective-permute-start.4 = (bf16[1408,128]{1,0:T(8,128)(2,1)}, bf16[1408,128]{1,0:T(8,128)(2,1)}, u32[]{:S(2)}, u32[]{:S(2)}) collective-permute-start(bf16[1408,128]{1,0:T(8,128)(2,1)} %get-tuple-element.28), channel_id=1, source_target_pairs={{0,12},{1,28},{2,14},{3,30},{4,0},{5,16},{6,2},{7,18},{8,4},{9,20}... | collective-permute-start | bytes 1081352 | tf_op jit(solution)/shard_map/ppermute | solution.py:502
  49.5 4.2 %copy-start.2 = (bf16[256,1536]{1,0:T(8,128)(2,1)}, bf16[256,1536]{1,0:T(8,128)(2,1)S(1)}, u32[]{:S(2)}) copy-start(bf16[256,1536]{1,0:T(8,128)(2,1)S(1)} %collective-permute-done.8.refs_4_) | copy-start | bytes 2359300
  49.6 25.7 %collective-permute-start.12 = (bf16[128,1536]{1,0:T(8,128)(2,1)S(1)}, bf16[128,1536]{1,0:T(8,128)(2,1)}, u32[]{:S(2)}, u32[]{:S(2)}) collective-permute-start(bf16[128,1536]{1,0:T(8,128)(2,1)S(1)} %get-tuple-element.54), channel_id=1, source_target_pairs={{8,0},{16,8},{24,16},{28,24},{20,28},{12,20},{4,12},{0,4},{9,1},{1... | collective-permute-start | bytes 1179656 | tf_op jit(solution)/shard_map/ppermute | solution.py:518
  53.7 22.1 %collective-permute-start.9 = (bf16[128,1536]{1,0:T(8,128)(2,1)}, bf16[128,1536]{1,0:T(8,128)(2,1)S(1)}, u32[]{:S(2)}, u32[]{:S(2)}) collective-permute-start(bf16[128,1536]{1,0:T(8,128)(2,1)} %get-tuple-element.57), channel_id=1, source_target_pairs={{0,8},{8,16},{16,24},{24,28},{28,20},{20,12},{12,4},{4,0},{1,9},{9... | collective-permute-start | bytes 1179656 | tf_op jit(solution)/shard_map/ppermute | solution.py:517
  73.2 20.1 %collective-permute-start.11 = (bf16[128,1536]{1,0:T(8,128)(2,1)S(1)}, bf16[128,1536]{1,0:T(8,128)(2,1)S(1)}, u32[]{:S(2)}, u32[]{:S(2)}) collective-permute-start(bf16[128,1536]{1,0:T(8,128)(2,1)S(1)} %get-tuple-element.55), channel_id=1, source_target_pairs={{8,0},{16,8},{24,16},{28,24},{20,28},{12,20},{4,12},{0,4},{9,1},{1... | collective-permute-start | bytes 1179656 | tf_op jit(solution)/shard_map/ppermute | solution.py:518
  73.2 20.2 %collective-permute-start.10 = (bf16[128,1536]{1,0:T(8,128)(2,1)S(1)}, bf16[128,1536]{1,0:T(8,128)(2,1)S(1)}, u32[]{:S(2)}, u32[]{:S(2)}) collective-permute-start(bf16[128,1536]{1,0:T(8,128)(2,1)S(1)} %get-tuple-element.56), channel_id=1, source_target_pairs={{0,8},{8,16},{16,24},{24,28},{28,20},{20,12},{12,4},{4,0},{1,9},{9... | collective-permute-start | bytes 1179656 | tf_op jit(solution)/shard_map/ppermute | solution.py:517
  75.3 19.2 %collective-permute-start.14 = (bf16[128,1536]{1,0:T(8,128)(2,1)}, bf16[128,1536]{1,0:T(8,128)(2,1)S(1)}, u32[]{:S(2)}, u32[]{:S(2)}) collective-permute-start(bf16[128,1536]{1,0:T(8,128)(2,1)} %collective-permute-done.12.refs_3_.refs_8_), channel_id=1, source_target_pairs={{8,0},{16,8},{24,16},{28,24},{20,28},{12,20},{4,12},{0,4},{9,1},{1... | collective-permute-start | bytes 1179656 | tf_op jit(solution)/shard_map/ppermute | solution.py:521
  75.8 17.4 %copy-start.9 = (bf16[128,1536]{1,0:T(8,128)(2,1)}, bf16[128,1536]{1,0:T(8,128)(2,1)S(1)}, u32[]{:S(2)}) copy-start(bf16[128,1536]{1,0:T(8,128)(2,1)S(1)} %collective-permute-done.9.refs_0_.refs_5_) | copy-start | bytes 1179652
  75.8 18.6 %collective-permute-start.13 = (bf16[128,1536]{1,0:T(8,128)(2,1)S(1)}, bf16[128,1536]{1,0:T(8,128)(2,1)S(1)}, u32[]{:S(2)}, u32[]{:S(2)}) collective-permute-start(bf16[128,1536]{1,0:T(8,128)(2,1)S(1)} %collective-permute-done.9.refs_0_.refs_5_), channel_id=1, source_target_pairs={{0,8},{8,16},{16,24},{24,28},{28,20},{20,12},{12,4},{4,0},{1,9},{9... | collective-permute-start | bytes 1179656 | tf_op jit(solution)/shard_map/ppermute | solution.py:521
  93.3 8.6 %copy-start.18 = (bf16[1024,128]{1,0:T(8,128)(2,1)S(1)}, bf16[1024,128]{1,0:T(8,128)(2,1)}, u32[]{:S(2)}) copy-start(bf16[1024,128]{1,0:T(8,128)(2,1)} %get-tuple-element.36.refs_11_) | copy-start | bytes 786436
  93.3 10.6 %collective-permute-start.16 = (bf16[1280,384]{1,0:T(8,128)(2,1)}, bf16[1280,384]{1,0:T(8,128)(2,1)S(1)}, u32[]{:S(2)}, u32[]{:S(2)}) collective-permute-start(bf16[1280,384]{1,0:T(8,128)(2,1)} %get-tuple-element.37.refs_13_), channel_id=1, source_target_pairs={{0,1},{1,0},{2,3},{3,2},{4,5},{5,4},{6,7},{7,6},{8,9},{9,8},{10,11... | collective-permute-start | bytes 2949128 | tf_op jit(solution)/shard_map/ppermute | solution.py:569
  93.4 1.1 copy-start.10
  93.4 1.1 copy-start.11
  94.5 0.8 copy-start.12
  95.2 0.8 copy-start.13
  101.1 2.7 %collective-permute-start.17 = (bf16[768,384]{1,0:T(8,128)(2,1)}, bf16[768,384]{1,0:T(8,128)(2,1)S(1)}, u32[]{:S(2)}, u32[]{:S(2)}) collective-permute-start(bf16[768,384]{1,0:T(8,128)(2,1)} %project.3.refs_15_), channel_id=1, source_target_pairs={{0,1},{1,0},{2,3},{3,2},{4,5},{5,4},{6,7},{7,6},{8,9},{9,8},{10,11... | collective-permute-start | bytes 1769480 | tf_op jit(solution)/shard_map/ppermute | solution.py:569
  101.8 2.0 %collective-permute-start.15 = (bf16[1024,128]{1,0:T(8,128)(2,1)S(1)}, bf16[1024,128]{1,0:T(8,128)(2,1)S(1)}, u32[]{:S(2)}, u32[]{:S(2)}) collective-permute-start(bf16[1024,128]{1,0:T(8,128)(2,1)S(1)} %copy-done.18), channel_id=1, source_target_pairs={{0,1},{1,0},{2,3},{3,2},{4,5},{5,4},{6,7},{7,6},{8,9},{9,8},{10,11... | collective-permute-start | bytes 786440 | tf_op jit(solution)/shard_map/ppermute | solution.py:573
  103.8 0.7 copy-start.19
  103.9 1.0 copy-start.7
  103.9 1.2 copy-start.8
  130.7 33.7 %collective-permute-start.23 = (bf16[1152,128]{1,0:T(8,128)(2,1)}, bf16[1152,128]{1,0:T(8,128)(2,1)S(1)}, u32[]{:S(2)}, u32[]{:S(2)}) collective-permute-start(bf16[1152,128]{1,0:T(8,128)(2,1)} %get-tuple-element.42), channel_id=1, source_target_pairs={{0,0},{16,1},{2,2},{18,3},{4,4},{20,5},{6,6},{22,7},{8,8},{24,9},{... | collective-permute-start | bytes 884744 | tf_op jit(solution)/shard_map/ppermute | solution.py:620
  132.3 32.1 %collective-permute-start.24 = (bf16[1152,128]{1,0:T(8,128)(2,1)}, bf16[1152,128]{1,0:T(8,128)(2,1)S(1)}, u32[]{:S(2)}, u32[]{:S(2)}) collective-permute-start(bf16[1152,128]{1,0:T(8,128)(2,1)} %get-tuple-element.43), channel_id=1, source_target_pairs={{4,0},{20,1},{6,2},{22,3},{8,4},{24,5},{10,6},{26,7},{12,8},{28,9}... | collective-permute-start | bytes 884744 | tf_op jit(solution)/shard_map/ppermute | solution.py:620
  137.6 26.8 %collective-permute-start.25 = (bf16[1152,128]{1,0:T(8,128)(2,1)}, bf16[1152,128]{1,0:T(8,128)(2,1)S(1)}, u32[]{:S(2)}, u32[]{:S(2)}) collective-permute-start(bf16[1152,128]{1,0:T(8,128)(2,1)} %get-tuple-element.44), channel_id=1, source_target_pairs={{8,0},{24,1},{10,2},{26,3},{12,4},{28,5},{14,6},{30,7},{0,8},{16,9... | collective-permute-start | bytes 884744 | tf_op jit(solution)/shard_map/ppermute | solution.py:620
  137.6 26.8 %collective-permute-start.26 = (bf16[1152,128]{1,0:T(8,128)(2,1)}, bf16[1152,128]{1,0:T(8,128)(2,1)S(1)}, u32[]{:S(2)}, u32[]{:S(2)}) collective-permute-start(bf16[1152,128]{1,0:T(8,128)(2,1)} %get-tuple-element.45), channel_id=1, source_target_pairs={{12,0},{28,1},{14,2},{30,3},{0,4},{16,5},{2,6},{18,7},{4,8},{20,9}... | collective-permute-start | bytes 884744 | tf_op jit(solution)/shard_map/ppermute | solution.py:620
  138.8 4.2 %collective-permute-start.18 = (f32[1,128]{1,0:T(1,128)S(1)}, f32[1,128]{1,0:T(1,128)S(1)}, u32[]{:S(2)}, u32[]{:S(2)}) collective-permute-start(f32[1,128]{1,0:T(1,128)S(1)} %slice.27), channel_id=1, source_target_pairs={{0,1},{1,0},{2,3},{3,2},{4,5},{5,4},{6,7},{7,6},{8,9},{9,8},{10,11... | collective-permute-start | bytes 1544 | tf_op jit(solution)/shard_map/ppermute | solution.py:624
  143.8 3.5 %collective-permute-start.19 = (f32[1,128]{1,0:T(1,128)S(1)}, f32[1,128]{1,0:T(1,128)S(1)}, u32[]{:S(2)}, u32[]{:S(2)}) collective-permute-start(f32[1,128]{1,0:T(1,128)S(1)} %slice_add_fusion), channel_id=1, source_target_pairs={{0,2},{1,3},{2,0},{3,1},{4,6},{5,7},{6,4},{7,5},{8,10},{9,11},{10,... | collective-permute-start | bytes 1544 | tf_op jit(solution)/shard_map/ppermute | solution.py:624
  147.3 5.1 %collective-permute-start.20 = (f32[1,128]{1,0:T(1,128)S(1)}, f32[1,128]{1,0:T(1,128)S(1)}, u32[]{:S(2)}, u32[]{:S(2)}) collective-permute-start(f32[1,128]{1,0:T(1,128)S(1)} %add.133), channel_id=1, source_target_pairs={{0,4},{4,0},{8,12},{12,8},{16,20},{20,16},{24,28},{28,24},{1,5},{5... | collective-permute-start | bytes 1544 | tf_op jit(solution)/shard_map/ppermute | solution.py:628
  152.4 3.5 %collective-permute-start.21 = (f32[1,128]{1,0:T(1,128)S(1)}, f32[1,128]{1,0:T(1,128)S(1)}, u32[]{:S(2)}, u32[]{:S(2)}) collective-permute-start(f32[1,128]{1,0:T(1,128)S(1)} %add.134), channel_id=1, source_target_pairs={{0,8},{4,12},{8,0},{12,4},{16,24},{20,28},{24,16},{28,20},{1,9},{5... | collective-permute-start | bytes 1544 | tf_op jit(solution)/shard_map/ppermute | solution.py:628
  156.0 7.9 %collective-permute-start.22 = (f32[1,128]{1,0:T(1,128)S(1)}, f32[1,128]{1,0:T(1,128)S(1)}, u32[]{:S(2)}, u32[]{:S(2)}) collective-permute-start(f32[1,128]{1,0:T(1,128)S(1)} %add.135), channel_id=1, source_target_pairs={{0,16},{4,20},{8,24},{12,28},{16,0},{20,4},{24,8},{28,12},{1,17},{... | collective-permute-start | bytes 1544 | tf_op jit(solution)/shard_map/ppermute | solution.py:628
  164.4 0.7 copy-start.14
  164.4 0.8 copy-start.15
  164.4 0.9 copy-start.16
  164.5 1.0 copy-start.17

commit v5 on v4

--- a/solution.py
+++ b/solution.py
@@ -141,14 +141,28 @@
     return (fisher_ratio, dampened)
 
 
-def project_kernel(nb, tb, rows, quarter, with_cot, place, *refs):
-    chunks = refs[:nb]
-    pieces = refs[nb : nb + quarter]
-    outs = refs[nb + quarter : -6]
+def token_copies(layout, arrays, place, bases, first, target, block_row, sem):
+    copies = []
+    for n, (array, row, block, base, offset, count) in enumerate(layout):
+        start = block_row(block - first) + place[bases + base] + offset
+        copies.append(
+            pltpu.make_async_copy(
+                arrays[array].at[pl.ds(row, count)],
+                target.at[pl.ds(pl.multiple_of(start, 16), count)],
+                sem.at[n],
+            )
+        )
+    return copies
+
+
+def project_kernel(nb, na, tb, rows, quarter, layout, bases, first, nb_all, with_cot, place, *refs):
+    chunks = refs[:na]
+    pieces = refs[na : na + quarter]
+    outs = refs[na + quarter : -6]
     xs, ws, cs, xsem, wsem, csem = refs[-6:]
     copies = []
     for k in range(quarter):
-        start = pl.multiple_of(place[k] * rows, rows)
+        start = pl.multiple_of(place[nb_all + k] * rows, rows)
         for j in range(3):
             copies.append(
                 pltpu.make_async_copy(
@@ -163,12 +177,7 @@
                     pieces[k].at[pl.ds(3 * rows, tb)], cs.at[pl.ds(k * tb, tb)], csem.at[k]
                 )
             )
-    xcopies = []
-    at = 0
-    for b, chunk in enumerate(chunks):
-        height = chunk.shape[0]
-        xcopies.append(pltpu.make_async_copy(chunk, xs.at[pl.ds(at, height)], xsem.at[b]))
-        at += height
+    xcopies = token_copies(layout, chunks, place, bases, first, xs, lambda b: b * tb, xsem)
     for copy in copies + xcopies:
         copy.start()
     for copy in copies:
@@ -181,35 +190,37 @@
     outs[0][...] = part.astype(jnp.bfloat16)
 
 
-def project(chunks, pieces, row_block, tb, with_cot):
-    nb, quarter = len(chunks), len(pieces)
-    half = chunks[0].shape[1]
-    total = sum(chunk.shape[0] for chunk in chunks)
+def project(arrays, layout, first, nb, nb_all, pieces, place, bases, tb, with_cot):
+    quarter = len(pieces)
+    used = sorted({entry[0] for entry in layout})
+    layout = tuple((used.index(entry[0]), *entry[1:]) for entry in layout)
+    arrays = [arrays[i] for i in used]
+    half = arrays[0].shape[1]
     rows = (pieces[0].shape[0] - tb) // 3
     vmem = pl.BlockSpec(memory_space=pltpu.VMEM)
-    shapes = [
-        jax.ShapeDtypeStruct((total, 3 * HD), jnp.bfloat16),
-    ]
+    shapes = [jax.ShapeDtypeStruct((nb * tb, 3 * HD), jnp.bfloat16)]
     if with_cot:
         shapes.append(jax.ShapeDtypeStruct((quarter * tb, HD), jnp.bfloat16))
     return pl.pallas_call(
-        functools.partial(project_kernel, nb, tb, rows, quarter, with_cot),
+        functools.partial(
+            project_kernel, nb, len(arrays), tb, rows, quarter, layout, bases, first, nb_all, with_cot
+        ),
         out_shape=shapes,
         in_specs=[pl.BlockSpec(memory_space=pltpu.SMEM)]
-        + [pl.BlockSpec(memory_space=pl.ANY)] * (nb + quarter),
+        + [pl.BlockSpec(memory_space=pl.ANY)] * (len(arrays) + quarter),
         out_specs=[vmem] * len(shapes),
         scratch_shapes=[
-            pltpu.VMEM((total, half), jnp.bfloat16),
+            pltpu.VMEM((nb * tb, half), jnp.bfloat16),
             pltpu.VMEM((half, 3 * HD), jnp.bfloat16),
             pltpu.VMEM((quarter * tb, HD), jnp.bfloat16),
-            pltpu.SemaphoreType.DMA((nb,)),
+            pltpu.SemaphoreType.DMA((len(layout),)),
             pltpu.SemaphoreType.DMA((quarter, 3)),
             pltpu.SemaphoreType.DMA((quarter,)),
         ],
         compiler_params=pltpu.CompilerParams(vmem_limit_bytes=VMEM_BYTES),
         cost_estimate=pl.CostEstimate(flops=8800000000, bytes_accessed=28800000, transcendentals=0),
         name="project",
-    )(row_block, *chunks, *pieces)
+    )(place, *arrays, *pieces)
 
 
 def cover(total, unit):
@@ -217,8 +228,7 @@
     return (unit,) * (count - 1) + (total - unit * (count - 1),)
 
 
-def head_kernel(nb, tb, rows, quarter, parts, layout, spans, place, windows, *refs):
-    nc = len(layout)
+def head_kernel(nb, nc, tb, rows, quarter, parts, layout, bases, spans, place, windows, *refs):
     chunks = refs[:nc]
     cots = refs[nc : nc + 2]
     ends = nc + 2 + 2 * len(parts)
@@ -241,10 +251,9 @@
                     src, do.at[pl.ds(pl.multiple_of(block * tb, tb), tb)], csem.at[side, k]
                 )
             )
-    xcopies = []
-    for b, (block, offset, count) in enumerate(layout):
-        start = pl.multiple_of(place[block] * tb + offset, count)
-        xcopies.append(pltpu.make_async_copy(chunks[b], xs.at[pl.ds(start, count)], xsem.at[b]))
+    xcopies = token_copies(
+        layout, chunks, place, bases, 0, xs, lambda b: place[b] * tb, xsem
+    )
     for copy in cot_copies + xcopies:
         copy.start()
     q_gain_t = jnp.concatenate([jnp.broadcast_to(gain[0:1, :], (HD, HD)).T] * (tb // HD), 1)
@@ -493,33 +502,59 @@
                 0,
             )
         )
-    pieces = []
-    for k in range(0, quarter, 2):
-        pair = outgoing[k : k + 2]
-        if k:
-            barred = lax.optimization_barrier((*pair, *pieces))
-            pair, pieces = list(barred[: len(pair)]), list(barred[len(pair) :])
-        pieces += [lax.ppermute(piece, AXES, out_perms[k + i]) for i, piece in enumerate(pair)]
-
     ring = list(range(0, ns, 2)) + list(range(1, ns, 2))[::-1]
     forth = [(ring[i], ring[(i + 1) % ns]) for i in range(ns)]
     back = [(b, a) for a, b in forth]
     position = [ring.index(i) for i in range(ns)]
     mine = lax.dynamic_slice_in_dim(tokens, core * half, half, 1)
-    def halved(parts):
-        return [half for part in parts for half in (part[: tb // 2], part[tb // 2 :])]
-
-    ahead, behind = [mine], [mine]
-    chunks, steps = [[mine]], [0]
+    share = 80
+    carried = tb - share
+    side = h // 2 % 2
+    across = [(i, i ^ 2) for i in range(nh)]
+    missing = side * (carried - share)
+    pieces = {}
+    plan = {2: (0, 1), 3: (2, 3)}
+
+    def tie(step, *arrays):
+        for k in plan.get(step, ()):
+            pieces[k] = lax.ppermute(outgoing[k], AXES, out_perms[k])
+        out = lax.optimization_barrier((*arrays, *[pieces[k] for k in plan.get(step, ())]))
+        for k, piece in zip(plan.get(step, ()), out[len(arrays) :]):
+            pieces[k] = piece
+        return out[: len(arrays)]
+
+    arrays, layout, steps = [mine], [(0, 0, 0, 0, 0, tb)], [0]
+    ahead = behind = lax.dynamic_slice_in_dim(mine, side * share, carried, 0)
     for step in range(1, ns // 2):
-        if step == 3:
-            ahead, behind = halved(ahead), halved(behind)
-        ahead = [lax.ppermute(part, "seq", forth) for part in ahead]
-        behind = [lax.ppermute(part, "seq", back) for part in behind]
-        chunks += [ahead, behind]
+        if step > 1:
+            ahead, behind = tie(step, ahead, behind)
+        ahead = lax.ppermute(ahead, "seq", forth)
+        behind = lax.ppermute(behind, "seq", back)
+        both = jnp.concatenate(
+            [lax.dynamic_slice_in_dim(a, missing, share, 0) for a in (ahead, behind)], 0
+        )
+        n, block = len(arrays), len(steps)
+        arrays += [ahead, behind, lax.ppermute(both, "head", across)]
+        layout += [
+            (n, 0, block, 1, 0, carried),
+            (n + 1, 0, block + 1, 1, 0, carried),
+            (n + 2, 0, block, 2, 0, share),
+            (n + 2, share, block + 1, 2, 0, share),
+        ]
         steps += [-step, step]
-    chunks.append([lax.ppermute(ahead[0], "seq", forth), lax.ppermute(behind[1], "seq", back)])
+    cut = carried - share
+    ahead = lax.ppermute(ahead[:cut], "seq", forth)
+    behind = lax.ppermute(behind[cut:], "seq", back)
+    both = jnp.where(side == 0, ahead[:share], behind)
+    n, block = len(arrays), len(steps)
+    arrays += [ahead, behind, lax.ppermute(both, "head", across)]
+    layout += [
+        (n, 0, block, 1, 0, cut),
+        (n + 1, 0, block, 1, cut, share),
+        (n + 2, 0, block, 2, 0, share),
+    ]
     steps.append(ns // 2)
+    pieces = [pieces[k] for k in range(quarter)]
     blocks = token_clip.reshape(ns, tb)
     edges = (blocks[:, 0], blocks[:, -1])
     order = jnp.array([[ring[(position[i] + d) % ns] for d in steps] for i in range(ns)], jnp.int32)
@@ -532,6 +567,7 @@
             row_block + core * quarter,
             row_block + (1 - core) * quarter,
             *edges,
+            jnp.stack([0 * side, side * share, (1 - side) * carried]),
         ]
     ).astype(jnp.int32)
 
@@ -551,29 +587,27 @@
     spans = (3 * all_tokens // 4 + HD,) + (all_tokens // 4 + HD,) * (CLIPS - 1)
     windows = jnp.minimum(starts[ordered] // HD * HD, all_tokens - jnp.array(spans, jnp.int32))
     windows = jnp.concatenate([windows, ordered]).astype(jnp.int32)
-    place, row_block, windows, gain, clip_row, key_row, *pieces = lax.optimization_barrier(
-        (place, row_block, windows, gain, clip_row, key_row, *pieces)
-    )
-    layout = []
-    for block, group in enumerate(chunks):
-        offset = 0
-        for part in group:
-            layout.append((block, offset, part.shape[0]))
-            offset += part.shape[0]
+    place, windows, gain, clip_row, key_row, *pieces = lax.optimization_barrier(
+        (place, windows, gain, clip_row, key_row, *pieces)
+    )
     parts = (ns - 3, 3)
+    bases = 3 * ns + 3 * quarter
     projections = []
-    at = 0
+    first = 0
     for part, count in enumerate(parts):
-        group = [array for block in chunks[at : at + count] for array in block]
-        partial, *cot = project(group, pieces, row_block, tb, part == 0)
+        entries = [entry for entry in layout if first <= entry[2] < first + count]
+        partial, *cot = project(
+            arrays, entries, first, count, ns, pieces, place, bases, tb, part == 0
+        )
         projections += [partial, lax.ppermute(partial, AXES, swap)]
-        at += count
+        first += count
         if part == 0:
             cot_mine = cot[0]
             cot_other = lax.ppermute(cot_mine, AXES, swap)
-    arrays = [array for block in chunks for array in block]
     *fisher, part_sum = pl.pallas_call(
-        functools.partial(head_kernel, ns, tb, rows, quarter, parts, tuple(layout), spans),
+        functools.partial(
+            head_kernel, ns, len(arrays), tb, rows, quarter, parts, tuple(layout), bases, spans
+        ),
         out_shape=(
             *[jax.ShapeDtypeStruct((3 * rows, HD), bf16)] * quarter,
             jax.ShapeDtypeStruct((8, HD), f32),
@@ -598,7 +632,7 @@
             pltpu.VMEM((3 * HD, all_tokens), bf16),
             pltpu.VMEM((all_tokens, half), bf16),
             pltpu.VMEM((3 * HD, half), f32),
-            pltpu.SemaphoreType.DMA((len(arrays),)),
+            pltpu.SemaphoreType.DMA((len(layout),)),
             pltpu.SemaphoreType.DMA((2, quarter)),
         ],
         compiler_params=params,
@@ -655,7 +689,7 @@
     ns, nh = mesh.shape["seq"], mesh.shape["head"]
 
     def on_device(*args):
-        if ns == 2 * (args[1].shape[2] // HD) and ns & (ns - 1) == 0 and nh % 2 == 0 and args[4].shape[0] % (4 * HD) == 0:
+        if ns == 2 * (args[1].shape[2] // HD) and ns & (ns - 1) == 0 and nh % 4 == 0 and args[4].shape[0] % (4 * HD) == 0:
             return chip_per_head(*args, ns=ns, nh=nh)
         return row_sharded(*args)
 

time: 170 us -> 169 us (level)
  starting transfers between devices: 65.3 us -> 45.4 us
  waiting for transfers between devices: 39.6 us -> 57.9 us
  other arithmetic: 9.31 us -> 6.06 us
  local copies, waits for them, and re-layouts: 11.7 us -> 14.6 us
    ppermute x14 -> x16, starting transfers between devices: 44.7 us -> 26.6 us  [the longest x3 7.49 us: chip_per_head(): ahead = lax.ppermute(ahead, 'seq', forth)]
    ppermute x14 -> x16, waiting for transfers between devices: 25.5 us -> 43.6 us  [the longest x3 21.2 us: chip_per_head(): ahead = lax.ppermute(ahead, 'seq', forth)]
    dynamic_slice x0 -> x6, local copies, waits for them, and re-layouts: none -> 4.27 us  [the longest x1 2.24 us: chip_per_head(): ahead = behind = lax.dynamic_slice_in_dim(mine, side * share, carried, 0)]
    ppermute x4, starting transfers between devices: 7.49 us -> 5.36 us  [chip_per_head(): lax.ppermute(fisher[k], AXES, back_perms[k])]
    slice x2, local copies, waits for them, and re-layouts: 1.96 us -> 0.05 us  [the longest x1 0.03 us: chip_per_head(): behind = lax.ppermute(behind[cut:], 'seq', back)]
    unnamed x42 -> x50, local copies, waits for them, and re-layouts: 5.09 us -> 5.27 us
  transfers between devices with their start and end apart: 27 -> 29, of which waited for: 12 -> 12; matrix products, arithmetic and copies ran while one was open for 9% -> 8% of each run, Pallas kernels for 7% -> 7%
where the time goes in v5:
time: 169 us; the launch traced here: 168 us
  waiting for transfers between devices  57.9 us (34%)
  starting transfers between devices  45.4 us (27%)
  Pallas kernels  41.8 us (25%)
  local copies, waits for them, and re-layouts  14.6 us (9%)
  other arithmetic  6.06 us (4%)
  between operations  2.42 us (1%)
    pallas_call x1, Pallas kernels, chip_per_head(): pl.pallas_call(functools.partial(head_kernel, ns, len(arrays), tb, rows,...  25.8 us
    ppermute x3, waiting for transfers between devices, chip_per_head(): ahead = lax.ppermute(ahead, 'seq', forth)  21.2 us
    pallas_call x2, Pallas kernels, project(): pl.pallas_call(functools.partial(project_kernel, nb, len(arrays), tb, row...  11.7 us
    ppermute x3, waiting for transfers between devices, chip_per_head(): lax.ppermute(total, 'seq', [(i, i ^ bit) for i in range(ns)])  9.44 us
    ppermute x4, waiting for transfers between devices, tie(): pieces[k] = lax.ppermute(outgoing[k], AXES, out_perms[k])  8.32 us
    ppermute x3, waiting for transfers between devices, chip_per_head(): behind = lax.ppermute(behind, 'seq', back)  8.27 us
    ppermute x3, starting transfers between devices, chip_per_head(): ahead = lax.ppermute(ahead, 'seq', forth)  7.49 us
    ppermute x3, starting transfers between devices, chip_per_head(): lax.ppermute(total, 'seq', [(i, i ^ bit) for i in range(ns)])  7.37 us
  transfers between devices with their start and end apart: 29, of which 12 were waited for; matrix products, arithmetic and copies ran while one was open for 8% of the time, Pallas kernels for 7%

profile of v5, /device:TPU:0, one launch (start us, length us, event | category | flops | bytes accessed | tf_op | source)
XLA Modules:
  0.0 168.2 jit_solution(2546132438517982138)
XLA Ops:
  0.7 2.2 %dynamic_slice.57 = bf16[176,1536]{1,0:T(8,128)(2,1)} dynamic-slice(bf16[256,3072]{1,0:T(8,128)(2,1)} %param.9, s32[]{:T(128)S(6)} %select_n.146, s32[]{:T(128)S(6)} %select_n.148), dynamic_slice_sizes={176,1536} | dynamic-slice | bytes 1081348 | tf_op jit(solution)/shard_map/dynamic_slice | solution.py:527
  2.9 3.0 %collective-permute-start.2 = (bf16[176,1536]{1,0:T(8,128)(2,1)}, bf16[176,1536]{1,0:T(8,128)(2,1)}, u32[]{:S(2)}, u32[]{:S(2)}) collective-permute-start(bf16[176,1536]{1,0:T(8,128)(2,1)} %dynamic_slice.57), channel_id=1, source_target_pairs={{8,0},{16,8},{24,16},{28,24},{20,28},{12,20},{4,12},{0,4},{9,1},{1... | collective-permute-start | bytes 1622024 | tf_op jit(solution)/shard_map/ppermute | solution.py:532
  6.0 1.0 constant_dynamic-slice_fusion.8
  7.0 0.2 constant_dynamic-slice_fusion.9
  7.2 1.6 collective-permute-start.3
  8.8 2.0 %collective-permute-start.4 = (bf16[1408,128]{1,0:T(8,128)(2,1)S(1)}, bf16[1408,128]{1,0:T(8,128)(2,1)}, u32[]{:S(2)}, u32[]{:S(2)}) collective-permute-start(bf16[1408,128]{1,0:T(8,128)(2,1)S(1)} %pad_maximum_fusion.4), channel_id=1, source_target_pairs={{0,4},{1,20},{2,6},{3,22},{4,8},{5,24},{6,10},{7,26},{8,12},{9,28}... | collective-permute-start | bytes 1081352 | tf_op jit(solution)/shard_map/ppermute | solution.py:520
  11.0 0.7 iota_reduce_fusion
  12.9 0.9 constant_dynamic-slice_fusion.7.refs_0_
  13.9 0.6 fusion.2
  14.5 0.6 compare_select_fusion
  15.1 0.6 gather_fusion
  15.9 0.7 fusion.3
  16.8 1.2 pad_add_fusion.windows
  17.9 0.7 concatenate.47.place
  18.6 1.6 collective-permute-start.7
  20.2 1.3 fusion.refs_19_
  21.5 1.4 collective-permute-start.8
  22.9 5.9 %collective-permute-done.4.refs_8_.refs_7_ = bf16[1408,128]{1,0:T(8,128)(2,1)} collective-permute-done((bf16[1408,128]{1,0:T(8,128)(2,1)S(1)}, bf16[1408,128]{1,0:T(8,128)(2,1)}, u32[]{:S(2)}, u32[]{:S(2)}) %collective-permute-start.4) | collective-permute-done | bytes 360480 | tf_op jit(solution)/shard_map/ppermute | solution.py:520
  28.8 1.4 collective-permute-start.5
  30.2 0.6 collective-permute-start.6
  30.8 1.0 constant_dynamic-slice_fusion.5
  31.8 1.0 constant_dynamic-slice_fusion.6
  32.8 1.5 collective-permute-start.9
  34.4 2.4 %collective-permute-done.8.refs_10_.refs_9_ = bf16[1408,128]{1,0:T(8,128)(2,1)S(1)} collective-permute-done((bf16[1408,128]{1,0:T(8,128)(2,1)S(1)}, bf16[1408,128]{1,0:T(8,128)(2,1)S(1)}, u32[]{:S(2)}, u32[]{:S(2)}) %collective-permute-start.8) | collective-permute-done | bytes 360480 | tf_op jit(solution)/shard_map/ppermute | solution.py:520
  36.8 11.7 %collective-permute-done.5.refs_4_ = bf16[176,1536]{1,0:T(8,128)(2,1)S(1)} collective-permute-done((bf16[176,1536]{1,0:T(8,128)(2,1)}, bf16[176,1536]{1,0:T(8,128)(2,1)S(1)}, u32[]{:S(2)}, u32[]{:S(2)}) %collective-permute-start.5) | collective-permute-done | bytes 540704 | tf_op jit(solution)/shard_map/ppermute | solution.py:531
  48.5 8.2 %collective-permute-done.6.refs_5_ = bf16[176,1536]{1,0:T(8,128)(2,1)S(1)} collective-permute-done((bf16[176,1536]{1,0:T(8,128)(2,1)}, bf16[176,1536]{1,0:T(8,128)(2,1)S(1)}, u32[]{:S(2)}, u32[]{:S(2)}) %collective-permute-start.6) | collective-permute-done | bytes 540704 | tf_op jit(solution)/shard_map/ppermute | solution.py:532
  56.7 6.0 %collective-permute-start.11 = (bf16[176,1536]{1,0:T(8,128)(2,1)S(1)}, bf16[176,1536]{1,0:T(8,128)(2,1)S(1)}, u32[]{:S(2)}, u32[]{:S(2)}) collective-permute-start(bf16[176,1536]{1,0:T(8,128)(2,1)S(1)} %collective-permute-done.5.refs_4_), channel_id=1, source_target_pairs={{0,8},{8,16},{16,24},{24,28},{28,20},{20,12},{12,4},{4,0},{1,9},{9... | collective-permute-start | bytes 1622024 | tf_op jit(solution)/shard_map/ppermute | solution.py:531
  62.8 1.5 collective-permute-start.10
  64.3 9.5 %collective-permute-done.11.refs_0_.refs_7_ = bf16[176,1536]{1,0:T(8,128)(2,1)S(1)} collective-permute-done((bf16[176,1536]{1,0:T(8,128)(2,1)S(1)}, bf16[176,1536]{1,0:T(8,128)(2,1)S(1)}, u32[]{:S(2)}, u32[]{:S(2)}) %collective-permute-start.11) | collective-permute-done | bytes 540704 | tf_op jit(solution)/shard_map/ppermute | solution.py:531
  73.9 2.5 %collective-permute-start.14 = (bf16[96,1536]{1,0:T(8,128)(2,1)S(1)}, bf16[96,1536]{1,0:T(8,128)(2,1)S(1)}, u32[]{:S(2)}, u32[]{:S(2)}) collective-permute-start(bf16[96,1536]{1,0:T(8,128)(2,1)S(1)} %slice.28), channel_id=1, source_target_pairs={{0,8},{8,16},{16,24},{24,28},{28,20},{20,12},{12,4},{4,0},{1,9},{9... | collective-permute-start | bytes 884744 | tf_op jit(solution)/shard_map/ppermute | solution.py:546
  76.6 0.2 collective-permute-start.15
  76.9 1.5 collective-permute-start.13
  78.4 5.8 %collective-permute-done.15.refs_4_.refs_11_ = bf16[80,1536]{1,0:T(8,128)(2,1)S(1)} collective-permute-done((bf16[80,1536]{1,0:T(8,128)(2,1)S(1)}, bf16[80,1536]{1,0:T(8,128)(2,1)S(1)}, u32[]{:S(2)}, u32[]{:S(2)}) %collective-permute-start.15) | collective-permute-done | bytes 245792 | tf_op jit(solution)/shard_map/ppermute | solution.py:547
  84.3 1.5 collective-permute-start.16
  85.8 0.8 copy-done.12
  86.6 0.8 copy-done.13
  87.4 6.6 %project.2 = (bf16[1280,384]{1,0:T(8,128)(2,1)}, bf16[1024,128]{1,0:T(8,128)(2,1)}) custom-call(s32[39]{0:T(128)} %concatenate.47.place, bf16[256,1536]{1,0:T(8,128)(2,1)} %constant_dynamic-slice_fusion.7.refs_0_, bf16[176,1536]{1,0:T(8,128)(2,1)} %collective-permute-done.1.refs_1_, bf16[176,1536]{1,0:T(8,128)(2,1)} %collective-permute-done.2.refs_2_, ...), custom_call_target="tpu_custom_call" | custom-call | flops 8800000000 | bytes 28800000 | tf_op jit(solution)/shard_map/project/pallas_call | solution.py:204
  94.2 0.8 copy-done.14
  94.9 0.7 copy-done.23
  95.6 5.1 %project.3.refs_17_ = bf16[768,384]{1,0:T(8,128)(2,1)} custom-call(s32[39]{0:T(128)} %concatenate.47.place, bf16[176,1536]{1,0:T(8,128)(2,1)} %copy-done.2, bf16[176,1536]{1,0:T(8,128)(2,1)} %copy-done.3, bf16[160,1536]{1,0:T(8,128)(2,1)} %copy-done.14, bf16[96,1536]{1,0:T(8,128)(2,1)} %copy-done.5, bf16[80,1536]{1,0:T(8,128)(2,1)} %copy-done.4, ...), custom_call_target="tpu_custom_call" | custom-call | flops 8800000000 | bytes 28800000 | tf_op jit(solution)/shard_map/project/pallas_call | solution.py:204
  100.8 0.6 collective-permute-start.19
  101.4 1.9 %collective-permute-done.17.refs_14_ = bf16[1024,128]{1,0:T(8,128)(2,1)S(1)} collective-permute-done((bf16[1024,128]{1,0:T(8,128)(2,1)S(1)}, bf16[1024,128]{1,0:T(8,128)(2,1)S(1)}, u32[]{:S(2)}, u32[]{:S(2)}) %collective-permute-start.17) | collective-permute-done | bytes 262176 | tf_op jit(solution)/shard_map/ppermute | solution.py:606
  103.4 0.7 copy-done.22
  104.0 0.3 copy-done.10
  104.4 0.2 copy-done.11
  104.6 25.8 %head.1 = (bf16[1152,128]{1,0:T(8,128)(2,1)}, bf16[1152,128]{1,0:T(8,128)(2,1)}, bf16[1152,128]{1,0:T(8,128)(2,1)}, bf16[1152,128]{1,0:T(8,128)(2,1)}, f32[8,128]{1,0:T(8,128)}) custom-call(s32[39]{0:T(128)} %concatenate.47.place, s32[6]{0:T(128)} %pad_add_fusion.windows, bf16[256,1536]{1,0:T(8,128)(2,1)} %constant_dynamic-slice_fusion.7.refs_0_, ...), custom_call_target="tpu_custom_call" | custom-call | flops 34100000768 | bytes 111600000 | tf_op jit(solution)/shard_map/head/pallas_call | solution.py:607
  130.4 1.6 collective-permute-start.25
  132.0 2.5 %collective-permute-start.26 = (bf16[1152,128]{1,0:T(8,128)(2,1)}, bf16[1152,128]{1,0:T(8,128)(2,1)S(1)}, u32[]{:S(2)}, u32[]{:S(2)}) collective-permute-start(bf16[1152,128]{1,0:T(8,128)(2,1)} %get-tuple-element.49), channel_id=1, source_target_pairs={{4,0},{20,1},{6,2},{22,3},{8,4},{24,5},{10,6},{26,7},{12,8},{28,9}... | collective-permute-start | bytes 884744 | tf_op jit(solution)/shard_map/ppermute | solution.py:654
  134.5 1.2 collective-permute-start.28
  135.7 0.7 slice.23
  136.4 3.9 %collective-permute-start.20 = (f32[1,128]{1,0:T(1,128)S(1)}, f32[1,128]{1,0:T(1,128)S(1)}, u32[]{:S(2)}, u32[]{:S(2)}) collective-permute-start(f32[1,128]{1,0:T(1,128)S(1)} %slice.23), channel_id=1, source_target_pairs={{0,1},{1,0},{2,3},{3,2},{4,5},{5,4},{6,7},{7,6},{8,9},{9,8},{10,11... | collective-permute-start | bytes 1544 | tf_op jit(solution)/shard_map/ppermute | solution.py:658
  140.3 0.8 collective-permute-done.20
  141.2 0.7 slice_add_fusion
  141.9 1.5 collective-permute-start.21
  143.3 2.1 %collective-permute-done.21 = f32[1,128]{1,0:T(1,128)S(1)} collective-permute-done((f32[1,128]{1,0:T(1,128)S(1)}, f32[1,128]{1,0:T(1,128)S(1)}, u32[]{:S(2)}, u32[]{:S(2)}) %collective-permute-start.21) | collective-permute-done | bytes 544 | tf_op jit(solution)/shard_map/ppermute | solution.py:658
  145.4 2.4 %collective-permute-start.22 = (f32[1,128]{1,0:T(1,128)S(1)}, f32[1,128]{1,0:T(1,128)S(1)}, u32[]{:S(2)}, u32[]{:S(2)}) collective-permute-start(f32[1,128]{1,0:T(1,128)S(1)} %add.153), channel_id=1, source_target_pairs={{0,4},{4,0},{8,12},{12,8},{16,20},{20,16},{24,28},{28,24},{1,5},{5... | collective-permute-start | bytes 1544 | tf_op jit(solution)/shard_map/ppermute | solution.py:662
  147.8 1.5 collective-permute-done.22
  149.3 0.3 collective-permute-start.23
  149.6 3.3 %collective-permute-done.23 = f32[1,128]{1,0:T(1,128)S(1)} collective-permute-done((f32[1,128]{1,0:T(1,128)S(1)}, f32[1,128]{1,0:T(1,128)S(1)}, u32[]{:S(2)}, u32[]{:S(2)}) %collective-permute-start.23) | collective-permute-done | bytes 544 | tf_op jit(solution)/shard_map/ppermute | solution.py:662
  152.9 4.7 %collective-permute-start.24 = (f32[1,128]{1,0:T(1,128)S(1)}, f32[1,128]{1,0:T(1,128)S(1)}, u32[]{:S(2)}, u32[]{:S(2)}) collective-permute-start(f32[1,128]{1,0:T(1,128)S(1)} %add.155), channel_id=1, source_target_pairs={{0,16},{4,20},{8,24},{12,28},{16,0},{20,4},{24,8},{28,12},{1,17},{... | collective-permute-start | bytes 1544 | tf_op jit(solution)/shard_map/ppermute | solution.py:662
  157.6 4.6 %collective-permute-done.24 = f32[1,128]{1,0:T(1,128)S(1)} collective-permute-done((f32[1,128]{1,0:T(1,128)S(1)}, f32[1,128]{1,0:T(1,128)S(1)}, u32[]{:S(2)}, u32[]{:S(2)}) %collective-permute-start.24) | collective-permute-done | bytes 544 | tf_op jit(solution)/shard_map/ppermute | solution.py:662
  162.2 0.5 add.156.total
  162.8 0.7 copy-done.17
  163.7 4.3 %finish.1 = (f32[3,384,512]{2,1,0:T(8,128)}, bf16[3,384,512]{2,1,0:T(8,128)(2,1)}) custom-call(s32[1]{0:T(128)} %bitcast.shift, f32[1,128]{1,0:T(1,128)} %add.156.total, bf16[3,384,512]{2,1,0:T(8,128)(2,1)} %w.1, s32[384,512]{1,0:T(8,128)} %mask.1, bf16[1152,128]{1,0:T(8,128)(2,1)} %copy-done.17, bf16[1152,128]{1,0:T(8,128)(2,1)} %copy-done.18, ...), custom_call_target="tpu_custom_call" | custom-call | flops 5500000256 | bytes 18000000 | tf_op jit(solution)/shard_map/finish/pallas_call | solution.py:666
  (88 shorter events, 1.5 us)
Async XLA Ops:
  0.6 6.3 %copy-start = (bf16[3,384,512]{2,1,0:T(8,128)(2,1)S(1)}, bf16[3,384,512]{2,1,0:T(8,128)(2,1)}, u32[]{:S(2)}) copy-start(bf16[3,384,512]{2,1,0:T(8,128)(2,1)} %w.1) | copy-start | bytes 3538948
  2.9 25.9 %collective-permute-start.2 = (bf16[176,1536]{1,0:T(8,128)(2,1)}, bf16[176,1536]{1,0:T(8,128)(2,1)}, u32[]{:S(2)}, u32[]{:S(2)}) collective-permute-start(bf16[176,1536]{1,0:T(8,128)(2,1)} %dynamic_slice.57), channel_id=1, source_target_pairs={{8,0},{16,8},{24,16},{28,24},{20,28},{12,20},{4,12},{0,4},{9,1},{1... | collective-permute-start | bytes 1622024 | tf_op jit(solution)/shard_map/ppermute | solution.py:532
  5.9 22.9 %collective-permute-start.1 = (bf16[176,1536]{1,0:T(8,128)(2,1)}, bf16[176,1536]{1,0:T(8,128)(2,1)}, u32[]{:S(2)}, u32[]{:S(2)}) collective-permute-start(bf16[176,1536]{1,0:T(8,128)(2,1)} %dynamic_slice.57), channel_id=1, source_target_pairs={{0,8},{8,16},{16,24},{24,28},{28,20},{20,12},{12,4},{4,0},{1,9},{9... | collective-permute-start | bytes 1622024 | tf_op jit(solution)/shard_map/ppermute | solution.py:531
  6.0 12.6 %collective-permute-start = (f32[2,512]{1,0:T(2,128)}, f32[2,512]{1,0:T(2,128)S(1)}, u32[]{:S(2)}, u32[]{:S(2)}) collective-permute-start(f32[2,512]{1,0:T(2,128)} %param.11), channel_id=1, source_target_pairs={{0,1},{1,0},{2,3},{3,2},{4,5},{5,4},{6,7},{7,6},{8,9},{9,8},{10,11... | collective-permute-start | bytes 12296 | tf_op jit(solution)/shard_map/ppermute | solution.py:492
  6.9 3.9 %copy-start.8 = (s32[2048]{0:T(1024)S(1)}, s32[2048]{0:T(1024)}, u32[]{:S(2)}) copy-start(s32[2048]{0:T(1024)} %param.13) | copy-start | bytes 24580
  7.0 6.0 %copy-start.1 = (bf16[256,3072]{1,0:T(8,128)(2,1)S(1)}, bf16[256,3072]{1,0:T(8,128)(2,1)}, u32[]{:S(2)}) copy-start(bf16[256,3072]{1,0:T(8,128)(2,1)} %param.9) | copy-start | bytes 4718596
  7.2 7.4 %copy-start.9 = (s32[2048]{0:T(1024)S(1)}, s32[2048]{0:T(1024)}, u32[]{:S(2)}) copy-start(s32[2048]{0:T(1024)} %param.14) | copy-start | bytes 24580
  7.2 8.6 %copy-start.24 = (s32[3]{0:T(128)S(1)}, s32[3]{0:T(128)}, u32[]{:S(2)}) copy-start(s32[3]{0:T(128)} %constant.153) | copy-start | bytes 40
  7.2 14.2 %collective-permute-start.3 = (bf16[1408,128]{1,0:T(8,128)(2,1)S(1)}, bf16[1408,128]{1,0:T(8,128)(2,1)}, u32[]{:S(2)}, u32[]{:S(2)}) collective-permute-start(bf16[1408,128]{1,0:T(8,128)(2,1)S(1)} %pad_maximum_fusion.3), channel_id=1, source_target_pairs={{0,0},{1,16},{2,2},{3,18},{4,4},{5,20},{6,6},{7,22},{8,8},{9,24},{... | collective-permute-start | bytes 1081352 | tf_op jit(solution)/shard_map/ppermute | solution.py:520
  8.8 19.9 %collective-permute-start.4 = (bf16[1408,128]{1,0:T(8,128)(2,1)S(1)}, bf16[1408,128]{1,0:T(8,128)(2,1)}, u32[]{:S(2)}, u32[]{:S(2)}) collective-permute-start(bf16[1408,128]{1,0:T(8,128)(2,1)S(1)} %pad_maximum_fusion.4), channel_id=1, source_target_pairs={{0,4},{1,20},{2,6},{3,22},{4,8},{5,24},{6,10},{7,26},{8,12},{9,28}... | collective-permute-start | bytes 1081352 | tf_op jit(solution)/shard_map/ppermute | solution.py:520
  18.6 15.8 %collective-permute-start.7 = (bf16[1408,128]{1,0:T(8,128)(2,1)S(1)}, bf16[1408,128]{1,0:T(8,128)(2,1)S(1)}, u32[]{:S(2)}, u32[]{:S(2)}) collective-permute-start(bf16[1408,128]{1,0:T(8,128)(2,1)S(1)} %pad_maximum_fusion.5), channel_id=1, source_target_pairs={{0,8},{1,24},{2,10},{3,26},{4,12},{5,28},{6,14},{7,30},{8,0},{9,16... | collective-permute-start | bytes 1081352 | tf_op jit(solution)/shard_map/ppermute | solution.py:520
  21.5 15.3 %collective-permute-start.8 = (bf16[1408,128]{1,0:T(8,128)(2,1)S(1)}, bf16[1408,128]{1,0:T(8,128)(2,1)S(1)}, u32[]{:S(2)}, u32[]{:S(2)}) collective-permute-start(bf16[1408,128]{1,0:T(8,128)(2,1)S(1)} %pad_maximum_fusion.6), channel_id=1, source_target_pairs={{0,12},{1,28},{2,14},{3,30},{4,0},{5,16},{6,2},{7,18},{8,4},{9,20}... | collective-permute-start | bytes 1081352 | tf_op jit(solution)/shard_map/ppermute | solution.py:520
  28.8 19.7 %collective-permute-start.5 = (bf16[176,1536]{1,0:T(8,128)(2,1)}, bf16[176,1536]{1,0:T(8,128)(2,1)S(1)}, u32[]{:S(2)}, u32[]{:S(2)}) collective-permute-start(bf16[176,1536]{1,0:T(8,128)(2,1)} %collective-permute-done.1.refs_1_), channel_id=1, source_target_pairs={{0,8},{8,16},{16,24},{24,28},{28,20},{20,12},{12,4},{4,0},{1,9},{9... | collective-permute-start | bytes 1622024 | tf_op jit(solution)/shard_map/ppermute | solution.py:531
  30.2 26.5 %collective-permute-start.6 = (bf16[176,1536]{1,0:T(8,128)(2,1)}, bf16[176,1536]{1,0:T(8,128)(2,1)S(1)}, u32[]{:S(2)}, u32[]{:S(2)}) collective-permute-start(bf16[176,1536]{1,0:T(8,128)(2,1)} %collective-permute-done.2.refs_2_), channel_id=1, source_target_pairs={{8,0},{16,8},{24,16},{28,24},{20,28},{12,20},{4,12},{0,4},{9,1},{1... | collective-permute-start | bytes 1622024 | tf_op jit(solution)/shard_map/ppermute | solution.py:532
  32.8 53.0 %collective-permute-start.9 = (bf16[160,1536]{1,0:T(8,128)(2,1)S(1)}, bf16[160,1536]{1,0:T(8,128)(2,1)S(1)}, u32[]{:S(2)}, u32[]{:S(2)}) collective-permute-start(bf16[160,1536]{1,0:T(8,128)(2,1)S(1)} %pad_maximum_fusion), channel_id=1, source_target_pairs={{0,2},{1,3},{2,0},{3,1},{4,6},{5,7},{6,4},{7,5},{8,10},{9,11},{10,... | collective-permute-start | bytes 1474568 | tf_op jit(solution)/shard_map/ppermute | solution.py:537
  34.4 42.1 %copy-start.15 = (bf16[1408,128]{1,0:T(8,128)(2,1)}, bf16[1408,128]{1,0:T(8,128)(2,1)S(1)}, u32[]{:S(2)}) copy-start(bf16[1408,128]{1,0:T(8,128)(2,1)S(1)} %collective-permute-done.7.refs_9_.refs_8_) | copy-start | bytes 1081348
  36.8 39.8 %copy-start.16 = (bf16[1408,128]{1,0:T(8,128)(2,1)}, bf16[1408,128]{1,0:T(8,128)(2,1)S(1)}, u32[]{:S(2)}) copy-start(bf16[1408,128]{1,0:T(8,128)(2,1)S(1)} %collective-permute-done.8.refs_10_.refs_9_) | copy-start | bytes 1081348
  48.5 28.1 %copy-start.6 = (bf16[176,1536]{1,0:T(8,128)(2,1)}, bf16[176,1536]{1,0:T(8,128)(2,1)S(1)}, u32[]{:S(2)}) copy-start(bf16[176,1536]{1,0:T(8,128)(2,1)S(1)} %collective-permute-done.5.refs_4_) | copy-start | bytes 1622020
  56.7 19.8 %copy-start.7 = (bf16[176,1536]{1,0:T(8,128)(2,1)}, bf16[176,1536]{1,0:T(8,128)(2,1)S(1)}, u32[]{:S(2)}) copy-start(bf16[176,1536]{1,0:T(8,128)(2,1)S(1)} %collective-permute-done.6.refs_5_) | copy-start | bytes 1622020
  56.7 17.2 %collective-permute-start.11 = (bf16[176,1536]{1,0:T(8,128)(2,1)S(1)}, bf16[176,1536]{1,0:T(8,128)(2,1)S(1)}, u32[]{:S(2)}, u32[]{:S(2)}) collective-permute-start(bf16[176,1536]{1,0:T(8,128)(2,1)S(1)} %collective-permute-done.5.refs_4_), channel_id=1, source_target_pairs={{0,8},{8,16},{16,24},{24,28},{28,20},{20,12},{12,4},{4,0},{1,9},{9... | collective-permute-start | bytes 1622024 | tf_op jit(solution)/shard_map/ppermute | solution.py:531
  62.7 13.8 %collective-permute-start.12 = (bf16[176,1536]{1,0:T(8,128)(2,1)S(1)}, bf16[176,1536]{1,0:T(8,128)(2,1)S(1)}, u32[]{:S(2)}, u32[]{:S(2)}) collective-permute-start(bf16[176,1536]{1,0:T(8,128)(2,1)S(1)} %collective-permute-done.6.refs_5_), channel_id=1, source_target_pairs={{8,0},{16,8},{24,16},{28,24},{20,28},{12,20},{4,12},{0,4},{9,1},{1... | collective-permute-start | bytes 1622024 | tf_op jit(solution)/shard_map/ppermute | solution.py:532
  62.8 23.0 %collective-permute-start.10 = (bf16[160,1536]{1,0:T(8,128)(2,1)S(1)}, bf16[160,1536]{1,0:T(8,128)(2,1)S(1)}, u32[]{:S(2)}, u32[]{:S(2)}) collective-permute-start(bf16[160,1536]{1,0:T(8,128)(2,1)S(1)} %pad_maximum_fusion.1), channel_id=1, source_target_pairs={{0,2},{1,3},{2,0},{3,1},{4,6},{5,7},{6,4},{7,5},{8,10},{9,11},{10,... | collective-permute-start | bytes 1474568 | tf_op jit(solution)/shard_map/ppermute | solution.py:537
  73.9 10.4 %copy-start.2 = (bf16[176,1536]{1,0:T(8,128)(2,1)}, bf16[176,1536]{1,0:T(8,128)(2,1)S(1)}, u32[]{:S(2)}) copy-start(bf16[176,1536]{1,0:T(8,128)(2,1)S(1)} %collective-permute-done.11.refs_0_.refs_7_) | copy-start | bytes 1622020
  73.9 10.3 %collective-permute-start.14 = (bf16[96,1536]{1,0:T(8,128)(2,1)S(1)}, bf16[96,1536]{1,0:T(8,128)(2,1)S(1)}, u32[]{:S(2)}, u32[]{:S(2)}) collective-permute-start(bf16[96,1536]{1,0:T(8,128)(2,1)S(1)} %slice.28), channel_id=1, source_target_pairs={{0,8},{8,16},{16,24},{24,28},{28,20},{20,12},{12,4},{4,0},{1,9},{9... | collective-permute-start | bytes 884744 | tf_op jit(solution)/shard_map/ppermute | solution.py:546
  76.5 7.8 %copy-start.3 = (bf16[176,1536]{1,0:T(8,128)(2,1)}, bf16[176,1536]{1,0:T(8,128)(2,1)S(1)}, u32[]{:S(2)}) copy-start(bf16[176,1536]{1,0:T(8,128)(2,1)S(1)} %collective-permute-done.12.refs_1_.refs_8_) | copy-start | bytes 1622020
  76.6 7.6 %collective-permute-start.15 = (bf16[80,1536]{1,0:T(8,128)(2,1)S(1)}, bf16[80,1536]{1,0:T(8,128)(2,1)S(1)}, u32[]{:S(2)}, u32[]{:S(2)}) collective-permute-start(bf16[80,1536]{1,0:T(8,128)(2,1)S(1)} %get-tuple-element.60), channel_id=1, source_target_pairs={{8,0},{16,8},{24,16},{28,24},{20,28},{12,20},{4,12},{0,4},{9,1},{1... | collective-permute-start | bytes 737288 | tf_op jit(solution)/shard_map/ppermute | solution.py:547
  76.9 17.2 %collective-permute-start.13 = (bf16[160,1536]{1,0:T(8,128)(2,1)S(1)}, bf16[160,1536]{1,0:T(8,128)(2,1)S(1)}, u32[]{:S(2)}, u32[]{:S(2)}) collective-permute-start(bf16[160,1536]{1,0:T(8,128)(2,1)S(1)} %pad_maximum_fusion.2), channel_id=1, source_target_pairs={{0,2},{1,3},{2,0},{3,1},{4,6},{5,7},{6,4},{7,5},{8,10},{9,11},{10,... | collective-permute-start | bytes 1474568 | tf_op jit(solution)/shard_map/ppermute | solution.py:537
  84.2 9.8 %copy-start.4 = (bf16[80,1536]{1,0:T(8,128)(2,1)}, bf16[80,1536]{1,0:T(8,128)(2,1)S(1)}, u32[]{:S(2)}) copy-start(bf16[80,1536]{1,0:T(8,128)(2,1)S(1)} %collective-permute-done.15.refs_4_.refs_11_) | copy-start | bytes 737284
  84.2 9.8 %copy-start.5 = (bf16[96,1536]{1,0:T(8,128)(2,1)}, bf16[96,1536]{1,0:T(8,128)(2,1)S(1)}, u32[]{:S(2)}) copy-start(bf16[96,1536]{1,0:T(8,128)(2,1)S(1)} %collective-permute-done.14.refs_3_.refs_10_) | copy-start | bytes 884740
  84.3 9.9 %collective-permute-start.16 = (bf16[80,1536]{1,0:T(8,128)(2,1)S(1)}, bf16[80,1536]{1,0:T(8,128)(2,1)S(1)}, u32[]{:S(2)}, u32[]{:S(2)}) collective-permute-start(bf16[80,1536]{1,0:T(8,128)(2,1)S(1)} %slice_select_fusion), channel_id=1, source_target_pairs={{0,2},{1,3},{2,0},{3,1},{4,6},{5,7},{6,4},{7,5},{8,10},{9,11},{10,... | collective-permute-start | bytes 737288 | tf_op jit(solution)/shard_map/ppermute | solution.py:550
  85.8 0.8 copy-start.12
  86.6 0.8 copy-start.13
  94.0 7.3 %copy-start.21 = (bf16[1024,128]{1,0:T(8,128)(2,1)S(1)}, bf16[1024,128]{1,0:T(8,128)(2,1)}, u32[]{:S(2)}) copy-start(bf16[1024,128]{1,0:T(8,128)(2,1)} %get-tuple-element.42.refs_13_) | copy-start | bytes 786436
  94.0 9.3 %collective-permute-start.18 = (bf16[1280,384]{1,0:T(8,128)(2,1)}, bf16[1280,384]{1,0:T(8,128)(2,1)S(1)}, u32[]{:S(2)}, u32[]{:S(2)}) collective-permute-start(bf16[1280,384]{1,0:T(8,128)(2,1)} %get-tuple-element.43.refs_15_), channel_id=1, source_target_pairs={{0,1},{1,0},{2,3},{3,2},{4,5},{5,4},{6,7},{7,6},{8,9},{9,8},{10,11... | collective-permute-start | bytes 2949128 | tf_op jit(solution)/shard_map/ppermute | solution.py:602
  94.1 0.8 copy-start.14
  94.9 0.7 copy-start.23
  100.8 2.6 %collective-permute-start.19 = (bf16[768,384]{1,0:T(8,128)(2,1)}, bf16[768,384]{1,0:T(8,128)(2,1)S(1)}, u32[]{:S(2)}, u32[]{:S(2)}) collective-permute-start(bf16[768,384]{1,0:T(8,128)(2,1)} %project.3.refs_17_), channel_id=1, source_target_pairs={{0,1},{1,0},{2,3},{3,2},{4,5},{5,4},{6,7},{7,6},{8,9},{9,8},{10,11... | collective-permute-start | bytes 1769480 | tf_op jit(solution)/shard_map/ppermute | solution.py:602
  101.3 2.0 %collective-permute-start.17 = (bf16[1024,128]{1,0:T(8,128)(2,1)S(1)}, bf16[1024,128]{1,0:T(8,128)(2,1)S(1)}, u32[]{:S(2)}, u32[]{:S(2)}) collective-permute-start(bf16[1024,128]{1,0:T(8,128)(2,1)S(1)} %copy-done.21), channel_id=1, source_target_pairs={{0,1},{1,0},{2,3},{3,2},{4,5},{5,4},{6,7},{7,6},{8,9},{9,8},{10,11... | collective-permute-start | bytes 786440 | tf_op jit(solution)/shard_map/ppermute | solution.py:606
  103.3 0.7 copy-start.22
  103.3 1.0 copy-start.10
  103.3 1.2 copy-start.11
  130.4 32.4 %collective-permute-start.25 = (bf16[1152,128]{1,0:T(8,128)(2,1)}, bf16[1152,128]{1,0:T(8,128)(2,1)S(1)}, u32[]{:S(2)}, u32[]{:S(2)}) collective-permute-start(bf16[1152,128]{1,0:T(8,128)(2,1)} %get-tuple-element.48), channel_id=1, source_target_pairs={{0,0},{16,1},{2,2},{18,3},{4,4},{20,5},{6,6},{22,7},{8,8},{24,9},{... | collective-permute-start | bytes 884744 | tf_op jit(solution)/shard_map/ppermute | solution.py:654
  132.0 30.8 %collective-permute-start.26 = (bf16[1152,128]{1,0:T(8,128)(2,1)}, bf16[1152,128]{1,0:T(8,128)(2,1)S(1)}, u32[]{:S(2)}, u32[]{:S(2)}) collective-permute-start(bf16[1152,128]{1,0:T(8,128)(2,1)} %get-tuple-element.49), channel_id=1, source_target_pairs={{4,0},{20,1},{6,2},{22,3},{8,4},{24,5},{10,6},{26,7},{12,8},{28,9}... | collective-permute-start | bytes 884744 | tf_op jit(solution)/shard_map/ppermute | solution.py:654
  134.5 28.3 %collective-permute-start.27 = (bf16[1152,128]{1,0:T(8,128)(2,1)}, bf16[1152,128]{1,0:T(8,128)(2,1)S(1)}, u32[]{:S(2)}, u32[]{:S(2)}) collective-permute-start(bf16[1152,128]{1,0:T(8,128)(2,1)} %get-tuple-element.50), channel_id=1, source_target_pairs={{8,0},{24,1},{10,2},{26,3},{12,4},{28,5},{14,6},{30,7},{0,8},{16,9... | collective-permute-start | bytes 884744 | tf_op jit(solution)/shard_map/ppermute | solution.py:654
  134.5 28.3 %collective-permute-start.28 = (bf16[1152,128]{1,0:T(8,128)(2,1)}, bf16[1152,128]{1,0:T(8,128)(2,1)S(1)}, u32[]{:S(2)}, u32[]{:S(2)}) collective-permute-start(bf16[1152,128]{1,0:T(8,128)(2,1)} %get-tuple-element.51), channel_id=1, source_target_pairs={{12,0},{28,1},{14,2},{30,3},{0,4},{16,5},{2,6},{18,7},{4,8},{20,9}... | collective-permute-start | bytes 884744 | tf_op jit(solution)/shard_map/ppermute | solution.py:654
  136.4 4.8 %collective-permute-start.20 = (f32[1,128]{1,0:T(1,128)S(1)}, f32[1,128]{1,0:T(1,128)S(1)}, u32[]{:S(2)}, u32[]{:S(2)}) collective-permute-start(f32[1,128]{1,0:T(1,128)S(1)} %slice.23), channel_id=1, source_target_pairs={{0,1},{1,0},{2,3},{3,2},{4,5},{5,4},{6,7},{7,6},{8,9},{9,8},{10,11... | collective-permute-start | bytes 1544 | tf_op jit(solution)/shard_map/ppermute | solution.py:658
  141.9 3.5 %collective-permute-start.21 = (f32[1,128]{1,0:T(1,128)S(1)}, f32[1,128]{1,0:T(1,128)S(1)}, u32[]{:S(2)}, u32[]{:S(2)}) collective-permute-start(f32[1,128]{1,0:T(1,128)S(1)} %slice_add_fusion), channel_id=1, source_target_pairs={{0,2},{1,3},{2,0},{3,1},{4,6},{5,7},{6,4},{7,5},{8,10},{9,11},{10,... | collective-permute-start | bytes 1544 | tf_op jit(solution)/shard_map/ppermute | solution.py:658
  145.4 3.9 %collective-permute-start.22 = (f32[1,128]{1,0:T(1,128)S(1)}, f32[1,128]{1,0:T(1,128)S(1)}, u32[]{:S(2)}, u32[]{:S(2)}) collective-permute-start(f32[1,128]{1,0:T(1,128)S(1)} %add.153), channel_id=1, source_target_pairs={{0,4},{4,0},{8,12},{12,8},{16,20},{20,16},{24,28},{28,24},{1,5},{5... | collective-permute-start | bytes 1544 | tf_op jit(solution)/shard_map/ppermute | solution.py:662
  149.3 3.6 %collective-permute-start.23 = (f32[1,128]{1,0:T(1,128)S(1)}, f32[1,128]{1,0:T(1,128)S(1)}, u32[]{:S(2)}, u32[]{:S(2)}) collective-permute-start(f32[1,128]{1,0:T(1,128)S(1)} %add.154), channel_id=1, source_target_pairs={{0,8},{4,12},{8,0},{12,4},{16,24},{20,28},{24,16},{28,20},{1,9},{5... | collective-permute-start | bytes 1544 | tf_op jit(solution)/shard_map/ppermute | solution.py:662
  152.9 9.3 %collective-permute-start.24 = (f32[1,128]{1,0:T(1,128)S(1)}, f32[1,128]{1,0:T(1,128)S(1)}, u32[]{:S(2)}, u32[]{:S(2)}) collective-permute-start(f32[1,128]{1,0:T(1,128)S(1)} %add.155), channel_id=1, source_target_pairs={{0,16},{4,20},{8,24},{12,28},{16,0},{20,4},{24,8},{28,12},{1,17},{... | collective-permute-start | bytes 1544 | tf_op jit(solution)/shard_map/ppermute | solution.py:662
  162.7 0.7 copy-start.17
  162.7 0.8 copy-start.18
  162.8 0.9 copy-start.19
  162.8 1.0 copy-start.20
